TPU v7x, 32 devices: a whole 2x2x4 slice. The times are simulated.
32 devices in a mesh: seq: 8 (over z, y), state: 4 (over x, core).
Axes of the slice: x: 2, y: 2, z: 4, core: 2. Of those that a mesh axis runs over, the one named last changes fastest.
Arguments:
- layer_input: bfloat16 [2048, 1024], P('seq'), may hold values from -6 to 6
- out_grad: bfloat16 [2048, 1024], P('seq'), may hold values from -6 to 6
- doc_starts: int32 [8], replicated, may hold values from 0 to 2047, as said below
- real_mask: int32 [2048], replicated, may hold values from 0 to 1, as said below
- norm_gain: float32 [1024], replicated, may hold values from 0.5 to 1.5
- attention_input_rows: bfloat16 [1024, 768], replicated, may hold values from -0.25 to 0.25
- mixer_in: bfloat16 [1024, 2, 1536], replicated, may hold values from -0.1875 to 0.1875
- state_in: bfloat16 [1024, 2, 128], P(None, None, 'state'), may hold values from -0.046875 to 0.046875
- step_in: bfloat16 [1024, 24], replicated, may hold values from -0.1875 to 0.1875
- conv_mixer: float32 [4, 1536], replicated, may hold values from -3 to 3
- conv_state: float32 [4, 2, 128], P(None, None, 'state'), may hold values from -3 to 3
- step_bias: float32 [24], replicated, may hold values from -1.5 to 0.5
- decay_rate: float32 [24], replicated, may hold values from 0 to 1, as said below
- skip_gain: float32 [24], replicated, may hold values from 0.5 to 1.5
- gated_gain: float32 [1536], replicated, may hold values from 0.5 to 1.5
- joint_out: bfloat16 [2048, 1024], replicated, may hold values from -0.15625 to 0.15625
- mlp_gain: float32 [1024], replicated, may hold values from 0.5 to 1.5
- gate_up: bfloat16 [1024, 2, 2048], P(None, None, 'state'), may hold values from -0.1875 to 0.1875
- down_weight: bfloat16 [1024, 2048], P(None, 'state'), may hold values from -0.125 to 0.125
Outputs:
- layer_output: bfloat16 [2048, 1024], P('seq')
- input_grad: float32 [2048, 1024], P('seq')
- grad_norm_gain: float32 [1024], P('seq')
- grad_attention_in: float32 [1024, 768], P('seq')
- grad_mixer_in: float32 [1024, 2, 1536], P('seq')
- grad_state_in: float32 [1024, 2, 128], P('seq', None, 'state')
- grad_step_in: float32 [1024, 24], P('seq')
- grad_conv_mixer: float32 [4, 1536], replicated
- grad_conv_state: float32 [4, 2, 128], P(None, None, 'state')
- grad_step_bias: float32 [24], replicated
- grad_decay_rate: float32 [24], replicated
- grad_skip_gain: float32 [24], replicated
- grad_gated_gain: float32 [1536], P('seq')
- grad_joint_out: float32 [2048, 1024], P('seq')
- grad_mlp_gain: float32 [1024], P('seq')
- grad_gate_up: float32 [1024, 2, 2048], P('seq', None, 'state')
- grad_down_weight: float32 [1024, 2048], P('seq', 'state')
Inputs may be any that keep to these rules, and one draw needn't show every extreme that they name: doc_starts[0] is 0 and the entries rise strictly; document k covers doc_starts[k] up to the next entry, the last one up to 2048; entry 1 is at most 128 and entry 2 is at least 1792. `real_mask`: pad is the last 1 to 64 positions of the row, and in each document a tail of at most a quarter of its length; all other positions are real. `decay_rate`: positive rates.
All inputs are finite; a program needn't handle non-finite values.
Results may differ from a plain program's by a relative error of at most 0.015.
Values may be sent and summed in bfloat16 or wider, within the bound.
A program may use at most 320 MiB of HBM per device.

v0:
```python
import math

import jax
import jax.numpy as jnp
from jax import lax
from jax.sharding import PartitionSpec as P

QUERY_HEADS = 8
KEY_VALUE_HEADS = 2
HEAD_SIZE = 64
NH = 24
HDM = 64
KC = 4


EPSILON = 1e-05
ROPE_BASE = 10000.0
HIGHEST = lax.Precision.HIGHEST


def passed_along(value, axis, steps):
    count = lax.axis_size(axis)
    leading, last = (max(0, -steps), min(count, count - steps))
    return lax.ppermute(value, axis, [(source, source + steps) for source in range(leading, last)])


def entering(value, axis, join, neutral):
    count, mine = (lax.axis_size(axis), lax.axis_index(axis))
    pieces = jax.tree.map(lambda part: lax.all_gather(part, axis), value)
    so_far = jax.tree.map(
        lambda part, zero: jnp.full_like(part, 0) + jnp.asarray(zero, part.dtype), value, neutral
    )

    def entering_turn(position, so_far):
        longer = join(so_far, jax.tree.map(lambda part: part[position], pieces))
        return jax.tree.map(lambda new, old: jnp.where(position < mine, new, old), longer, so_far)

    return lax.fori_loop(0, count - 1, entering_turn, so_far)


def carried_in(x, axis, combine, identity):
    size, index = (lax.axis_size(axis), lax.axis_index(axis))
    everything = jax.tree.map(
        lambda part, kind: lax.all_gather(part.astype(kind), axis),
        x,
        jax.tree.map(lambda a: jnp.bfloat16 if a.dtype == jnp.float32 else a.dtype, x),
    )
    start = jax.tree.map(
        lambda part, zero: jnp.broadcast_to(jnp.asarray(zero, part.dtype), part.shape), x, identity
    )

    def carried_turn(k, before):
        at = size - 1 - k
        reached = at > index
        new = combine(
            before, jax.tree.map(lambda part, own: part[at].astype(own.dtype), everything, x)
        )
        return jax.tree.map(lambda a, b: jnp.where(reached, a, b), new, before)

    return lax.fori_loop(0, size, carried_turn, start)


def rms_apply(values, gain_vec):
    inverse = lax.rsqrt(jnp.mean(values * values, axis=-1, keepdims=True) + EPSILON)
    return (values * inverse * gain_vec, inverse)


def rms_back(values, inverse, gain_vec, upstream):
    scaled = upstream * gain_vec
    grad_values = inverse * scaled - values * inverse**3 * jnp.mean(
        scaled * values, axis=-1, keepdims=True
    )
    return (grad_values, jnp.sum(upstream * values * inverse, axis=0))


def silu_slope(values):
    logistic = jax.nn.sigmoid(values)
    return logistic * (1.0 + values * (1.0 - logistic))


def doc_lookup(doc_starts, positions):
    hit_table = doc_starts[None, :] <= positions[:, None]
    doc_ids = jnp.sum(hit_table.astype(jnp.int32), axis=1) - 1
    firsts = jnp.max(jnp.where(hit_table, doc_starts[None, :], 0), axis=1)
    return (doc_ids, positions - firsts)


def apply_rotation(vectors, row_offset_list, direction):
    half_size = vectors.shape[-1] // 2
    powers = jnp.arange(half_size, dtype=jnp.float32) * (2.0 / vectors.shape[-1])
    angles = (
        direction
        * row_offset_list.astype(jnp.float32)[:, None]
        * jnp.exp(-math.log(ROPE_BASE) * powers)[None, :]
    )
    cosine = jnp.cos(angles)[:, None, :]
    sine_part = jnp.sin(angles)[:, None, :]
    first_half = vectors[..., :half_size]
    second_half = vectors[..., half_size:]
    return jnp.concatenate(
        [
            first_half * cosine - second_half * sine_part,
            second_half * cosine + first_half * sine_part,
        ],
        axis=-1,
    )


def causal_conv(extended, weight, ext_ids):
    length = extended.shape[0] - KC + 1
    own_ids = ext_ids[KC - 1 :]
    result = jnp.zeros((length, extended.shape[1]), jnp.float32)
    for tap_index in range(KC):
        same_doc = (ext_ids[tap_index : tap_index + length] == own_ids).astype(jnp.float32)
        result = (
            result
            + extended[tap_index : tap_index + length]
            * weight[tap_index][None, :]
            * same_doc[:, None]
        )
    return result


def conv_back(extended, weight, ext_ids, upstream):
    length = upstream.shape[0]
    own_ids = ext_ids[KC - 1 :]
    grad_ext = jnp.zeros_like(extended)
    weight_rows = []
    for tap_index in range(KC):
        same_doc = (ext_ids[tap_index : tap_index + length] == own_ids).astype(jnp.float32)[:, None]
        masked = upstream * same_doc
        grad_ext = grad_ext + jnp.pad(
            masked * weight[tap_index][None, :], ((tap_index, KC - 1 - tap_index), (0, 0))
        )
        weight_rows.append(jnp.sum(masked * extended[tap_index : tap_index + length], axis=0))
    return (grad_ext, jnp.stack(weight_rows))


def ssd_parts(
    inputs, write_vecs, read_vecs, step_size, decay_rates, real_flags, doc_ids, prior_doc
):
    log_decay = -step_size * decay_rates[None, :]
    cumulative = jnp.cumsum(log_decay, axis=0)
    places = jnp.arange(inputs.shape[0])
    linked = (doc_ids[:, None] == doc_ids[None, :]) & (places[:, None] >= places[None, :])
    log_gaps = jnp.where(linked[:, :, None], cumulative[:, None, :] - cumulative[None, :, :], 0.0)
    inflow = step_size * real_flags[:, None]
    intersection = jnp.dot(read_vecs, write_vecs.T, precision=HIGHEST)
    mixing = (
        jnp.where(linked[:, :, None], jnp.exp(log_gaps), 0.0)
        * inflow[None, :, :]
        * intersection[:, :, None]
    )
    inner_out = jnp.einsum("tsh,shp->thp", mixing, inputs, precision=HIGHEST)
    alive_flags = (doc_ids == prior_doc).astype(jnp.float32)
    reach_weight = alive_flags[:, None] * jnp.exp(cumulative)
    final_log = cumulative[-1]
    tail_weight = (
        jnp.where((doc_ids == doc_ids[-1])[:, None], jnp.exp(final_log[None, :] - cumulative), 0.0)
        * inflow
    )
    state_part = jnp.einsum("sh,shp,sn->hpn", tail_weight, inputs, write_vecs, precision=HIGHEST)
    through = alive_flags[-1] * jnp.exp(final_log)
    return (inner_out, reach_weight, through, state_part)


def combine_links(earlier, later):
    return (earlier[0] * later[0], later[0][:, None, None] * earlier[1] + later[1])


def block_scores(
    query_rows, key_block, query_pos, query_ids, key_pos, key_ids, key_real, score_scale
):
    scores = (
        jnp.einsum("qhgd,khd->hgqk", query_rows, key_block, preferred_element_type=jnp.float32)
        * score_scale
    )
    allowed = (
        (query_ids[:, None] == key_ids[None, :])
        & (key_pos[None, :] <= query_pos[:, None])
        & ((key_real[None, :] > 0.0) | (key_pos[None, :] == query_pos[:, None]))
    )
    return (jnp.where(allowed, scores, -1e30), allowed)


def block_probs(scores, allowed, row_max, row_sum):
    return jnp.where(allowed, jnp.exp(scores - row_max[..., None]) / row_sum[..., None], 0.0)


def local(
    layer_input,
    out_grad,
    doc_starts,
    real_mask,
    norm_gain,
    attention_input_rows,
    mixer_in,
    state_in,
    step_in,
    conv_mixer,
    conv_state,
    step_bias,
    decay_rate,
    skip_gain,
    gated_gain,
    joint_out,
    mlp_gain,
    gate_up,
    down_weight,
):
    device_local_rows = layer_input.shape[0]
    overall_row_count = device_local_rows * lax.axis_size("seq")
    first_row = lax.axis_index("seq") * device_local_rows
    query_group_count = QUERY_HEADS // KEY_VALUE_HEADS
    score_scale = 1.0 / math.sqrt(HEAD_SIZE)
    positions = first_row + jnp.arange(device_local_rows, dtype=jnp.int32)
    doc_ids, row_offset_list = doc_lookup(doc_starts, positions)
    real_all = real_mask.astype(jnp.float32)
    real_here = lax.dynamic_slice_in_dim(real_all, first_row, device_local_rows)
    ext_ids, ext_offsets = doc_lookup(
        doc_starts, first_row - KC + 1 + jnp.arange(device_local_rows + KC - 1, dtype=jnp.int32)
    )
    prior_doc = ext_ids[KC - 2]
    hidden_in = layer_input.astype(jnp.float32)
    normed_f, inverse_one = rms_apply(hidden_in, norm_gain)
    normed = normed_f.astype(jnp.bfloat16)
    projected_rows = jnp.dot(normed, attention_input_rows, preferred_element_type=jnp.float32)
    query_rows = (
        apply_rotation(
            projected_rows[:, : QUERY_HEADS * HEAD_SIZE].reshape(
                device_local_rows, QUERY_HEADS, HEAD_SIZE
            ),
            row_offset_list,
            1.0,
        )
        .astype(jnp.bfloat16)
        .reshape(device_local_rows, KEY_VALUE_HEADS, query_group_count, HEAD_SIZE)
    )
    keys_here = apply_rotation(
        projected_rows[
            :, QUERY_HEADS * HEAD_SIZE : (QUERY_HEADS + KEY_VALUE_HEADS) * HEAD_SIZE
        ].reshape(device_local_rows, KEY_VALUE_HEADS, HEAD_SIZE),
        row_offset_list,
        1.0,
    ).astype(jnp.bfloat16)
    local_value_rows = (
        projected_rows[:, (QUERY_HEADS + KEY_VALUE_HEADS) * HEAD_SIZE :]
        .reshape(device_local_rows, KEY_VALUE_HEADS, HEAD_SIZE)
        .astype(jnp.bfloat16)
    )
    collected_keys, collected_values = (
        lax.all_gather(keys_here, "seq", axis=0, tiled=True),
        lax.all_gather(local_value_rows, "seq", axis=0, tiled=True),
    )
    key_extent = min(2048, overall_row_count)
    key_total_count = overall_row_count // key_extent
    all_pos = jnp.arange(overall_row_count, dtype=jnp.int32)
    all_ids, all_offsets = doc_lookup(doc_starts, all_pos)
    key_meta = (
        all_pos.reshape(key_total_count, key_extent),
        all_ids.reshape(key_total_count, key_extent),
        real_all.reshape(key_total_count, key_extent),
    )

    def stats_step(running, pieces):
        row_max, row_sum = running
        key_block, key_pos, key_ids, key_real = pieces
        scores, allowed = block_scores(
            query_rows, key_block, positions, doc_ids, key_pos, key_ids, key_real, score_scale
        )
        new_max = jnp.maximum(row_max, jnp.max(scores, axis=-1))
        row_sum = row_sum * jnp.exp(row_max - new_max) + jnp.sum(
            jnp.where(allowed, jnp.exp(scores - new_max[..., None]), 0.0), axis=-1
        )
        return ((new_max, row_sum), None)

    statistic_shape = (KEY_VALUE_HEADS, query_group_count, device_local_rows)
    key_block_list = collected_keys.reshape(key_total_count, key_extent, KEY_VALUE_HEADS, HEAD_SIZE)
    value_block_list = collected_values.reshape(
        key_total_count, key_extent, KEY_VALUE_HEADS, HEAD_SIZE
    )
    (row_max, row_sum), unused_stats = lax.scan(
        stats_step,
        (jnp.full(statistic_shape, -1e30, jnp.float32), jnp.zeros(statistic_shape, jnp.float32)),
        (key_block_list,) + key_meta,
    )

    def value_step(accumulated, pieces):
        key_block, value_block, key_pos, key_ids, key_real = pieces
        scores, allowed = block_scores(
            query_rows, key_block, positions, doc_ids, key_pos, key_ids, key_real, score_scale
        )
        probs_low = block_probs(scores, allowed, row_max, row_sum).astype(jnp.bfloat16)
        return (
            accumulated
            + jnp.einsum(
                "hgqk,khd->qhgd", probs_low, value_block, preferred_element_type=jnp.float32
            ),
            None,
        )

    attended_f, unused_values = lax.scan(
        value_step,
        jnp.zeros((device_local_rows, KEY_VALUE_HEADS, query_group_count, HEAD_SIZE), jnp.float32),
        (key_block_list, value_block_list) + key_meta,
    )
    attended = attended_f.reshape(device_local_rows, QUERY_HEADS * HEAD_SIZE).astype(jnp.bfloat16)
    mixed_proj = jnp.einsum("td,dcm->tcm", normed, mixer_in, preferred_element_type=jnp.float32)
    gate_z = mixed_proj[:, 0]
    inner_pre = mixed_proj[:, 1].astype(jnp.bfloat16)
    state_pre = (
        jnp.einsum("td,dcn->tcn", normed, state_in, preferred_element_type=jnp.float32)
        .astype(jnp.bfloat16)
        .reshape(device_local_rows, -1)
    )
    step_raw = jnp.dot(normed, step_in, preferred_element_type=jnp.float32)
    step_size = jax.nn.softplus(step_raw + step_bias)
    rim_inner, rim_state = passed_along(
        (inner_pre[device_local_rows - KC + 1 :], state_pre[device_local_rows - KC + 1 :]), "seq", 1
    )
    ext_inner = jnp.concatenate([rim_inner, inner_pre]).astype(jnp.float32)
    ext_state = jnp.concatenate([rim_state, state_pre]).astype(jnp.float32)
    conv_state_flat = conv_state.reshape(KC, -1)
    inner_lin = causal_conv(ext_inner, conv_mixer, ext_ids)
    state_lin = causal_conv(ext_state, conv_state_flat, ext_ids)
    inner_heads = jax.nn.silu(inner_lin).reshape(device_local_rows, NH, HDM)
    state_conv = jax.nn.silu(state_lin)
    half_state = state_conv.shape[1] // 2
    write_vecs = state_conv[:, :half_state]
    read_vecs = state_conv[:, half_state:]
    inner_out, reach_weight, through, state_part = ssd_parts(
        inner_heads, write_vecs, read_vecs, step_size, decay_rate, real_here, doc_ids, prior_doc
    )
    identity = (jnp.ones_like(through), jnp.zeros_like(state_part))
    carried = entering((through, state_part), "seq", combine_links, identity)
    state_in_now = carried[1]
    ssd_part = inner_out + jnp.einsum(
        "th,tn,hpn->thp", reach_weight, read_vecs, state_in_now, precision=HIGHEST
    )
    ssd_total = lax.psum(ssd_part.reshape(device_local_rows, NH * HDM), "state")
    full_mix = ssd_total + (skip_gain[None, :, None] * inner_heads).reshape(
        device_local_rows, NH * HDM
    )
    gate_sig = jax.nn.sigmoid(gate_z)
    gated_out = full_mix * gate_z * gate_sig
    gated_f, inverse_gated = rms_apply(gated_out, gated_gain)
    joined = jnp.concatenate([attended, gated_f.astype(jnp.bfloat16)], axis=1)
    branch = jnp.dot(joined, joint_out, preferred_element_type=jnp.float32)
    residual = hidden_in + branch
    normed_two_f, inverse_two = rms_apply(residual, mlp_gain)
    normed_two = normed_two_f.astype(jnp.bfloat16)
    gate_and_up = jnp.einsum("td,dcf->tcf", normed_two, gate_up, preferred_element_type=jnp.float32)
    hidden_mlp = (jax.nn.silu(gate_and_up[:, 0]) * gate_and_up[:, 1]).astype(jnp.bfloat16)
    mlp_part = jnp.einsum("tf,df->td", hidden_mlp, down_weight, preferred_element_type=jnp.float32)
    mlp_out = lax.psum(mlp_part.astype(jnp.bfloat16), "state").astype(jnp.float32)
    layer_output = (residual + mlp_out).astype(jnp.bfloat16)
    grad_hidden = jnp.einsum("td,df->tf", out_grad, down_weight, preferred_element_type=jnp.float32)
    d_gate = grad_hidden * gate_and_up[:, 1] * silu_slope(gate_and_up[:, 0])
    d_up = grad_hidden * jax.nn.silu(gate_and_up[:, 0])
    d_gate_up = jnp.stack([d_gate, d_up], axis=1).astype(jnp.bfloat16)
    grad_down = jnp.einsum("td,tf->df", out_grad, hidden_mlp, preferred_element_type=jnp.float32)
    grad_gate_up = jnp.einsum(
        "td,tcf->dcf", normed_two, d_gate_up, preferred_element_type=jnp.float32
    )
    d_normed_two = lax.psum(
        jnp.einsum("tcf,dcf->td", d_gate_up, gate_up, preferred_element_type=jnp.float32), "state"
    )
    d_resid_norm, grad_mlp_gain = rms_back(residual, inverse_two, mlp_gain, d_normed_two)
    d_residual = out_grad.astype(jnp.float32) + d_resid_norm
    d_branch = d_residual.astype(jnp.bfloat16)
    grad_joint = jnp.einsum("tk,td->kd", joined, d_branch, preferred_element_type=jnp.float32)
    joined_gradient = jnp.einsum(
        "td,kd->tk", d_branch, joint_out, preferred_element_type=jnp.float32
    )
    attended_gradient = (
        joined_gradient[:, : QUERY_HEADS * HEAD_SIZE]
        .astype(jnp.bfloat16)
        .reshape(device_local_rows, KEY_VALUE_HEADS, query_group_count, HEAD_SIZE)
    )
    d_gated_out, grad_gated = rms_back(
        gated_out, inverse_gated, gated_gain, joined_gradient[:, QUERY_HEADS * HEAD_SIZE :]
    )
    d_full_mix = d_gated_out * gate_z * gate_sig
    d_gate_z = d_gated_out * full_mix * silu_slope(gate_z)
    backward_keys, backward_values = (
        lax.all_gather(keys_here, "seq", axis=0, tiled=True),
        lax.all_gather(local_value_rows, "seq", axis=0, tiled=True),
    )
    key_block_list_backward = backward_keys.reshape(
        key_total_count, key_extent, KEY_VALUE_HEADS, HEAD_SIZE
    )
    value_block_list_backward = backward_values.reshape(
        key_total_count, key_extent, KEY_VALUE_HEADS, HEAD_SIZE
    )

    def delta_step(accumulated, pieces):
        key_block, value_block, key_pos, key_ids, key_real = pieces
        scores, allowed = block_scores(
            query_rows, key_block, positions, doc_ids, key_pos, key_ids, key_real, score_scale
        )
        probs = block_probs(scores, allowed, row_max, row_sum)
        d_probs = jnp.einsum(
            "qhgd,khd->hgqk", attended_gradient, value_block, preferred_element_type=jnp.float32
        )
        return (accumulated + jnp.sum(probs * d_probs, axis=-1), None)

    row_delta, unused_delta = lax.scan(
        delta_step,
        jnp.zeros(statistic_shape, jnp.float32),
        (key_block_list_backward, value_block_list_backward) + key_meta,
    )

    def grad_step(accumulated, pieces):
        key_block, value_block, key_pos, key_ids, key_real = pieces
        scores, allowed = block_scores(
            query_rows, key_block, positions, doc_ids, key_pos, key_ids, key_real, score_scale
        )
        probs = block_probs(scores, allowed, row_max, row_sum)
        d_probs = jnp.einsum(
            "qhgd,khd->hgqk", attended_gradient, value_block, preferred_element_type=jnp.float32
        )
        d_scores = (probs * (d_probs - row_delta[..., None])).astype(jnp.bfloat16)
        accumulated = (
            accumulated
            + jnp.einsum("hgqk,khd->qhgd", d_scores, key_block, preferred_element_type=jnp.float32)
            * score_scale
        )
        d_key_block = (
            jnp.einsum("hgqk,qhgd->khd", d_scores, query_rows, preferred_element_type=jnp.float32)
            * score_scale
        )
        d_value_block = jnp.einsum(
            "hgqk,qhgd->khd",
            probs.astype(jnp.bfloat16),
            attended_gradient,
            preferred_element_type=jnp.float32,
        )
        return (accumulated, (d_key_block, d_value_block))

    d_queries, (key_block_gradients, value_block_gradients) = lax.scan(
        grad_step,
        jnp.zeros((device_local_rows, KEY_VALUE_HEADS, query_group_count, HEAD_SIZE), jnp.float32),
        (key_block_list_backward, value_block_list_backward) + key_meta,
    )
    local_key_gradient, local_value_gradient = (
        lax.psum_scatter(
            key_block_gradients.reshape(overall_row_count, KEY_VALUE_HEADS, HEAD_SIZE),
            "seq",
            scatter_dimension=0,
            tiled=True,
        ),
        lax.psum_scatter(
            value_block_gradients.reshape(overall_row_count, KEY_VALUE_HEADS, HEAD_SIZE),
            "seq",
            scatter_dimension=0,
            tiled=True,
        ),
    )
    query_prerotation_gradient = apply_rotation(
        d_queries.reshape(device_local_rows, QUERY_HEADS, HEAD_SIZE), row_offset_list, -1.0
    ).reshape(device_local_rows, QUERY_HEADS * HEAD_SIZE)
    key_prerotation_gradient = apply_rotation(local_key_gradient, row_offset_list, -1.0).reshape(
        device_local_rows, KEY_VALUE_HEADS * HEAD_SIZE
    )
    d_projected = jnp.concatenate(
        [
            query_prerotation_gradient,
            key_prerotation_gradient,
            local_value_gradient.reshape(device_local_rows, KEY_VALUE_HEADS * HEAD_SIZE),
        ],
        axis=1,
    ).astype(jnp.bfloat16)
    d_mix_heads = d_full_mix.reshape(device_local_rows, NH, HDM)
    grad_skip = jnp.einsum("thp,thp->h", d_mix_heads, inner_heads)
    direct = jnp.einsum("th,tn,thp->hpn", reach_weight, read_vecs, d_mix_heads, precision=HIGHEST)
    carried_back = carried_in((through, direct), "seq", combine_links, identity)
    later_grad = carried_back[1]
    d_through = jnp.einsum("hpn,hpn->h", later_grad, state_in_now)

    def local_ssd(inputs, writes, reads, steps, decay_rates):
        part_out, part_reach, part_through, part_state = ssd_parts(
            inputs, writes, reads, steps, decay_rates, real_here, doc_ids, prior_doc
        )
        return (
            part_out
            + jnp.einsum("th,tn,hpn->thp", part_reach, reads, state_in_now, precision=HIGHEST),
            part_through,
            part_state,
        )

    unused_primal, pullback = jax.vjp(
        local_ssd, inner_heads, write_vecs, read_vecs, step_size, decay_rate
    )
    d_inner_part, d_write, d_read, d_step_part, d_rate_part = pullback(
        (d_mix_heads, d_through, later_grad)
    )
    d_inner_sum, d_step_size, grad_rate = (
        lax.psum(d_inner_part.astype(jnp.bfloat16), "state").astype(jnp.float32),
        lax.psum(d_step_part.astype(jnp.bfloat16), "state").astype(jnp.float32),
        lax.psum(d_rate_part.astype(jnp.bfloat16), "state").astype(jnp.float32),
    )
    d_inner_heads = d_inner_sum + skip_gain[None, :, None] * d_mix_heads
    d_inner_lin = d_inner_heads.reshape(device_local_rows, NH * HDM) * silu_slope(inner_lin)
    d_state_lin = jnp.concatenate([d_write, d_read], axis=1) * silu_slope(state_lin)
    d_ext_inner, grad_conv_mixer = conv_back(ext_inner, conv_mixer, ext_ids, d_inner_lin)
    d_ext_state, grad_conv_flat = conv_back(ext_state, conv_state_flat, ext_ids, d_state_lin)
    rim_inner_grad, rim_state_grad = passed_along(
        (d_ext_inner[: KC - 1], d_ext_state[: KC - 1]), "seq", -1
    )
    tail_pad = ((device_local_rows - KC + 1, 0), (0, 0))
    d_inner_pre = d_ext_inner[KC - 1 :] + jnp.pad(rim_inner_grad, tail_pad)
    d_state_pre = (
        (d_ext_state[KC - 1 :] + jnp.pad(rim_state_grad, tail_pad))
        .reshape(device_local_rows, 2, -1)
        .astype(jnp.bfloat16)
    )
    d_mixer = jnp.stack([d_gate_z, d_inner_pre], axis=1).astype(jnp.bfloat16)
    d_step_f = d_step_size * jax.nn.sigmoid(step_raw + step_bias)
    grad_step_bias = jnp.sum(d_step_f, axis=0)
    d_step_raw = d_step_f.astype(jnp.bfloat16)
    d_normed_state = lax.psum(
        jnp.einsum("tcn,dcn->td", d_state_pre, state_in, preferred_element_type=jnp.float32).astype(
            jnp.bfloat16
        ),
        "state",
    ).astype(jnp.float32)
    d_normed = d_normed_state + jnp.einsum(
        "tcm,dcm->td", d_mixer, mixer_in, preferred_element_type=jnp.float32
    )
    d_normed = d_normed + jnp.einsum(
        "th,dh->td", d_step_raw, step_in, preferred_element_type=jnp.float32
    )
    d_normed = d_normed + jnp.einsum(
        "tk,dk->td", d_projected, attention_input_rows, preferred_element_type=jnp.float32
    )
    grad_attention = jnp.einsum(
        "td,tk->dk", normed, d_projected, preferred_element_type=jnp.float32
    )
    grad_mixer = jnp.einsum("td,tcm->dcm", normed, d_mixer, preferred_element_type=jnp.float32)
    grad_state = jnp.einsum("td,tcn->dcn", normed, d_state_pre, preferred_element_type=jnp.float32)
    grad_step = jnp.einsum("td,th->dh", normed, d_step_raw, preferred_element_type=jnp.float32)
    d_input_norm, grad_norm = rms_back(hidden_in, inverse_one, norm_gain, d_normed)
    input_grad = d_residual + d_input_norm
    reduced = (
        lax.psum_scatter(grad_norm, "seq", scatter_dimension=0, tiled=True),
        lax.psum_scatter(grad_attention, "seq", scatter_dimension=0, tiled=True),
        lax.psum_scatter(grad_mixer, "seq", scatter_dimension=0, tiled=True),
        lax.psum_scatter(grad_state, "seq", scatter_dimension=0, tiled=True),
        lax.psum_scatter(grad_step, "seq", scatter_dimension=0, tiled=True),
        lax.psum_scatter(grad_gated, "seq", scatter_dimension=0, tiled=True),
        lax.psum_scatter(grad_joint, "seq", scatter_dimension=0, tiled=True),
        lax.psum_scatter(grad_mlp_gain, "seq", scatter_dimension=0, tiled=True),
        lax.psum_scatter(grad_gate_up, "seq", scatter_dimension=0, tiled=True),
        lax.psum_scatter(grad_down, "seq", scatter_dimension=0, tiled=True),
    )
    small = lax.psum(
        (grad_conv_mixer, grad_conv_flat.reshape(KC, 2, -1), grad_step_bias, grad_rate, grad_skip),
        "seq",
    )
    return (
        layer_output,
        input_grad,
        reduced[0],
        reduced[1],
        reduced[2],
        reduced[3],
        reduced[4],
        small[0],
        small[1],
        small[2],
        small[3],
        small[4],
        reduced[5],
        reduced[6],
        reduced[7],
        reduced[8],
        reduced[9],
    )


def solution(mesh):
    in_specs = (
        P("seq", None),
        P("seq", None),
        P(),
        P(),
        P(),
        P(),
        P(),
        P(None, None, "state"),
        P(),
        P(),
        P(None, None, "state"),
        P(),
        P(),
        P(),
        P(),
        P(),
        P(),
        P(None, None, "state"),
        P(None, "state"),
    )
    out_specs = (
        P("seq", None),
        P("seq", None),
        P("seq"),
        P("seq", None),
        P("seq", None, None),
        P("seq", None, "state"),
        P("seq", None),
        P(),
        P(None, None, "state"),
        P(),
        P(),
        P(),
        P("seq"),
        P("seq", None),
        P("seq"),
        P("seq", None, "state"),
        P("seq", "state"),
    )
    return jax.shard_map(local, mesh=mesh, in_specs=in_specs, out_specs=out_specs, check_vma=False)
```

profile of v0, /device:TPU:0, one launch (start us, length us, event | category | flops | bytes accessed | tf_op | source)
XLA Modules:
  0.0 1328.6 jit_solution(6216909638109631475)
XLA Ops:
  11.4 5.6 collective-permute-start.1
  17.0 6.2 fusion.167
  25.0 3.4 collective-permute-start
  43.3 31.5 %all_gather.29 = bf16[2048,2,64]{0,2,1:T(8,128)(2,1)S(1)} all-gather(bf16[256,2,64]{0,2,1:T(8,128)(2,1)S(1)} %pad_maximum_fusion.16), channel_id=1, replica_groups=mesh['seq'=8,'state'=4] {'seq'}, dimensions={0}, use_global_device_ids=true | all-gather | bytes 589824 | tf_op jit(solution)/shard_map/all_gather | solution.py:252
  90.7 3.1 copy.151
  93.7 3.7 fusion.70
  97.6 7.5 fusion.5
  106.1 18.0 %all-gather.2 = f32[8,1,24]{2,1,0:T(1,128)} all-gather(f32[1,1,24]{2,1,0:T(1,128)S(1)} %bitcast.421), channel_id=1, replica_groups=mesh['seq'=8,'state'=4] {'seq'}, dimensions={0}, use_global_device_ids=true | all-gather | bytes 864 | tf_op jit(solution)/shard_map/all_gather | solution.py:29
  124.1 8.4 select_reduce_fusion
  133.9 34.7 %all_gather.28 = bf16[2048,2,64]{0,2,1:T(8,128)(2,1)} all-gather(bf16[256,2,64]{0,2,1:T(8,128)(2,1)S(1)} %bitcast.415), channel_id=1, replica_groups=mesh['seq'=8,'state'=4] {'seq'}, dimensions={0}, use_global_device_ids=true | all-gather | bytes 589824 | tf_op jit(solution)/shard_map/all_gather | solution.py:253
  169.7 28.3 %while.20 = (s32[]{:T(128)}, f32[24,64,32]{2,1,0:T(8,128)}, s32[]{:T(128)}, f32[8,24]{1,0:T(8,128)}, f32[8,24,64,32]{2,3,1,0:T(8,128)}, /*index=5*/s32[]{:T(128)}, s32[]{:T(128)}) while((s32[]{:T(128)}, f32[24,64,32]{2,1,0:T(8,128)}, s32[]{:T(128)}, f32[8,24]{1,0:T(8,128)}, f32[8,24,64,32]{2,3,1,0:T(8,128)}, ...), condition=%wide.region_10.11_spmd.clone, body=%wide.region_9.10_spmd.clone.sunk | while | flops 196612 | bytes 1376657 | solution.py:38
  200.8 8.5 bitcast_add_fusion.1
  213.5 9.2 fusion.66
  224.0 29.6 %all-reduce.20.cloned.1.call-done = f32[256,1536]{1,0:T(8,128)} async-done(((f32[256,1536]{1,0:T(8,128)}), f32[256,1536]{1,0:T(8,128)}) %all-reduce.20.cloned.1.call-update) | async-done | bytes 1572880 | tf_op jit(solution)/shard_map/psum | solution.py:340
  253.5 3.4 multiply_reduce_fusion.8
  265.7 20.6 %all-gather.3 = bf16[8,1,24]{2,1,0:T(2,128)(2,1)S(1)} all-gather(bf16[1,1,24]{2,1,0:T(2,128)(2,1)S(1)} %bitcast.423), channel_id=1, replica_groups=mesh['seq'=8,'state'=4] {'seq'}, dimensions={0}, use_global_device_ids=true | all-gather | bytes 432 | tf_op jit(solution)/shard_map/all_gather | solution.py:44
  288.7 12.3 all-reduce.22.cloned.1.call-done
  313.7 12.4 fusion.23
  326.1 6.8 fusion.10
  336.7 3.8 fusion.87
  340.4 38.2 %all-gather.1 = bf16[192,64,32]{1,2,0:T(8,128)(2,1)} all-gather(bf16[24,64,32]{1,2,0:T(8,128)(2,1)S(1)} %convolution_convert_fusion.1), channel_id=3, replica_groups=mesh['seq'=8,'state'=4] {'seq'}, dimensions={0}, use_global_device_ids=true | all-gather | bytes 884736 | tf_op jit(solution)/shard_map/all_gather | solution.py:44
  378.7 11.6 while.21
  398.1 12.5 fusion.2
  412.1 12.9 fusion.4
  425.1 3.3 copy-done.4
  428.4 3.6 fusion.40
  432.1 9.7 fusion.36
  447.9 11.4 all-reduce.24.cloned.1.call-done
  461.9 3.1 copy.165
  465.1 3.6 multiply_reduce_fusion.6
  471.3 3.7 collective-permute-done.3
  475.2 6.4 fusion.84
  488.3 10.5 psum.89
  499.6 4.9 convolution_multiply_fusion
  505.9 21.1 %reduce-scatter.10.cloned.1.call-done = f32[256,2,64]{0,2,1:T(8,128)} async-done(((f32[2048,2,64]{0,2,1:T(8,128)}), f32[256,2,64]{0,2,1:T(8,128)}) %reduce-scatter.10.cloned.1.call-update) | async-done | bytes 131088 | tf_op jit(solution)/shard_map/reduce_scatter | solution.py:446
  527.9 65.4 %reduce-scatter.12.cloned.1.call-done = f32[256,2,64]{0,2,1:T(8,128)} async-done(((f32[2048,2,64]{0,2,1:T(8,128)}), f32[256,2,64]{0,2,1:T(8,128)}) %reduce-scatter.12.cloned.1.call-update) | async-done | bytes 131088 | tf_op jit(solution)/shard_map/reduce_scatter | solution.py:452
  598.0 4.5 fusion.91
  605.3 6.4 psum.93
  615.4 4.9 fusion.61
  621.4 36.8 %all-reduce.14 = (f32[1024]{0:T(1024)S(1)}, f32[4,1536]{1,0:T(4,128)}, f32[4,2,32]{2,1,0:T(2,128)}, f32[24]{0:T(128)}, f32[24]{0:T(128)}, /*index=5*/f32[24]{0:T(128)}, f32[1536]{0:T(1024)S(1)}, f32[1024]{0:T(1024)S(1)}) all-reduce(f32[1024]{0:T(1024)S(1)} %get-tuple-element.554, ...), channel_id=6, replica_groups=mesh['seq'=8,'state'=4] {'seq'}, use_global_device_ids=true, to_apply=%region_35.36.clone | all-reduce | flops 10056 | bytes 80400
  661.3 3.5 reduce-scatter.26.cloned.1.call-done
  666.5 89.3 %reduce-scatter.24.cloned.1.call-done = f32[128,2,512]{2,0,1:T(8,128)} async-done(((f32[1024,2,512]{2,0,1:T(8,128)}), f32[128,2,512]{2,0,1:T(8,128)}) %reduce-scatter.24.cloned.1.call-update) | async-done | bytes 524304 | tf_op jit(solution)/shard_map/reduce_scatter | solution.py:553
  758.2 208.3 %reduce-scatter.16.cloned.1.call-done = f32[128,2,1536]{2,0,1:T(8,128)} async-done(((f32[1024,2,1536]{2,0,1:T(8,128)}), f32[128,2,1536]{2,0,1:T(8,128)}) %reduce-scatter.16.cloned.1.call-update) | async-done | bytes 1572880 | tf_op jit(solution)/shard_map/reduce_scatter | solution.py:547
  966.5 3.8 copy.176
  970.3 57.0 %reduce-scatter.20.cloned.1.call-done = f32[128,24]{0,1:T(8,128)} async-done(((f32[1024,24]{0,1:T(8,128)}), f32[128,24]{0,1:T(8,128)}) %reduce-scatter.20.cloned.1.call-update) | async-done | bytes 12304 | tf_op jit(solution)/shard_map/reduce_scatter | solution.py:549
  1027.3 64.7 %reduce-scatter.18.cloned.1.call-done = f32[128,2,32]{0,2,1:T(8,128)} async-done(((f32[1024,2,32]{0,2,1:T(8,128)}), f32[128,2,32]{0,2,1:T(8,128)}) %reduce-scatter.18.cloned.1.call-update) | async-done | bytes 32784 | tf_op jit(solution)/shard_map/reduce_scatter | solution.py:548
  1092.0 77.5 %reduce-scatter.14.cloned.1.call-done = f32[128,768]{1,0:T(8,128)} async-done(((f32[1024,768]{1,0:T(8,128)}), f32[128,768]{1,0:T(8,128)}) %reduce-scatter.14.cloned.1.call-update) | async-done | bytes 393232 | tf_op jit(solution)/shard_map/reduce_scatter | solution.py:546
  1169.5 152.4 %reduce-scatter.22.cloned.1.call-done = f32[256,1024]{1,0:T(8,128)} async-done(((f32[2048,1024]{1,0:T(8,128)}), f32[256,1024]{1,0:T(8,128)}) %reduce-scatter.22.cloned.1.call-update) | async-done | bytes 1048592 | tf_op jit(solution)/shard_map/reduce_scatter | solution.py:551
  (573 shorter events, 162.6 us)
Async XLA Ops:
  7.2 252.7 %copy-start = (bf16[1024,2,512]{2,1,0:T(2,128)(2,1)S(1)}, bf16[1024,2,512]{2,1,0:T(2,128)(2,1)}, u32[]{:S(2)}) copy-start(bf16[1024,2,512]{2,1,0:T(2,128)(2,1)} %param.40) | copy-start | bytes 6291460
  7.2 162.5 %all-gather.6.cloned.1.call-start = ((), (), s32[]{:S(2)}) async-start(), calls=%async_computation.20 | async-start | bytes 3538944 | tf_op jit(solution)/shard_map/all_gather | solution.py:29
  10.4 29.6 %copy-start.7 = (bf16[256,1024]{1,0:T(8,128)(2,1)}, bf16[256,1024]{1,0:T(8,128)(2,1)S(1)}, u32[]{:S(2)}) copy-start(bf16[256,1024]{1,0:T(8,128)(2,1)S(1)} %fusion.77) | copy-start | bytes 1572868
  11.4 17.0 %copy-start.141 = (s32[8]{0:T(128)S(1)}, s32[8]{0:T(128)}, u32[]{:S(2)}) copy-start(s32[8]{0:T(128)} %param.25) | copy-start | bytes 100
  11.4 18.4 %copy-start.116 = (s32[2048]{0:T(1024)S(1)}, s32[2048]{0:T(1024)}, u32[]{:S(2)}) copy-start(s32[2048]{0:T(1024)} %param.26) | copy-start | bytes 24580
  11.4 72.0 %collective-permute-start.1 = (bf16[3,64]{0,1:T(8,128)(2,1)}, bf16[3,64]{0,1:T(8,128)(2,1)}, u32[]{:S(2)}, u32[]{:S(2)}) collective-permute-start(bf16[3,64]{0,1:T(8,128)(2,1)} %bitcast.26), channel_id=1, source_target_pairs={{0,4},{4,8},{8,12},{12,16},{16,20},{20,24},{24,28},{1,5},{5,9},{9,... | collective-permute-start | bytes 1160 | tf_op jit(solution)/shard_map/ppermute | solution.py:24
  25.0 61.3 %collective-permute-start = (bf16[3,1536]{1,0:T(4,128)(2,1)}, bf16[3,1536]{1,0:T(4,128)(2,1)}, u32[]{:S(2)}, u32[]{:S(2)}) collective-permute-start(bf16[3,1536]{1,0:T(4,128)(2,1)} %slice_bitcast_fusion.4), channel_id=1, source_target_pairs={{0,4},{4,8},{8,12},{12,16},{16,20},{20,24},{24,28},{1,5},{5,9},{9,... | collective-permute-start | bytes 27656 | tf_op jit(solution)/shard_map/ppermute | solution.py:24
  40.1 47.6 %copy-start.91 = (f32[1536]{0:T(1024)}, f32[1536]{0:T(1024)S(1)}, u32[]{:S(2)}) copy-start(f32[1536]{0:T(1024)S(1)} %get-tuple-element.564) | copy-start | bytes 18436
  40.1 47.6 %copy-start.93 = (f32[1536]{0:T(1024)}, f32[1536]{0:T(1024)S(1)}, u32[]{:S(2)}) copy-start(f32[1536]{0:T(1024)S(1)} %get-tuple-element.565) | copy-start | bytes 18436
  40.3 39.2 %copy-start.60 = (f32[256,24]{0,1:T(8,128)}, f32[256,24]{0,1:T(8,128)S(1)}, u32[]{:S(2)}) copy-start(f32[256,24]{0,1:T(8,128)S(1)} %convolution_add_fusion.3) | copy-start | bytes 73732
  41.0 38.6 %copy-start.47 = (f32[24,2,128]{2,0,1:T(8,128)}, f32[24,2,128]{2,0,1:T(8,128)S(1)}, u32[]{:S(2)}) copy-start(f32[24,2,128]{2,0,1:T(8,128)S(1)} %reduce-window.14) | copy-start | bytes 73732
  41.2 38.4 %copy-start.107 = (f32[24,2]{0,1:T(2,128)}, f32[24,2]{0,1:T(2,128)S(1)}, u32[]{:S(2)}) copy-start(f32[24,2]{0,1:T(2,128)S(1)} %slice.234) | copy-start | bytes 580
  41.3 36.9 %copy-start.88 = (f32[256,24]{0,1:T(8,128)}, f32[256,24]{0,1:T(8,128)S(1)}, u32[]{:S(2)}) copy-start(f32[256,24]{0,1:T(8,128)S(1)} %bitcast_bitcast_fusion.1) | copy-start | bytes 73732
  41.3 34.2 %copy-start.114 = (s32[2048]{0:T(1024)S(1)}, s32[2048]{0:T(1024)}, u32[]{:S(2)}) copy-start(s32[2048]{0:T(1024)} %broadcast_add_fusion) | copy-start | bytes 24580
  41.3 34.2 %copy-start.128 = (s32[256]{0:T(256)S(1)}, s32[256]{0:T(256)}, u32[]{:S(2)}) copy-start(s32[256]{0:T(256)} %copy-done.127) | copy-start | bytes 3076
  41.5 38.1 %copy-start.132 = (pred[256]{0:T(512)(128)(4,1)S(1)}, pred[256]{0:T(512)(128)(4,1)}, u32[]{:S(2)}) copy-start(pred[256]{0:T(512)(128)(4,1)} %get-tuple-element.654) | copy-start | bytes 772
  41.5 38.1 %copy-start.137 = (f32[256]{0:T(256)S(1)}, f32[256]{0:T(256)}, u32[]{:S(2)}) copy-start(f32[256]{0:T(256)} %copy-done.136) | copy-start | bytes 3076
  74.8 22.8 %copy-start.27 = (bf16[2048,2,64]{0,2,1:T(8,128)(2,1)}, bf16[2048,2,64]{0,2,1:T(8,128)(2,1)S(1)}, u32[]{:S(2)}) copy-start(bf16[2048,2,64]{0,2,1:T(8,128)(2,1)S(1)} %all_gather.29) | copy-start | bytes 1572868
  78.2 45.9 %copy-start.23 = (pred[256,2048]{0,1:T(8,128)(4,1)}, pred[256,2048]{0,1:T(8,128)(4,1)S(1)}, u32[]{:S(2)}) copy-start(pred[256,2048]{0,1:T(8,128)(4,1)S(1)} %fusion.42) | copy-start | bytes 1572868
  97.5 156.0 %all-reduce.20.cloned.1.call-start = ((), (), s32[]{:S(2)}) async-start(), calls=%async_computation.9 | async-start | bytes 3145728 | tf_op jit(solution)/shard_map/psum | solution.py:340
  124.1 44.5 %copy-start.54 = (f32[256,64]{0,1:T(8,128)S(1)}, f32[256,64]{0,1:T(8,128)}, u32[]{:S(2)}) copy-start(f32[256,64]{0,1:T(8,128)} %copy-done.53) | copy-start | bytes 196612
  212.4 88.6 %all-reduce.22.cloned.1.call-start = ((), (), s32[]{:S(2)}) async-start(), calls=%async_computation.10 | async-start | bytes 2097152 | tf_op jit(solution)/shard_map/psum | solution.py:365
  223.9 33.2 %copy-start.58 = (bf16[256,512]{1,0:T(8,128)(2,1)}, bf16[256,512]{1,0:T(8,128)(2,1)S(1)}, u32[]{:S(2)}) copy-start(bf16[256,512]{1,0:T(8,128)(2,1)S(1)} %copy.157) | copy-start | bytes 786436
  259.8 43.4 %copy-start.130 = (f32[256]{0:T(256)}, f32[256]{0:T(256)S(1)}, u32[]{:S(2)}) copy-start(f32[256]{0:T(256)S(1)} %get-tuple-element.653) | copy-start | bytes 3076
  262.2 24.1 %copy-start.56 = (bf16[256,512]{1,0:T(8,128)(2,1)}, bf16[256,512]{1,0:T(8,128)(2,1)S(1)}, u32[]{:S(2)}) copy-start(bf16[256,512]{1,0:T(8,128)(2,1)S(1)} %get-tuple-element.621) | copy-start | bytes 786436
  264.7 36.3 %copy-start.20 = (f32[256,1024]{1,0:T(8,128)S(1)}, f32[256,1024]{1,0:T(8,128)}, u32[]{:S(2)}) copy-start(f32[256,1024]{1,0:T(8,128)} %copy-done.19) | copy-start | bytes 3145732
  264.7 194.6 %all-reduce.24.cloned.1.call-start = ((), (), s32[]{:S(2)}) async-start(), calls=%async_computation.21 | async-start | bytes 3670016 | tf_op jit(solution)/shard_map/psum | solution.py:355
  313.7 12.5 copy-start.9
  378.7 11.6 copy-start.13
  378.7 11.6 copy-start.70
  396.8 14.0 %collective-permute-start.2 = (f32[3,64]{0,1:T(8,128)S(1)}, f32[3,64]{0,1:T(8,128)S(1)}, u32[]{:S(2)}, u32[]{:S(2)}) collective-permute-start(f32[3,64]{0,1:T(8,128)S(1)} %pad_add_fusion.2), channel_id=1, source_target_pairs={{4,0},{8,4},{12,8},{16,12},{20,16},{24,20},{28,24},{5,1},{9,5},{13... | collective-permute-start | bytes 2312 | tf_op jit(solution)/shard_map/ppermute | solution.py:24
  398.1 12.8 copy-start.67
  412.0 115.0 %reduce-scatter.10.cloned.1.call-start = ((), (), s32[]{:S(2)}) async-start(), calls=%async_computation.11 | async-start | bytes 1179648 | tf_op jit(solution)/shard_map/reduce_scatter | solution.py:446
  412.1 16.3 %copy-start.50 = (bf16[256,8,32]{0,2,1:T(8,128)(2,1)S(1)}, bf16[256,8,32]{0,2,1:T(8,128)(2,1)}, u32[]{:S(2)}) copy-start(bf16[256,8,32]{0,2,1:T(8,128)(2,1)} %get-tuple-element.625) | copy-start | bytes 393220
  432.0 161.3 %reduce-scatter.12.cloned.1.call-start = ((), (), s32[]{:S(2)}) async-start(), calls=%async_computation.12 | async-start | bytes 1179648 | tf_op jit(solution)/shard_map/reduce_scatter | solution.py:452
  441.8 223.0 %reduce-scatter.26.cloned.1.call-start = ((), (), s32[]{:S(2)}) async-start(), calls=%async_computation.19 | async-start | bytes 2359296 | tf_op jit(solution)/shard_map/reduce_scatter | solution.py:554
  443.6 312.2 %reduce-scatter.24.cloned.1.call-start = ((), (), s32[]{:S(2)}) async-start(), calls=%async_computation.18 | async-start | bytes 4718592 | tf_op jit(solution)/shard_map/reduce_scatter | solution.py:553
  447.9 11.5 copy-start.156
  447.9 518.6 %reduce-scatter.16.cloned.1.call-start = ((), (), s32[]{:S(2)}) async-start(), calls=%async_computation.14 | async-start | bytes 14155776 | tf_op jit(solution)/shard_map/reduce_scatter | solution.py:547
  469.3 5.7 collective-permute-start.3
  481.7 545.7 %reduce-scatter.20.cloned.1.call-start = ((), (), s32[]{:S(2)}) async-start(), calls=%async_computation.16 | async-start | bytes 110592 | tf_op jit(solution)/shard_map/reduce_scatter | solution.py:549
  482.9 15.9 %copy-start.61 = (f32[256,24]{0,1:T(8,128)S(1)}, f32[256,24]{0,1:T(8,128)}, u32[]{:S(2)}) copy-start(f32[256,24]{0,1:T(8,128)} %copy-done.60) | copy-start | bytes 73732
  483.1 16.5 %copy-start.28 = (bf16[2048,2,64]{0,2,1:T(8,128)(2,1)S(1)}, bf16[2048,2,64]{0,2,1:T(8,128)(2,1)}, u32[]{:S(2)}) copy-start(bf16[2048,2,64]{0,2,1:T(8,128)(2,1)} %copy-done.27) | copy-start | bytes 1572868
  504.6 587.4 %reduce-scatter.18.cloned.1.call-start = ((), (), s32[]{:S(2)}) async-start(), calls=%async_computation.15 | async-start | bytes 294912 | tf_op jit(solution)/shard_map/reduce_scatter | solution.py:548
  505.7 663.8 %reduce-scatter.14.cloned.1.call-start = ((), (), s32[]{:S(2)}) async-start(), calls=%async_computation.13 | async-start | bytes 3538944 | tf_op jit(solution)/shard_map/reduce_scatter | solution.py:546
  596.6 725.4 %reduce-scatter.22.cloned.1.call-start = ((), (), s32[]{:S(2)}) async-start(), calls=%async_computation.17 | async-start | bytes 9437184 | tf_op jit(solution)/shard_map/reduce_scatter | solution.py:551
  620.4 39.6 %copy-start.142 = (f32[256]{0:T(256)S(1)}, f32[256]{0:T(256)}, u32[]{:S(2)}) copy-start(f32[256]{0:T(256)} %get-tuple-element.648) | copy-start | bytes 3076
  755.8 566.1 %copy-start.1 = (bf16[1024,2,512]{2,1,0:T(2,128)(2,1)S(1)}, bf16[1024,2,512]{2,1,0:T(2,128)(2,1)}, u32[]{:S(2)}) copy-start(bf16[1024,2,512]{2,1,0:T(2,128)(2,1)} %param.40) | copy-start | bytes 6291460
  (135 other events, 509.0 us)
Sparse Core Ops, SparseCore 0:
  97.6 66.8 all-gather.5
  212.5 40.9 all-reduce.19
  264.9 36.1 all-reduce.21
  412.2 47.1 all-reduce.23
  463.0 63.9 reduce-scatter.9
  530.3 62.9 reduce-scatter.11
  597.3 67.4 reduce-scatter.25
  668.8 86.9 reduce-scatter.23
  759.4 207.0 reduce-scatter.15
  970.2 57.0 reduce-scatter.19
  1031.2 60.7 reduce-scatter.17
  1096.0 73.4 reduce-scatter.13
  1173.7 148.1 reduce-scatter.21
where the time goes:
time: 1340 us; the launch traced here: 1330 us
  waiting for transfers between devices  796 us (59%)
  blocking collectives  197 us (15%)
  matrix products  138 us (10%)
  other arithmetic  91.9 us (7%)
  local copies, waits for them, and re-layouts  75.2 us (6%)
  between operations  17.3 us (1%)
    reduce_scatter x1, waiting for transfers between devices, local(): lax.psum_scatter(grad_mixer, 'seq', scatter_dimension=0, tiled=True)  208 us
    reduce_scatter x1, waiting for transfers between devices, local(): lax.psum_scatter(grad_joint, 'seq', scatter_dimension=0, tiled=True)  152 us
    reduce_scatter x1, waiting for transfers between devices, local(): lax.psum_scatter(grad_gate_up, 'seq', scatter_dimension=0, tiled=True)  89.3 us
    reduce_scatter x1, waiting for transfers between devices, local(): lax.psum_scatter(grad_attention, 'seq', scatter_dimension=0, tiled=True)  77.5 us
    reduce_scatter x1, waiting for transfers between devices, local(): lax.psum_scatter(value_block_gradients.reshape(overall_row_count, KEY_VAL...  65.4 us
    reduce_scatter x1, waiting for transfers between devices, local(): lax.psum_scatter(grad_state, 'seq', scatter_dimension=0, tiled=True)  64.7 us
    all_gather x2, blocking collectives, carried_in(): lax.all_gather(part.astype(kind), axis)  58.8 us
    reduce_scatter x1, waiting for transfers between devices, local(): lax.psum_scatter(grad_step, 'seq', scatter_dimension=0, tiled=True)  57 us
  transfers between devices with their start and end apart: 17, of which 13 were waited for; matrix products, arithmetic and copies ran while one was open for 13% of the time, Pallas kernels for 0%

commit v1 on v0

v1 whole, which is shorter than its diff:
```python
import math

import jax
import jax.numpy as jnp
from jax import lax
from jax.sharding import PartitionSpec as P

QUERY_HEADS = 8
KEY_VALUE_HEADS = 2
HEAD_SIZE = 64
NH = 24
HDM = 64
KC = 4
EPSILON = 1e-05
ROPE_BASE = 10000.0
HI = lax.Precision.HIGHEST
F32 = jnp.float32
BF16 = jnp.bfloat16
LANES = 128
HALO = 16
FAR = -1e30


def nn(a, b, p=None):
    return lax.dot_general(a, b, (((1,), (0,)), ((), ())), precision=p, preferred_element_type=F32)


def nt(a, b, p=None):
    return lax.dot_general(a, b, (((1,), (1,)), ((), ())), precision=p, preferred_element_type=F32)


def tn(a, b, p=None):
    return lax.dot_general(a, b, (((0,), (0,)), ((), ())), precision=p, preferred_element_type=F32)


def sigmoid(v):
    return 1.0 / (1.0 + jnp.exp(-v))


def silu(v):
    return v * sigmoid(v)


def silu_slope(v):
    s = sigmoid(v)
    return s * (1.0 + v * (1.0 - s))


def softplus(v):
    return jnp.maximum(v, 0.0) + jnp.log1p(jnp.exp(-jnp.abs(v)))


def iota(shape, dim):
    return lax.broadcasted_iota(jnp.int32, shape, dim)


def doc_of(starts, pos):
    found = jnp.full(pos.shape, -1, jnp.int32)
    for start in starts:
        found = found + (pos >= start).astype(jnp.int32)
    return found


def roll(v, shift):
    return jnp.roll(v, shift, axis=1)


def rope(v, cosine, sine, direction):
    first = (iota(v.shape, 1) % HEAD_SIZE) < HEAD_SIZE // 2
    half = HEAD_SIZE // 2
    partner = jnp.where(first, -roll(v, v.shape[1] - half), roll(v, half))
    return v * cosine + partner * (direction * sine)


def expander(width):
    return (iota((LANES, width), 1) // HDM == iota((LANES, width), 0)).astype(F32)


def conv_fwd(ext, taps, masks):
    rows = ext.shape[0] - HALO
    total = 0.0
    for k in range(KC):
        at = HALO - KC + 1 + k
        total = total + ext[at : at + rows] * taps[k : k + 1] * masks[k]
    return total


def conv_bwd(ext, taps, masks, up):
    rows = up.shape[0]
    total, weights = 0.0, []
    for k in range(KC):
        at = HALO - KC + 1 + k
        masked = up * masks[k]
        weights.append(jnp.sum(masked * ext[at : at + rows], axis=0, keepdims=True))
        parts = [jnp.zeros((at, up.shape[1]), F32), masked * taps[k : k + 1]]
        if KC - 1 - k:
            parts.append(jnp.zeros((KC - 1 - k, up.shape[1]), F32))
        total = total + jnp.concatenate(parts, axis=0)
    return total, jnp.concatenate(weights, axis=0)


def masks_of(starts, first_row, rows):
    pos = first_row + iota((rows, 1), 0)
    doc = doc_of(starts, pos)
    masks = [(doc_of(starts, pos - (KC - 1 - k)) == doc).astype(F32) for k in range(KC)]
    return doc, masks


def local(
    layer_input,
    out_grad,
    doc_starts,
    real_mask,
    norm_gain,
    attention_input_rows,
    mixer_in,
    state_in,
    step_in,
    conv_mixer,
    conv_state,
    step_bias,
    decay_rate,
    skip_gain,
    gated_gain,
    joint_out,
    mlp_gain,
    gate_up,
    down_weight,
):
    T, D = layer_input.shape
    NS, n = lax.axis_size("state"), lax.axis_size("seq")
    t, s = lax.axis_index("state"), lax.axis_index("seq")
    HL = NH // NS
    C = HL * HDM
    QC = QUERY_HEADS * HEAD_SIZE // NS
    TO = T // NS
    DM = NH * HDM
    NW = state_in.shape[2]
    AQ = QUERY_HEADS * HEAD_SIZE
    KW = KEY_VALUE_HEADS * HEAD_SIZE
    kvh = t * KEY_VALUE_HEADS // NS
    first_row = s * T
    starts = [doc_starts[k] for k in range(doc_starts.shape[0])]
    dsl = lax.dynamic_slice_in_dim

    w_q = dsl(attention_input_rows, QC * t, QC, 1)
    w_k = dsl(attention_input_rows, AQ + HEAD_SIZE * kvh, HEAD_SIZE, 1)
    w_v = dsl(attention_input_rows, AQ + KW + HEAD_SIZE * kvh, HEAD_SIZE, 1)
    w_qkv = jnp.concatenate([w_q, w_k, w_v], axis=1)
    w_mix = dsl(mixer_in, C * t, C, 2)
    w_mix = jnp.concatenate([w_mix[:, 0], w_mix[:, 1]], axis=1)
    w_step = jnp.pad(dsl(step_in, HL * t, HL, 1), ((0, 0), (0, LANES - HL)))
    pad_row = lambda v: jnp.pad(dsl(v, HL * t, HL, 0), (0, LANES - HL))[None, :]
    bias_row, rate_row = pad_row(step_bias), pad_row(decay_rate)
    skip_row = jnp.repeat(dsl(skip_gain, HL * t, HL, 0), HDM)[None, :]
    taps_mix = dsl(conv_mixer, C * t, C, 1)
    ggain_row = dsl(gated_gain, C * t, C, 0)[None, :]
    w_joint = jnp.concatenate([dsl(joint_out, QC * t, QC, 0), dsl(joint_out, AQ + C * t, C, 0)], axis=0)
    st_own = jnp.transpose(state_in, (1, 2, 0))
    taps_own = conv_state.reshape(KC, 2 * NW)
    w_gu = jnp.concatenate([gate_up[:, 0], gate_up[:, 1]], axis=1)
    F = gate_up.shape[2]
    ngain, mgain = norm_gain[None, :], mlp_gain[None, :]
    real_f = real_mask.astype(F32)
    real_col = dsl(real_f, first_row, T, 0)[:, None]
    all_doc = doc_of(starts, jnp.arange(n * T, dtype=jnp.int32)[None, :])[0]
    codes = jnp.where(real_mask > 0, all_doc, -7).reshape(n, 1, T)
    pos = first_row + jnp.arange(T, dtype=jnp.int32)
    firsts = jnp.max(jnp.where(doc_starts[None, :] <= pos[:, None], doc_starts[None, :], 0), axis=1)
    powers = (jnp.arange(LANES) % (HEAD_SIZE // 2)).astype(F32) * (2.0 / HEAD_SIZE)
    angles = (pos - firsts).astype(F32)[:, None] * jnp.exp(-math.log(ROPE_BASE) * powers)[None, :]
    cosine, sine = jnp.cos(angles), jnp.sin(angles)

    halo = lax.ppermute(layer_input[T - HALO :], "seq", [(i, (i + 1) % n) for i in range(n)])
    st_all = lax.all_gather(st_own, "state", axis=1, tiled=True).reshape(-1, D)
    taps_all = lax.all_gather(conv_state, "state", axis=2, tiled=True).reshape(KC, -1)

    doc, masks = masks_of(starts, first_row, T)
    x_ext = jnp.concatenate([halo, layer_input]).astype(F32)
    inv1 = lax.rsqrt(jnp.mean(x_ext * x_ext, axis=1, keepdims=True) + EPSILON)
    normed = (x_ext * inv1 * ngain).astype(BF16)
    main = normed[HALO:]
    qkv = nn(main, w_qkv)
    scale = 1.0 / math.sqrt(HEAD_SIZE)
    q = (rope(qkv[:, :QC], cosine, sine, 1.0).astype(BF16) * scale).astype(BF16)
    lane = iota((T, LANES), 1)
    is_k = lane < HEAD_SIZE
    kcos, ksin = jnp.where(is_k, cosine, 1.0), jnp.where(is_k, sine, 0.0)
    kv = rope(qkv[:, QC:], kcos, ksin, 1.0).astype(BF16)
    z = nn(main, w_mix[:, :C])
    inner_ext = nn(normed, w_mix[:, C:]).astype(BF16).astype(F32)
    state_ext = nt(normed, st_all).astype(BF16).astype(F32)
    step_raw = nn(main, w_step)
    inner_lin = conv_fwd(inner_ext, taps_mix, masks)
    inner = silu(inner_lin)
    state_conv = silu(conv_fwd(state_ext, taps_all, masks))
    N = state_conv.shape[1] // 2
    write, read = state_conv[:, :N], state_conv[:, N:]
    step = softplus(step_raw + bias_row)
    tri = (iota((T, T), 0) >= iota((T, T), 1)).astype(F32)
    cum = nn(tri, -step * rate_row, HI)
    cum_t = cum.T
    doc_row = doc.T
    linked = (doc == doc_row) & (iota((T, T), 0) >= iota((T, T), 1))
    inflow = step * real_col
    E = expander(C)
    g_mat = nt(read, write, HI)
    in_x = inner * nn(inflow, E, HI)

    def link(h):
        return jnp.exp(jnp.where(linked, cum[:, h : h + 1] - cum_t[h : h + 1, :], FAR))

    y = []
    for p in range(C // LANES):
        xp = in_x[:, LANES * p : LANES * (p + 1)]
        y0 = nn(link(2 * p) * g_mat, xp, HI)
        y1 = nn(link(2 * p + 1) * g_mat, xp, HI)
        y.append(jnp.where(is_k, y0, y1))
    y_intra = jnp.concatenate(y, axis=1)
    doc_last = doc[T - 1 : T]
    cum_last = cum[T - 1 : T]
    tail = jnp.where(doc == doc_last, jnp.exp(cum_last - cum), 0.0)
    tail_e = nn(tail, E, HI)
    state_part = tn(tail_e * in_x, write, HI)
    prior = doc_of(starts, jnp.full((1, 1), first_row - 1, jnp.int32))
    alive = (doc == prior).astype(F32)
    through = alive[T - 1 : T] * jnp.exp(cum_last)
    reach_e = nn(alive * jnp.exp(cum), E, HI)
    thr_col = tn(E, through.T, HI)

    def carry(value, direction):
        thr, total = thr_col, value
        move = lambda v, d: lax.ppermute(
            v, "seq", [(i, i + d * direction) for i in range(n) if 0 <= i + d * direction < n]
        )
        thr, total = move(thr, 1), move(total, 1)
        d = 1
        while d < n:
            thr_e, total_e = move(thr, d), move(total, d)
            total = total + thr * total_e
            thr = thr * thr_e
            d *= 2
        return total

    s_in = carry(state_part, 1)
    kv_all = lax.all_gather(kv, "seq")
    head0 = lane < HEAD_SIZE
    qf = q.astype(F32)
    q2 = jnp.where(
        jnp.concatenate([head0, head0]), jnp.concatenate([qf, roll(qf, HEAD_SIZE)]), 0.0
    ).astype(BF16)
    doc2 = jnp.concatenate([doc, doc])
    row2 = jnp.concatenate([iota((T, T), 0), iota((T, T), 0)])
    col2 = iota((2 * T, T), 1)

    def allowed_at(j):
        code = codes[j]
        return ((code == doc2) & ((j < s) | (col2 <= row2))) | ((j == s) & (col2 == row2))

    def attend(j, carried):
        m, l, acc = carried
        scores = jnp.where(allowed_at(j), nt(q2, kv_all[j]), FAR)
        m_new = jnp.maximum(m, jnp.max(scores, axis=1, keepdims=True))
        shrink = jnp.exp(m - m_new)
        p = jnp.exp(scores - m_new)
        return m_new, l * shrink + jnp.sum(p, axis=1, keepdims=True), acc * shrink + nn(
            p.astype(BF16), kv_all[j]
        )

    begin = attend(
        s, (jnp.full((2 * T, 1), FAR), jnp.zeros((2 * T, 1)), jnp.zeros((2 * T, LANES)))
    )
    m, l, acc = lax.fori_loop(0, s, attend, begin)
    out2 = acc / l
    lse = m + jnp.log(l)
    attended_f = jnp.where(head0, roll(out2[:T], HEAD_SIZE), out2[T:])
    attended = attended_f.astype(BF16)

    y_inter = reach_e * nt(read, s_in, HI)
    ssd = y_intra + y_inter
    full_mix = ssd + skip_row * inner
    gated = full_mix * silu(z)
    sumsq = lax.psum(jnp.sum(gated * gated, axis=1, keepdims=True), "state")
    inv_g = lax.rsqrt(sumsq / DM + EPSILON)
    joined = jnp.concatenate([attended, (gated * inv_g * ggain_row).astype(BF16)], axis=1)
    part = nn(joined, w_joint).astype(BF16)

    def rs_state(v):
        return lax.psum_scatter(v.astype(F32), "state", scatter_dimension=0, tiled=True)

    def ag_state(v):
        return lax.all_gather(v, "state", axis=0, tiled=True)

    x_own = dsl(layer_input, TO * t, TO, 0).astype(F32)
    res = x_own + rs_state(part)
    inv2 = lax.rsqrt(jnp.mean(res * res, axis=1, keepdims=True) + EPSILON)
    n2 = ag_state((res * inv2 * mgain).astype(BF16))

    gu = nn(n2, w_gu)
    gate, up = gu[:, :F], gu[:, F:]
    dh = nn(out_grad, down_weight)
    sig = sigmoid(gate)
    act = gate * sig
    hidden = (act * up).astype(BF16)
    d_gu = jnp.concatenate(
        [dh * up * (sig * (1.0 + gate * (1.0 - sig))), dh * act], axis=1
    ).astype(BF16)
    mlp_part = nt(hidden, down_weight).astype(BF16)
    dn2_part = nt(d_gu, w_gu).astype(BF16)
    gw_down = tn(out_grad, hidden).astype(BF16)
    gw_gu = tn(n2, d_gu).astype(BF16)
    layer_output = ag_state((res + rs_state(mlp_part)).astype(BF16))
    dn2 = rs_state(dn2_part)
    g_own = dsl(out_grad, TO * t, TO, 0).astype(F32)
    scaled = dn2 * mgain
    d_res = g_own + inv2 * scaled - res * inv2**3 * jnp.mean(scaled * res, axis=1, keepdims=True)
    g_mgain = jnp.sum(dn2 * res * inv2, axis=0, keepdims=True)
    d_branch = ag_state(d_res.astype(BF16))

    d_joined = nt(d_branch, w_joint)
    gw_joint = tn(joined, d_branch).astype(BF16)
    d_att = d_joined[:, :QC].astype(BF16).astype(F32)
    d_gn = d_joined[:, QC:]
    scaled_g = d_gn * ggain_row
    row_dot = lax.psum(jnp.sum(scaled_g * gated, axis=1, keepdims=True), "state") / DM
    d_gated = inv_g * scaled_g - gated * inv_g**3 * row_dot
    g_ggain = jnp.sum(d_gn * gated * inv_g, axis=0, keepdims=True)
    sig_z = sigmoid(z)
    dy = d_gated * z * sig_z
    d_z = d_gated * full_mix * (sig_z * (1.0 + z * (1.0 - sig_z)))
    g_skip = jnp.sum(dy * inner, axis=0, keepdims=True)
    direct = tn(reach_e * dy, read, HI)
    later = carry(direct, -1)

    dout2 = jnp.where(
        jnp.concatenate([head0, head0]), 0.0, jnp.concatenate([roll(d_att, HEAD_SIZE), d_att])
    )
    delta = jnp.sum(dout2 * out2, axis=1, keepdims=True)
    dout2 = dout2.astype(BF16)

    def attend_back(j, carried):
        dq2, dkv = carried
        scores = jnp.where(allowed_at(j), nt(q2, kv_all[j]), FAR)
        p = jnp.exp(scores - lse)
        ds = (p * (nt(dout2, kv_all[j]) - delta)).astype(BF16)
        dkv = lax.dynamic_update_index_in_dim(dkv, tn(ds, q2) + tn(p.astype(BF16), dout2), j, 0)
        return dq2 + nn(ds, kv_all[j]), dkv

    dq2, dkv_all = lax.fori_loop(
        0, s + 1, attend_back, (jnp.zeros((2 * T, LANES)), jnp.zeros((n, T, LANES)))
    )
    dq = jnp.where(head0, dq2[:T], roll(dq2[T:], HEAD_SIZE)) * scale
    d_q = rope(dq, cosine, sine, -1.0).astype(BF16)
    dkv = lax.psum_scatter(dkv_all, "seq", scatter_dimension=0, tiled=False)
    pair = NS // KEY_VALUE_HEADS
    groups = [[g * pair + i for i in range(pair)] for g in range(KEY_VALUE_HEADS)]
    dkv = lax.psum(dkv, "state", axis_index_groups=groups)
    d_kv = rope(dkv, kcos, ksin, -1.0).astype(BF16)

    w_r = nt(write, later, HI)
    tail_r = tail_e * w_r
    d_g = 0.0
    ws = []
    for p in range(C // LANES):
        xp = in_x[:, LANES * p : LANES * (p + 1)]
        dyp = dy[:, LANES * p : LANES * (p + 1)]
        halves = []
        for k in range(2):
            lk = link(2 * p + k)
            mine = is_k if k == 0 else ~is_k
            halves.append(tn(lk * g_mat, dyp, HI))
            d_g = d_g + lk * nt(jnp.where(mine, dyp, 0.0), xp, HI)
        ws.append(jnp.where(is_k, halves[0], halves[1]))
    w_intra = jnp.concatenate(ws, axis=1)
    w_tot = w_intra + tail_r
    ET = E.T
    inflow_e = nn(inflow, E, HI)
    u = nn(inner * w_tot, ET, HI)
    tl = nn(in_x * tail_r, ET, HI)
    dx = inflow_e * w_tot
    thr_s = nn(jnp.sum((later * s_in), axis=1, keepdims=True).T, ET, HI) * through
    d_cum = nn(dy * ssd, ET, HI) - inflow * u
    last = iota((T, LANES), 0) == T - 1
    d_cum = d_cum + jnp.where(last, jnp.sum(tl, axis=0, keepdims=True) + thr_s, 0.0)
    d_ld = tn(tri, d_cum, HI)
    d_step = real_col * u - rate_row * d_ld
    g_rate = -jnp.sum(step * d_ld, axis=0, keepdims=True)
    d_read = nn(d_g, write, HI) + nn(reach_e * dy, s_in, HI)
    d_write = tn(d_g, read, HI) + nn(tail_e * in_x, later, HI)
    d_step_f = d_step * sigmoid(step_raw + bias_row)
    g_bias = jnp.sum(d_step_f, axis=0, keepdims=True)
    d_step_b = d_step_f.astype(BF16)
    d_inner_lin = (dx + skip_row * dy) * silu_slope(inner_lin)
    d_inner_ext, g_taps_mix = conv_bwd(inner_ext, taps_mix, masks, d_inner_lin)
    wr_t = jnp.concatenate([d_write.T, d_read.T], axis=0).reshape(2, NS, NW, T).transpose(1, 0, 2, 3)
    wr_own = lax.psum_scatter(wr_t, "state", scatter_dimension=0, tiled=False).reshape(2 * NW, T).T
    st_ext_own = nt(normed, st_own.reshape(-1, D)).astype(BF16).astype(F32)
    d_st_lin = wr_own * silu_slope(conv_fwd(st_ext_own, taps_own, masks))
    d_st_ext, g_taps_st = conv_bwd(st_ext_own, taps_own, masks, d_st_lin)
    d_st_ext = d_st_ext.astype(BF16)
    d_inner_ext = d_inner_ext.astype(BF16)
    d_z = d_z.astype(BF16)
    gw_mix = jnp.concatenate([tn(main, d_z), tn(normed, d_inner_ext)], axis=1).astype(BF16)
    gw_st = tn(normed, d_st_ext).astype(BF16)
    gw_step = tn(main, d_step_b).astype(BF16)
    odd = t % pair
    d_kv_mine = jnp.where(is_k == (odd == 0), d_kv, jnp.zeros_like(d_kv))
    gw_q = tn(main, d_q).astype(BF16)
    gw_kv = tn(main, d_kv).astype(BF16)
    gw_kv = jnp.where(odd == 0, gw_kv[:, :HEAD_SIZE], gw_kv[:, HEAD_SIZE:])
    halo_part = nt(d_inner_ext[:HALO], w_mix[:, C:]) + nn(d_st_ext[:HALO], st_own.reshape(-1, D))
    back = lax.ppermute(halo_part, "seq", [((i + 1) % n, i) for i in range(n)])
    d_n = (
        nt(jnp.concatenate([d_q, d_kv_mine], axis=1), w_qkv)
        + nt(jnp.concatenate([d_z, d_inner_ext[HALO:]], axis=1), w_mix)
        + nn(d_st_ext[HALO:], st_own.reshape(-1, D))
        + nt(d_step_b, w_step)
    )
    d_n = jnp.concatenate([d_n[: T - HALO], d_n[T - HALO :] + back])
    d_n = rs_state(d_n.astype(BF16))
    inv1_own = dsl(inv1, HALO + TO * t, TO, 0)
    scaled_n = d_n * ngain
    in_g = d_res + inv1_own * scaled_n - x_own * inv1_own**3 * jnp.mean(
        scaled_n * x_own, axis=1, keepdims=True
    )
    g_ngain = jnp.sum(d_n * x_own * inv1_own, axis=0, keepdims=True)
    input_grad = ag_state(in_g)

    def rs_seq(v):
        return lax.psum_scatter(v, "seq", scatter_dimension=0, tiled=True)

    r_down, r_gu = rs_seq(gw_down), rs_seq(gw_gu)
    r_a = rs_seq(jnp.concatenate([gw_q, gw_kv, gw_mix, gw_step[:, :HL], gw_st], axis=1))
    rows = D // n
    gj = lax.all_gather(gw_joint, "state", axis=0)
    gj = jnp.concatenate([gj[:, :QC].reshape(AQ, D), gj[:, QC:].reshape(DM, D)], axis=0)
    r_joint = lax.psum_scatter(gj, "seq", scatter_dimension=0, tiled=True)
    W = QC + HEAD_SIZE + 2 * C + HL
    ga = lax.all_gather(r_a[:, :W], "state", axis=1)
    g_att = jnp.concatenate(
        [ga[:, :, :QC].reshape(rows, AQ)]
        + [ga[:, h * pair + k, QC : QC + HEAD_SIZE] for k in range(2) for h in range(KEY_VALUE_HEADS)],
        axis=1,
    )
    o = QC + HEAD_SIZE
    g_mix = jnp.stack(
        [ga[:, :, o : o + C].reshape(rows, DM), ga[:, :, o + C : o + 2 * C].reshape(rows, DM)], axis=1
    )
    g_step = ga[:, :, o + 2 * C :].reshape(rows, NH)
    g_st = r_a[:, W:].reshape(rows, 2, NW)
    sums = lax.psum((g_ngain, g_mgain), ("seq", "state"))
    small = lax.psum(
        (g_ggain, g_taps_mix, g_taps_st, g_bias[:, :HL], g_rate[:, :HL], g_skip), "seq"
    )
    s_ggain, s_taps, s_st, s_bias, s_rate, s_skip = small
    s_skip = jnp.sum(s_skip.reshape(1, HL, HDM), axis=2)
    cat = lambda v: lax.all_gather(v, "state", axis=1, tiled=True)
    s_ggain, s_taps, s_bias, s_rate, s_skip = map(cat, (s_ggain, s_taps, s_bias, s_rate, s_skip))
    take = lambda v: dsl(v[0], s * (v.shape[1] // n), v.shape[1] // n, 0)
    f = lambda v: v.astype(F32)
    return (
        layer_output,
        input_grad,
        take(sums[0]),
        f(g_att),
        f(g_mix),
        f(g_st),
        f(g_step),
        s_taps,
        s_st.reshape(KC, 2, NW),
        s_bias[0],
        s_rate[0],
        s_skip[0],
        take(s_ggain),
        f(r_joint),
        take(sums[1]),
        f(r_gu).reshape(rows, 2, F),
        f(r_down),
    )


def solution(mesh):
    rep = P()
    in_specs = (
        P("seq", None),
        P("seq", None),
        rep,
        rep,
        rep,
        rep,
        rep,
        P(None, None, "state"),
        rep,
        rep,
        P(None, None, "state"),
        rep,
        rep,
        rep,
        rep,
        rep,
        rep,
        P(None, None, "state"),
        P(None, "state"),
    )
    out_specs = (
        P("seq", None),
        P("seq", None),
        P("seq"),
        P("seq", None),
        P("seq", None, None),
        P("seq", None, "state"),
        P("seq", None),
        rep,
        P(None, None, "state"),
        rep,
        rep,
        rep,
        P("seq"),
        P("seq", None),
        P("seq"),
        P("seq", None, "state"),
        P("seq", "state"),
    )
    return jax.shard_map(local, mesh=mesh, in_specs=in_specs, out_specs=out_specs, check_vma=False)
```

time: 1340 us -> 940 us (0.70)
  waiting for transfers between devices: 796 us -> 433 us
  matrix products: 138 us -> 69.5 us
  starting transfers between devices: 12.3 us -> 58.2 us
  other arithmetic: 91.9 us -> 68.7 us
  local copies, waits for them, and re-layouts: 75.2 us -> 90.9 us
  blocking collectives: 197 us -> 183 us
    reduce_scatter x9 -> x7, waiting for transfers between devices: 739 us -> 214 us  [the longest x1 74.3 us: local(): r_joint = lax.psum_scatter(gj, 'seq', scatter_dimension=0, tiled=True)]
    unnamed x13 -> x16, waiting for transfers between devices: 0.22 us -> 118 us
    psum x2 -> x4, blocking collectives: 16.8 us -> 87.6 us  [the longest x1 40 us: local(): sums = lax.psum((g_ngain, g_mgain), ('seq', 'state'))]
    dot_general x37 -> x71, matrix products: 137 us -> 69.5 us  [the longest x28 27.7 us: nn(): lax.dot_general(a, b, (((1,), (0,)), ((), ())), precision=p, preferred_el...]
    ppermute x4 -> x16, waiting for transfers between devices: 3.68 us -> 61.5 us  [the longest x14 61.5 us: carry(): lax.ppermute(v, 'seq', [(i, i + d * direction) for i in range(n) if 0 <=...]
    all_gather x5 -> x9, blocking collectives: 143 us -> 88.3 us  [the longest x1 33.6 us: local(): kv_all = lax.all_gather(kv, 'seq')]
    ppermute x4 -> x16, starting transfers between devices: 11.6 us -> 57.2 us  [the longest x14 51.9 us: carry(): lax.ppermute(v, 'seq', [(i, i + d * direction) for i in range(n) if 0 <=...]
    psum x3 -> x1, waiting for transfers between devices: 53.2 us -> 15.2 us  [local(): dkv = lax.psum(dkv, 'state', axis_index_groups=groups)]
  transfers between devices with their start and end apart: 17 -> 29, of which waited for: 13 -> 18; matrix products, arithmetic and copies ran while one was open for 13% -> 18% of each run, Pallas kernels for 0% -> 0%
where the time goes in v1:
time: 940 us; the launch traced here: 928 us
  waiting for transfers between devices  433 us (46%)
  blocking collectives  183 us (19%)
  local copies, waits for them, and re-layouts  90.9 us (10%)
  matrix products  69.5 us (7%)
  other arithmetic  68.7 us (7%)
  starting transfers between devices  58.2 us (6%)
  between operations  23.8 us (3%)
    unnamed x16, waiting for transfers between devices  118 us
    reduce_scatter x1, waiting for transfers between devices, local(): r_joint = lax.psum_scatter(gj, 'seq', scatter_dimension=0, tiled=True)  74.3 us
    reduce_scatter x1, waiting for transfers between devices, local(): dkv = lax.psum_scatter(dkv_all, 'seq', scatter_dimension=0, tiled=False)  63.9 us
    reduce_scatter x4, waiting for transfers between devices, rs_state(): lax.psum_scatter(v.astype(F32), 'state', scatter_dimension=0, tiled=True)  62.3 us
    ppermute x14, waiting for transfers between devices, carry(): lax.ppermute(v, 'seq', [(i, i + d * direction) for i in range(n) if 0 <=...  61.5 us
    ppermute x14, starting transfers between devices, carry(): lax.ppermute(v, 'seq', [(i, i + d * direction) for i in range(n) if 0 <=...  51.9 us
    psum x1, blocking collectives, local(): sums = lax.psum((g_ngain, g_mgain), ('seq', 'state'))  40 us
    psum x1, blocking collectives, local(): lax.psum((g_ggain, g_taps_mix, g_taps_st, g_bias[:, :HL], g_rate[:, :HL],...  35.4 us
  transfers between devices with their start and end apart: 29, of which 18 were waited for; matrix products, arithmetic and copies ran while one was open for 18% of the time, Pallas kernels for 0%

profile of v1, /device:TPU:0, one launch (start us, length us, event | category | flops | bytes accessed | tf_op | source)
XLA Modules:
  0.0 927.9 jit_solution(7541552607275414953)
XLA Ops:
  13.8 5.8 compare_convert_fusion.27
  19.6 5.2 fusion.366
  36.1 5.2 add_select_fusion
  41.9 7.6 all_gather.53
  49.7 5.4 all_gather.54
  61.5 6.4 compare_convert_fusion.18
  67.9 6.8 constant_dynamic-slice_fusion.3
  104.8 4.1 collective-permute-start.1
  109.7 3.8 collective-permute-start.2
  115.4 33.6 %all-gather = bf16[2048,128]{0,1:T(8,128)(2,1)} all-gather(bf16[256,128]{0,1:T(8,128)(2,1)S(1)} %fusion.143), channel_id=2, replica_groups=mesh['seq'=8,'state'=4] {'seq'}, dimensions={0}, use_global_device_ids=true | all-gather | bytes 589824 | tf_op jit(solution)/shard_map/all_gather | solution.py:246
  163.7 6.6 collective-permute-start.3
  171.0 6.5 collective-permute-start.6
  178.5 10.1 %collective-permute-start.5 = (f32[384,128]{1,0:T(8,128)S(1)}, f32[384,128]{1,0:T(8,128)S(1)}, u32[]{:S(2)}, u32[]{:S(2)}) collective-permute-start(f32[384,128]{1,0:T(8,128)S(1)} %multiply_add_fusion.8), channel_id=1, source_target_pairs={{0,8},{4,12},{8,16},{12,20},{16,24},{20,28},{1,9},{5,13},{9,17},{1... | collective-permute-start | bytes 589832 | tf_op jit(solution)/shard_map/ppermute | solution.py:233
  188.7 4.1 collective-permute-done.5
  192.9 9.2 collective-permute-start.7
  207.4 5.8 psum.77
  217.7 5.6 fusion.415
  225.2 19.6 %reduce-scatter.17.cloned.1.call-done = f32[64,1024]{1,0:T(8,128)} async-done(((f32[256,1024]{1,0:T(8,128)}), f32[64,1024]{1,0:T(8,128)}) %reduce-scatter.17.cloned.1.call-update) | async-done | bytes 262160 | tf_op jit(solution)/shard_map/reduce_scatter | solution.py:289
  246.5 6.8 all_gather.55
  276.0 3.8 collective-permute-done.11
  282.3 4.4 collective-permute-done.13
  289.0 24.2 %reduce-scatter.19.cloned.1.call-done = f32[64,1024]{1,0:T(8,128)} async-done(((f32[256,1024]{1,0:T(8,128)}), f32[64,1024]{1,0:T(8,128)}) %reduce-scatter.19.cloned.1.call-update) | async-done | bytes 262160 | tf_op jit(solution)/shard_map/reduce_scatter | solution.py:289
  315.2 6.8 all_gather.57
  325.4 6.5 psum.79
  332.0 3.0 multiply_reduce_fusion.1
  352.1 3.7 while.31
  357.8 10.9 %collective-permute-done.10 = f32[384,128]{1,0:T(8,128)S(1)} collective-permute-done((f32[384,128]{1,0:T(8,128)}, f32[384,128]{1,0:T(8,128)S(1)}, u32[]{:S(2)}, u32[]{:S(2)}) %collective-permute-start.10) | collective-permute-done | bytes 196640 | tf_op jit(solution)/shard_map/ppermute | solution.py:233
  371.2 13.1 %collective-permute-done.12 = f32[384,128]{1,0:T(8,128)S(1)} collective-permute-done((f32[384,128]{1,0:T(8,128)S(1)}, f32[384,128]{1,0:T(8,128)S(1)}, u32[]{:S(2)}, u32[]{:S(2)}) %collective-permute-start.12) | collective-permute-done | bytes 196640 | tf_op jit(solution)/shard_map/ppermute | solution.py:233
  385.8 22.8 %collective-permute-done.14 = f32[384,128]{1,0:T(8,128)S(1)} collective-permute-done((f32[384,128]{1,0:T(8,128)S(1)}, f32[384,128]{1,0:T(8,128)S(1)}, u32[]{:S(2)}, u32[]{:S(2)}) %collective-permute-start.14) | collective-permute-done | bytes 196640 | tf_op jit(solution)/shard_map/ppermute | solution.py:233
  411.6 3.6 multiply_reduce_fusion.5
  421.9 16.6 %all-reduce.17.cloned.1.call-done = f32[4,2,32,256]{3,2,0,1:T(8,128)} async-done(((f32[4,2,32,256]{3,2,0,1:T(8,128)}), f32[4,2,32,256]{3,2,0,1:T(8,128)}) %all-reduce.17.cloned.1.call-update) | async-done | bytes 262160
  441.9 63.9 %reduce-scatter.23.cloned.1.call-done = f32[1,256,128]{1,2,0:T(8,128)} async-done(((f32[8,256,128]{1,2,0:T(8,128)}), f32[1,256,128]{1,2,0:T(8,128)}) %reduce-scatter.23.cloned.1.call-update) | async-done | bytes 131088 | tf_op jit(solution)/shard_map/reduce_scatter | solution.py:354
  509.8 15.2 %all-reduce.15.cloned.1.call-done = f32[256,128]{0,1:T(8,128)} async-done(((f32[256,128]{0,1:T(8,128)}), f32[256,128]{0,1:T(8,128)}) %all-reduce.15.cloned.1.call-update) | async-done | bytes 131088 | tf_op jit(solution)/shard_map/psum | solution.py:357
  536.5 3.2 convolution_convert_fusion
  540.6 18.6 %reduce-scatter.25.cloned.1.call-done = f32[64,1024]{1,0:T(8,128)} async-done(((f32[256,1024]{1,0:T(8,128)}), f32[64,1024]{1,0:T(8,128)}) %reduce-scatter.25.cloned.1.call-update) | async-done | bytes 262160 | tf_op jit(solution)/shard_map/reduce_scatter | solution.py:289
  565.1 3.5 concatenate.176
  571.6 24.3 %all-gather.10.cloned.1.call-done = bf16[2048,1024]{1,0:T(8,128)(2,1)} async-done(((bf16[512,1024]{1,0:T(8,128)(2,1)}), bf16[2048,1024]{1,0:T(8,128)(2,1)}) %all-gather.10.cloned.1.call-update) | async-done | bytes 4194320 | tf_op jit(solution)/shard_map/all_gather | solution.py:435
  602.7 7.6 all_gather.56
  610.4 52.8 %reduce-scatter.33.cloned.1.call-done = bf16[128,512]{1,0:T(8,128)(2,1)} async-done(((bf16[1024,512]{1,0:T(8,128)(2,1)}), bf16[128,512]{1,0:T(8,128)(2,1)}) %reduce-scatter.33.cloned.1.call-update) | async-done | bytes 131088
  665.3 35.4 %all-reduce.10 = (f32[4,384]{1,0:T(4,128)S(1)}, f32[4,2,32]{2,1,0:T(2,128)}, f32[1,6]{1,0:T(1,128)S(1)}, f32[1,6]{1,0:T(1,128)S(1)}, f32[6,64]{1,0:T(8,128)S(1)}, /*index=5*/f32[1,384]{1,0:T(1,128)S(1)}) all-reduce(f32[4,384]{1,0:T(4,128)S(1)} %pad_maximum_fusion.22, ...), channel_id=1, replica_groups=mesh['seq'=8,'state'=4] {'seq'}, use_global_device_ids=true, to_apply=%region_34.35 | all-reduce | flops 2572 | bytes 20576 | tf_op jit(solution)/shard_map/psum | solution.py:452
  700.7 5.6 all_gather.61
  706.9 7.5 all-reduce.11
  714.4 5.1 all_gather.65
  720.2 13.7 %reduce-scatter.29.cloned.1.call-done = bf16[128,1024]{1,0:T(8,128)(2,1)} async-done(((bf16[1024,1024]{1,0:T(8,128)(2,1)}), bf16[128,1024]{1,0:T(8,128)(2,1)}) %reduce-scatter.29.cloned.1.call-update) | async-done | bytes 262160 | tf_op jit(solution)/shard_map/reduce_scatter | solution.py:430
  736.1 40.0 %all-reduce.9 = (f32[1,1024]{1,0:T(1,128)S(1)}, f32[1,1024]{1,0:T(1,128)S(1)}) all-reduce(f32[1,1024]{1,0:T(1,128)S(1)} %bitcast.350, f32[1,1024]{1,0:T(1,128)S(1)} %bitcast.349), channel_id=1, replica_groups=mesh['seq'=8,'state'=4] {'seq','state'}, use_global_device_ids=true, to_apply=%region_28.29 | all-reduce | flops 2048 | bytes 16384 | tf_op jit(solution)/shard_map/psum | solution.py:451
  777.1 48.1 %reduce-scatter.31.cloned.1.call-done = bf16[128,1030]{1,0:T(8,128)(2,1)} async-done(((bf16[1024,1030]{1,0:T(8,128)(2,1)}), bf16[128,1030]{1,0:T(8,128)(2,1)}) %reduce-scatter.31.cloned.1.call-update) | async-done | bytes 263696
  826.3 9.7 %all-gather.4 = bf16[4,966,128]{2,1,0:T(8,128)(2,1)S(1)} all-gather(bf16[1,966,128]{2,1,0:T(8,128)(2,1)S(1)} %bitcast.326), channel_id=3, replica_groups=mesh['seq'=8,'state'=4] {'state'}, dimensions={0}, use_global_device_ids=true | all-gather | bytes 1236480 | tf_op jit(solution)/shard_map/all_gather | solution.py:439
  842.1 74.3 %reduce-scatter.27.cloned.1.call-done = bf16[256,1024]{1,0:T(8,128)(2,1)} async-done(((bf16[2048,1024]{1,0:T(8,128)(2,1)}), bf16[256,1024]{1,0:T(8,128)(2,1)}) %reduce-scatter.27.cloned.1.call-update) | async-done | bytes 524304 | tf_op jit(solution)/shard_map/reduce_scatter | solution.py:437
  (685 shorter events, 201.9 us)
Async XLA Ops:
  7.2 248.6 %copy-start = (bf16[1024,512]{1,0:T(8,128)(2,1)S(1)}, bf16[1024,512]{1,0:T(8,128)(2,1)}, u32[]{:S(2)}) copy-start(bf16[1024,512]{1,0:T(8,128)(2,1)} %param.41) | copy-start | bytes 3145732
  7.2 237.5 %reduce-scatter.17.cloned.1.call-start = ((), (), s32[]{:S(2)}) async-start(), calls=%async_computation.9 | async-start | bytes 1310720 | tf_op jit(solution)/shard_map/reduce_scatter | solution.py:289
  8.7 82.7 %collective-permute-start = (bf16[16,1024]{1,0:T(8,128)(2,1)}, bf16[16,1024]{1,0:T(8,128)(2,1)}, u32[]{:S(2)}, u32[]{:S(2)}) collective-permute-start(bf16[16,1024]{1,0:T(8,128)(2,1)} %slice.418), channel_id=1, source_target_pairs={{0,4},{4,8},{8,12},{12,16},{16,20},{20,24},{24,28},{28,0},{1,5},{5... | collective-permute-start | bytes 98312 | tf_op jit(solution)/shard_map/ppermute | solution.py:174
  11.7 97.2 %copy-start.71 = (s32[384]{0:T(512)}, s32[384]{0:T(512)S(1)}, u32[]{:S(2)}) copy-start(s32[384]{0:T(512)S(1)} %broadcast_add_fusion) | copy-start | bytes 4612
  104.8 58.9 %collective-permute-start.1 = (f32[384,128]{1,0:T(8,128)}, f32[384,128]{1,0:T(8,128)}, u32[]{:S(2)}, u32[]{:S(2)}) collective-permute-start(f32[384,128]{1,0:T(8,128)} %fusion.251), channel_id=1, source_target_pairs={{0,4},{4,8},{8,12},{12,16},{16,20},{20,24},{24,28},{1,5},{5,9},{9,... | collective-permute-start | bytes 589832 | tf_op jit(solution)/shard_map/ppermute | solution.py:233
  109.7 51.4 %collective-permute-start.2 = (f32[384,1]{0,1:T(1,128)}, f32[384,1]{0,1:T(1,128)}, u32[]{:S(2)}, u32[]{:S(2)}) collective-permute-start(f32[384,1]{0,1:T(1,128)} %convolution_bitcast_fusion.2), channel_id=1, source_target_pairs={{0,4},{4,8},{8,12},{12,16},{16,20},{20,24},{24,28},{1,5},{5,9},{9,... | collective-permute-start | bytes 4616 | tf_op jit(solution)/shard_map/ppermute | solution.py:233
  161.1 9.2 collective-permute-start.4
  163.7 13.8 %collective-permute-start.3 = (f32[384,128]{1,0:T(8,128)}, f32[384,128]{1,0:T(8,128)S(1)}, u32[]{:S(2)}, u32[]{:S(2)}) collective-permute-start(f32[384,128]{1,0:T(8,128)} %collective-permute-done.1), channel_id=1, source_target_pairs={{0,4},{4,8},{8,12},{12,16},{16,20},{20,24},{24,28},{1,5},{5,9},{9,... | collective-permute-start | bytes 589832 | tf_op jit(solution)/shard_map/ppermute | solution.py:233
  171.0 17.7 %collective-permute-start.6 = (f32[384,1]{0,1:T(1,128)S(1)}, f32[384,1]{0,1:T(1,128)S(1)}, u32[]{:S(2)}, u32[]{:S(2)}) collective-permute-start(f32[384,1]{0,1:T(1,128)S(1)} %get-tuple-element.758), channel_id=1, source_target_pairs={{0,8},{4,12},{8,16},{12,20},{16,24},{20,28},{1,9},{5,13},{9,17},{1... | collective-permute-start | bytes 4616 | tf_op jit(solution)/shard_map/ppermute | solution.py:233
  178.5 14.2 %collective-permute-start.5 = (f32[384,128]{1,0:T(8,128)S(1)}, f32[384,128]{1,0:T(8,128)S(1)}, u32[]{:S(2)}, u32[]{:S(2)}) collective-permute-start(f32[384,128]{1,0:T(8,128)S(1)} %multiply_add_fusion.8), channel_id=1, source_target_pairs={{0,8},{4,12},{8,16},{12,20},{16,24},{20,28},{1,9},{5,13},{9,17},{1... | collective-permute-start | bytes 589832 | tf_op jit(solution)/shard_map/ppermute | solution.py:233
  192.9 12.3 %collective-permute-start.7 = (f32[384,128]{1,0:T(8,128)S(1)}, f32[384,128]{1,0:T(8,128)S(1)}, u32[]{:S(2)}, u32[]{:S(2)}) collective-permute-start(f32[384,128]{1,0:T(8,128)S(1)} %multiply_add_fusion.7), channel_id=1, source_target_pairs={{0,16},{4,20},{8,24},{12,28},{1,17},{5,21},{9,25},{13,29},{2,18},{... | collective-permute-start | bytes 589832 | tf_op jit(solution)/shard_map/ppermute | solution.py:233
  217.6 69.7 %reduce-scatter.21.cloned.1.call-start = ((), (), s32[]{:S(2)}) async-start(), calls=%async_computation.11 | async-start | bytes 1310720 | tf_op jit(solution)/shard_map/reduce_scatter | solution.py:289
  259.7 53.5 %reduce-scatter.19.cloned.1.call-start = ((), (), s32[]{:S(2)}) async-start(), calls=%async_computation.10 | async-start | bytes 1310720 | tf_op jit(solution)/shard_map/reduce_scatter | solution.py:289
  262.2 176.4 %all-reduce.17.cloned.1.call-start = ((), (), s32[]{:S(2)}) async-start(), calls=%async_computation.21 | async-start | bytes 524288
  264.6 9.1 collective-permute-start.9
  273.7 6.1 collective-permute-start.11
  280.4 6.3 collective-permute-start.13
  345.4 11.0 %collective-permute-start.8 = (f32[384,128]{1,0:T(8,128)}, f32[384,128]{1,0:T(8,128)}, u32[]{:S(2)}, u32[]{:S(2)}) collective-permute-start(f32[384,128]{1,0:T(8,128)} %fusion.112), channel_id=1, source_target_pairs={{4,0},{8,4},{12,8},{16,12},{20,16},{24,20},{28,24},{5,1},{9,5},{13... | collective-permute-start | bytes 589832 | tf_op jit(solution)/shard_map/ppermute | solution.py:233
  356.0 53.3 %copy-start.45 = (f32[128,256]{1,0:T(8,128)S(1)}, f32[128,256]{1,0:T(8,128)}, u32[]{:S(2)}) copy-start(f32[128,256]{1,0:T(8,128)} %convolution_add_fusion.6) | copy-start | bytes 393220
  356.4 12.3 %collective-permute-start.10 = (f32[384,128]{1,0:T(8,128)}, f32[384,128]{1,0:T(8,128)S(1)}, u32[]{:S(2)}, u32[]{:S(2)}) collective-permute-start(f32[384,128]{1,0:T(8,128)} %collective-permute-done.8), channel_id=1, source_target_pairs={{4,0},{8,4},{12,8},{16,12},{20,16},{24,20},{28,24},{5,1},{9,5},{13... | collective-permute-start | bytes 589832 | tf_op jit(solution)/shard_map/ppermute | solution.py:233
  369.7 14.5 %collective-permute-start.12 = (f32[384,128]{1,0:T(8,128)S(1)}, f32[384,128]{1,0:T(8,128)S(1)}, u32[]{:S(2)}, u32[]{:S(2)}) collective-permute-start(f32[384,128]{1,0:T(8,128)S(1)} %multiply_add_fusion.5), channel_id=1, source_target_pairs={{8,0},{12,4},{16,8},{20,12},{24,16},{28,20},{9,1},{13,5},{17,9},{2... | collective-permute-start | bytes 589832 | tf_op jit(solution)/shard_map/ppermute | solution.py:233
  384.4 24.1 %collective-permute-start.14 = (f32[384,128]{1,0:T(8,128)S(1)}, f32[384,128]{1,0:T(8,128)S(1)}, u32[]{:S(2)}, u32[]{:S(2)}) collective-permute-start(f32[384,128]{1,0:T(8,128)S(1)} %multiply_add_fusion.4), channel_id=1, source_target_pairs={{16,0},{20,4},{24,8},{28,12},{17,1},{21,5},{25,9},{29,13},{18,2},{... | collective-permute-start | bytes 589832 | tf_op jit(solution)/shard_map/ppermute | solution.py:233
  410.0 95.8 %reduce-scatter.23.cloned.1.call-start = ((), (), s32[]{:S(2)}) async-start(), calls=%async_computation.12 | async-start | bytes 1179648 | tf_op jit(solution)/shard_map/reduce_scatter | solution.py:354
  410.6 114.4 %all-reduce.15.cloned.1.call-start = ((), (), s32[]{:S(2)}) async-start(), calls=%async_computation.13 | async-start | bytes 262144 | tf_op jit(solution)/shard_map/psum | solution.py:357
  421.6 107.4 %copy-start.27 = (bf16[1024,64]{1,0:T(8,128)(2,1)S(1)}, bf16[1024,64]{1,0:T(8,128)(2,1)}, u32[]{:S(2)}) copy-start(bf16[1024,64]{1,0:T(8,128)(2,1)} %copy-done.26) | copy-start | bytes 393220
  505.8 53.3 %reduce-scatter.25.cloned.1.call-start = ((), (), s32[]{:S(2)}) async-start(), calls=%async_computation.14 | async-start | bytes 1310720 | tf_op jit(solution)/shard_map/reduce_scatter | solution.py:289
  507.5 23.4 %collective-permute-start.15 = (f32[16,1024]{1,0:T(8,128)}, f32[16,1024]{1,0:T(8,128)}, u32[]{:S(2)}, u32[]{:S(2)}) collective-permute-start(f32[16,1024]{1,0:T(8,128)} %convolution_add_fusion.9), channel_id=1, source_target_pairs={{4,0},{8,4},{12,8},{16,12},{20,16},{24,20},{28,24},{0,28},{5,1},{9... | collective-permute-start | bytes 196616 | tf_op jit(solution)/shard_map/ppermute | solution.py:412
  533.0 62.8 %all-gather.10.cloned.1.call-start = ((), (), s32[]{:S(2)}) async-start(), calls=%async_computation.18 | async-start | bytes 5242880 | tf_op jit(solution)/shard_map/all_gather | solution.py:435
  534.5 128.7 %reduce-scatter.33.cloned.1.call-start = ((), (), s32[]{:S(2)}) async-start(), calls=%async_computation.20 | async-start | bytes 1179648
  536.4 197.4 %reduce-scatter.29.cloned.1.call-start = ((), (), s32[]{:S(2)}) async-start(), calls=%async_computation.17 | async-start | bytes 2359296 | tf_op jit(solution)/shard_map/reduce_scatter | solution.py:430
  539.8 237.4 %all-gather.8.cloned.1.call-start = ((), (), s32[]{:S(2)}) async-start(), calls=%async_computation.15 | async-start | bytes 1310720 | tf_op jit(solution)/shard_map/all_gather | solution.py:292
  562.2 263.0 %reduce-scatter.31.cloned.1.call-start = ((), (), s32[]{:S(2)}) async-start(), calls=%async_computation.19 | async-start | bytes 2654208
  571.3 345.1 %reduce-scatter.27.cloned.1.call-start = ((), (), s32[]{:S(2)}) async-start(), calls=%async_computation.16 | async-start | bytes 4718592 | tf_op jit(solution)/shard_map/reduce_scatter | solution.py:437
  601.8 63.3 %copy-start.169 = (f32[384]{0:T(512)S(1)}, f32[384]{0:T(512)}, u32[]{:S(2)}) copy-start(f32[384]{0:T(512)} %get-tuple-element.575) | copy-start | bytes 4612
  601.8 63.3 %copy-start.168 = (f32[384]{0:T(512)S(1)}, f32[384]{0:T(512)}, u32[]{:S(2)}) copy-start(f32[384]{0:T(512)} %get-tuple-element.576) | copy-start | bytes 4612
  601.8 63.3 %copy-start.167 = (f32[384]{0:T(512)S(1)}, f32[384]{0:T(512)}, u32[]{:S(2)}) copy-start(f32[384]{0:T(512)} %get-tuple-element.577) | copy-start | bytes 4612
  601.8 63.3 %copy-start.166 = (f32[384]{0:T(512)S(1)}, f32[384]{0:T(512)}, u32[]{:S(2)}) copy-start(f32[384]{0:T(512)} %get-tuple-element.574) | copy-start | bytes 4612
  601.9 63.3 %copy-start.186 = (f32[128]{0:T(128)S(1)}, f32[128]{0:T(128)}, u32[]{:S(2)}) copy-start(f32[128]{0:T(128)} %get-tuple-element.702) | copy-start | bytes 1540
  601.9 63.3 %copy-start.161 = (f32[64]{0:T(128)S(1)}, f32[64]{0:T(128)}, u32[]{:S(2)}) copy-start(f32[64]{0:T(128)} %get-tuple-element.584) | copy-start | bytes 772
  601.9 63.3 %copy-start.162 = (f32[64]{0:T(128)S(1)}, f32[64]{0:T(128)}, u32[]{:S(2)}) copy-start(f32[64]{0:T(128)} %get-tuple-element.585) | copy-start | bytes 772
  601.9 63.3 %copy-start.163 = (f32[64]{0:T(128)S(1)}, f32[64]{0:T(128)}, u32[]{:S(2)}) copy-start(f32[64]{0:T(128)} %get-tuple-element.586) | copy-start | bytes 772
  601.9 63.3 %copy-start.164 = (f32[64]{0:T(128)S(1)}, f32[64]{0:T(128)}, u32[]{:S(2)}) copy-start(f32[64]{0:T(128)} %get-tuple-element.587) | copy-start | bytes 772
  601.9 63.4 %copy-start.176 = (f32[128]{0:T(128)S(1)}, f32[128]{0:T(128)}, u32[]{:S(2)}) copy-start(f32[128]{0:T(128)} %get-tuple-element.661) | copy-start | bytes 1540
  602.0 134.2 %copy-start.102 = (f32[1024]{0:T(1024)S(1)}, f32[1024]{0:T(1024)}, u32[]{:S(2)}) copy-start(f32[1024]{0:T(1024)} %get-tuple-element.582) | copy-start | bytes 12292
  837.8 80.8 %copy-start.16 = (bf16[256,1024]{1,0:T(8,128)(2,1)S(1)}, bf16[256,1024]{1,0:T(8,128)(2,1)}, u32[]{:S(2)}) copy-start(bf16[256,1024]{1,0:T(8,128)(2,1)} %all_gather.56) | copy-start | bytes 1572868
  841.5 77.8 %copy-start.31 = (f32[256,1024]{1,0:T(8,128)S(1)}, f32[256,1024]{1,0:T(8,128)}, u32[]{:S(2)}) copy-start(f32[256,1024]{1,0:T(8,128)} %all-gather.8.cloned.1.call-done) | copy-start | bytes 3145732
  841.5 79.4 %copy-start.1 = (bf16[1024,512]{1,0:T(8,128)(2,1)S(1)}, bf16[1024,512]{1,0:T(8,128)(2,1)}, u32[]{:S(2)}) copy-start(bf16[1024,512]{1,0:T(8,128)(2,1)} %param.41) | copy-start | bytes 3145732
  842.1 78.2 %copy-start.68 = (f32[4,1536]{1,0:T(4,128)S(1)}, f32[4,1536]{1,0:T(4,128)}, u32[]{:S(2)}) copy-start(f32[4,1536]{1,0:T(4,128)} %all_gather.61) | copy-start | bytes 73732
  (168 other events, 2065.3 us)
Sparse Core Ops, SparseCore 0:
  217.7 27.0 reduce-scatter.16
  259.8 25.2 reduce-scatter.20
  288.2 24.8 reduce-scatter.18
  410.2 28.3 all-reduce.16
  442.4 63.3 reduce-scatter.22
  508.1 16.9 all-reduce.14
  533.1 26.0 reduce-scatter.24
  561.3 34.4 all-gather.9
  599.8 63.3 reduce-scatter.32
  667.0 66.7 reduce-scatter.28
  736.1 15.7 all-gather.7
  755.7 69.4 reduce-scatter.30
  829.3 87.1 reduce-scatter.26

commit v2 on v1

--- a/solution.py
+++ b/solution.py
@@ -1,8 +1,11 @@
+import functools
 import math
 
 import jax
 import jax.numpy as jnp
 from jax import lax
+from jax.experimental import pallas as pl
+from jax.experimental.pallas import tpu as pltpu
 from jax.sharding import PartitionSpec as P
 
 QUERY_HEADS = 8
@@ -19,6 +22,8 @@
 LANES = 128
 HALO = 16
 FAR = -1e30
+MESH = pl.DeviceIdType.MESH
+VMEM_LIMIT = 60 << 20
 
 
 def nn(a, b, p=None):
@@ -62,7 +67,7 @@
 
 
 def roll(v, shift):
-    return jnp.roll(v, shift, axis=1)
+    return pltpu.roll(v, shift, 1)
 
 
 def rope(v, cosine, sine, direction):
@@ -104,6 +109,422 @@
     doc = doc_of(starts, pos)
     masks = [(doc_of(starts, pos - (KC - 1 - k)) == doc).astype(F32) for k in range(KC)]
     return doc, masks
+
+
+def push(src, dst, send_sem, recv_sem, device):
+    copy = pltpu.make_async_remote_copy(
+        src_ref=src,
+        dst_ref=dst,
+        send_sem=send_sem,
+        recv_sem=recv_sem,
+        device_id=device,
+        device_id_type=MESH,
+    )
+    copy.start()
+    return copy
+
+
+def greet(n, ns, s, t):
+    barrier = pltpu.get_barrier_semaphore()
+
+    def seq_turn(k, carried):
+        pl.semaphore_signal(
+            barrier, inc=1, device_id={"seq": lax.rem(s + k, n)}, device_id_type=MESH
+        )
+        return carried
+
+    lax.fori_loop(1, n, seq_turn, 0)
+    for k in range(1, ns):
+        pl.semaphore_signal(
+            barrier, inc=1, device_id={"state": lax.rem(t + k, ns)}, device_id_type=MESH
+        )
+    pl.semaphore_wait(barrier, n - 1 + ns - 1)
+
+
+def spread(ref, ns, t, src, send, recv):
+    return [
+        push(src, ref, send.at[k - 1], recv.at[k - 1], {"state": lax.rem(t + k, ns)})
+        for k in range(1, ns)
+    ]
+
+
+def conv_ref(ext_ref, taps, masks, rows):
+    total = 0.0
+    for k in range(KC):
+        at = HALO - KC + 1 + k
+        total = total + ext_ref[at : at + rows, :] * taps[k : k + 1] * masks[k]
+    return total
+
+
+class Carry:
+    def __init__(self, n, s, direction, tx, rx, thr_tx, thr_rx, sems):
+        self.n, self.s, self.direction = n, s, direction
+        self.tx, self.rx, self.thr_tx, self.thr_rx = tx, rx, thr_tx, thr_rx
+        self.send, self.recv, self.thr_send, self.thr_recv = sems
+        self.steps = carry_steps(n)
+
+    def copies(self, slot):
+        d, source = self.steps[slot]
+        to = lax.rem(self.s + self.direction * d + self.n, self.n)
+        make = lambda src, dst, a, b: pltpu.make_async_remote_copy(
+            src_ref=src,
+            dst_ref=dst,
+            send_sem=a,
+            recv_sem=b,
+            device_id={"seq": to},
+            device_id_type=MESH,
+        )
+        return (
+            make(self.tx.at[source], self.rx.at[slot], self.send.at[slot], self.recv.at[slot]),
+            make(
+                self.thr_tx.at[source],
+                self.thr_rx.at[slot],
+                self.thr_send.at[slot],
+                self.thr_recv.at[slot],
+            ),
+        )
+
+    def sends(self, slot):
+        to = self.s + self.direction * self.steps[slot][0]
+        return (to >= 0) & (to < self.n)
+
+    def gets(self, slot):
+        source = self.s - self.direction * self.steps[slot][0]
+        return (source >= 0) & (source < self.n)
+
+    def start(self, slot):
+        @pl.when(self.sends(slot))
+        def _():
+            for copy in self.copies(slot):
+                copy.start()
+
+    def finish(self, slot):
+        @pl.when(self.sends(slot))
+        def _():
+            for copy in self.copies(slot):
+                copy.wait_send()
+
+    def arrive(self, slot):
+        @pl.when(self.gets(slot))
+        def _():
+            for copy in self.copies(slot):
+                copy.wait_recv()
+
+        @pl.when(jnp.logical_not(self.gets(slot)))
+        def _():
+            self.rx[slot] = jnp.zeros(self.rx.shape[1:], self.rx.dtype)
+            self.thr_rx[slot] = jnp.zeros(self.thr_rx.shape[1:], F32)
+
+        return self.rx[slot].astype(F32), self.thr_rx[slot]
+
+    def begin(self, part, thr):
+        self.tx[0] = part.astype(BF16)
+        self.thr_tx[0] = thr
+        self.start(0)
+        if len(self.steps) > 1:
+            self.start(1)
+
+    def put(self, source, part, thr):
+        self.tx[source] = part.astype(BF16)
+        self.thr_tx[source] = thr
+
+
+def carry_steps(n):
+    steps = [(1, 0)]
+    if n > 2:
+        steps.append((2, 0))
+    d, source = 2, 1
+    while 2 * d < n + 1 and d < n - 1:
+        steps.append((d, source))
+        d, source = 2 * d, source + 1
+    return steps
+
+
+def expand_rows(width):
+    return (iota((width, LANES), 0) // HDM == iota((width, LANES), 1)).astype(F32)
+
+
+def link_of(linked, cum, cum_t, h):
+    return jnp.exp(jnp.where(linked, cum[:, h : h + 1] - cum_t[h : h + 1, :], FAR))
+
+
+def forward_kernel(
+    n, ns, x, w_qkv, w_mix, w_step, st_own, taps_st, taps_mix, ngain, bias_row, rate_row, skip_row,
+    ggain_row, w_joint, mgain, real_col, codes, cosine, sine, doc_starts,
+    n2, res, inv2, normed, inv1, q2_out, kv_out, out2, lse, z_out, inner_ext, state_ext, step_raw,
+    ssd_out, s_in_out, inv_g_out, joined,
+    halo, st_all, taps_all, kv_all, ext_f, ext_s, m_ref, l_ref, acc_ref,
+    carry_tx, carry_rx, thr_tx, thr_rx, sq_tx, sq_rx, rs_tx, rs_rx, n2_all,
+    halo_sem, st_send, st_recv, taps_send, taps_recv, kv_send, kv_recv,
+    c_send, c_recv, ct_send, ct_recv, sq_send, sq_recv, rs_send, rs_recv, ag_send, ag_recv,
+):
+    T, D = x.shape
+    t, s = lax.axis_index("state"), lax.axis_index("seq")
+    C = taps_mix.shape[1]
+    QC = 2 * HEAD_SIZE
+    NW = st_own.shape[1]
+    N = NW * ns
+    TO = T // ns
+    DM = C * ns
+    scale = 1.0 / math.sqrt(HEAD_SIZE)
+    greet(n, ns, s, t)
+    halo_copy = push(
+        x.at[pl.ds(T - HALO, HALO)], halo, halo_sem.at[0], halo_sem.at[1], {"seq": lax.rem(s + 1, n)}
+    )
+    mine = pl.ds(pl.multiple_of(NW * t, NW), NW)
+    st_copies = spread(st_all.at[:, mine, :], ns, t, st_own, st_send, st_recv)
+    taps_copies = spread(taps_all.at[:, mine, :], ns, t, taps_st, taps_send, taps_recv)
+    st_all[:, mine, :] = st_own[...]
+    taps_all[:, mine, :] = taps_st[...]
+
+    first_row = s * T
+    starts = [doc_starts[k] for k in range(doc_starts.shape[0])]
+    doc, masks = masks_of(starts, first_row, T)
+    doc_row = doc_of(starts, first_row + iota((1, T), 1))
+    lane = iota((T, LANES), 1)
+    low = lane < HEAD_SIZE
+
+    xf = x[...].astype(F32)
+    inv = lax.rsqrt(jnp.mean(xf * xf, axis=1, keepdims=True) + EPSILON)
+    inv1[HALO:, :] = inv
+    normed[HALO:, :] = (xf * inv * ngain[...]).astype(BF16)
+    main = normed[HALO:, :]
+    qkv = nn(main, w_qkv[...])
+    q = (rope(qkv[:, :QC], cosine[...], sine[...], 1.0).astype(BF16) * scale).astype(F32)
+    kcos, ksin = jnp.where(low, cosine[...], 1.0), jnp.where(low, sine[...], 0.0)
+    kv = rope(qkv[:, QC:], kcos, ksin, 1.0).astype(BF16)
+    kv_all[s] = kv
+    kv_out[s] = kv
+
+    def kv_copy(k, to):
+        return pltpu.make_async_remote_copy(
+            src_ref=kv_all.at[s],
+            dst_ref=kv_all.at[s],
+            send_sem=kv_send.at[k - 1],
+            recv_sem=kv_recv.at[k - 1],
+            device_id={"seq": to},
+            device_id_type=MESH,
+        )
+
+    def kv_turn(k, carried):
+        kv_copy(k, lax.rem(s + k, n)).start()
+        return carried
+
+    lax.fori_loop(1, n - s, kv_turn, 0)
+    q2_out[:T, :] = jnp.where(low, q, 0.0).astype(BF16)
+    q2_out[T:, :] = jnp.where(low, roll(q, HEAD_SIZE), 0.0).astype(BF16)
+    z_out[...] = nn(main, w_mix[:, :C])
+    raw = nn(main, w_step[...])
+    step_raw[...] = raw
+
+    halo_copy.wait_recv()
+    hf = halo[...].astype(F32)
+    inv_h = lax.rsqrt(jnp.mean(hf * hf, axis=1, keepdims=True) + EPSILON)
+    inv1[:HALO, :] = inv_h
+    normed[:HALO, :] = (hf * inv_h * ngain[...]).astype(BF16)
+    ext = nn(normed[...], w_mix[:, C:]).astype(BF16)
+    inner_ext[...] = ext
+    ext_f[...] = ext.astype(F32)
+    inner = silu(conv_ref(ext_f, taps_mix[...], masks, T))
+    for copy in st_copies + taps_copies:
+        copy.wait_recv()
+    state_conv = []
+    for c in range(2):
+        ext = nt(normed[...], st_all[c]).astype(BF16)
+        state_ext[:, N * c : N * (c + 1)] = ext
+        ext_s[...] = ext.astype(F32)
+        taps = taps_all[c].T
+        state_conv.append(silu(conv_ref(ext_s, taps, masks, T)))
+    write, read = state_conv
+    step = softplus(raw + bias_row[...])
+    causal = iota((T, T), 0) >= iota((T, T), 1)
+    cum = nn(causal.astype(F32), -step * rate_row[...], HI)
+    cum_t = cum.T
+    linked = (doc == doc_row) & causal
+    E = expander(C)
+    in_x = inner * nn(step * real_col[...], E, HI)
+    cum_last = cum[T - 1 : T]
+    last = first_row + T - 1
+    doc_last = doc_of(starts, jnp.full((T, 1), last, jnp.int32))
+    prior = doc_of(starts, jnp.full((T, 1), first_row - 1, jnp.int32))
+    tail = jnp.where(doc == doc_last, jnp.exp(cum_last - cum), 0.0)
+    state_part = tn(nn(tail, E, HI) * in_x, write, HI)
+    alive = (doc == prior).astype(F32)
+    alive_last = (doc_last == prior).astype(F32)[:8]
+    thr = alive_last * jnp.exp(jnp.broadcast_to(cum_last, (8, LANES)))
+    carry = Carry(
+        n, s, 1, carry_tx, carry_rx, thr_tx, thr_rx, (c_send, c_recv, ct_send, ct_recv)
+    )
+    carry.begin(state_part, thr)
+    steps = len(carry.steps)
+    rows_e = expand_rows(C)
+    window = [None]
+
+    def advance(slot):
+        total, thr_got = carry.arrive(slot)
+        if slot == 0:
+            window[0] = (total, thr_got)
+        else:
+            now, thr_now = window[0]
+            window[0] = (now + nt(rows_e, thr_now, HI)[:, :1] * total, thr_now * thr_got)
+        if slot >= 1 and slot + 1 < steps:
+            carry.put(carry.steps[slot + 1][1], *window[0])
+            carry.start(slot + 1)
+
+    g_mat = nt(read, write, HI)
+    for p in range(C // LANES):
+        at = slice(LANES * p, LANES * (p + 1))
+        y0 = nn(link_of(linked, cum, cum_t, 2 * p) * g_mat, in_x[:, at], HI)
+        y1 = nn(link_of(linked, cum, cum_t, 2 * p + 1) * g_mat, in_x[:, at], HI)
+        ssd_out[:, at] = jnp.where(low, y0, y1)
+        if p == 0:
+            advance(0)
+            if steps > 1:
+                advance(1)
+        elif p + 1 < steps:
+            advance(p + 1)
+    done = max(2, C // LANES + 1)
+
+    q2 = q2_out[...]
+    doc2 = jnp.concatenate([doc, doc], axis=0)
+    m_ref[...] = jnp.full(m_ref.shape, FAR, F32)
+    l_ref[...] = jnp.zeros(l_ref.shape, F32)
+    acc_ref[...] = jnp.zeros(acc_ref.shape, F32)
+
+    def attend(j, diagonal):
+        block = kv_all[j]
+        allowed = codes[j] == doc2
+        if diagonal:
+            rows2 = jnp.concatenate([iota((T, T), 0)] * 2, axis=0)
+            cols2 = iota((2 * T, T), 1)
+            allowed = (allowed & (cols2 <= rows2)) | (cols2 == rows2)
+        scores = jnp.where(allowed, nt(q2, block), FAR)
+        m = m_ref[...]
+        m_new = jnp.maximum(m, jnp.max(scores, axis=1, keepdims=True))
+        shrink = jnp.exp(m - m_new)
+        p = jnp.exp(scores - m_new)
+        l_ref[...] = l_ref[...] * shrink + jnp.sum(p, axis=1, keepdims=True)
+        acc_ref[...] = acc_ref[...] * shrink + nn(p.astype(BF16), block)
+        m_ref[...] = m_new
+
+    attend(s, True)
+
+    def attend_turn(k, carried):
+        kv_copy(k, lax.rem(s + k, n)).wait_recv()
+        attend(s - k, False)
+        kv_out[s - k] = kv_all[s - k]
+        return carried
+
+    lax.fori_loop(1, s + 1, attend_turn, 0)
+    lse[...] = m_ref[...] + jnp.log(l_ref[...])
+    out = acc_ref[...] / l_ref[...]
+    out2[...] = out
+    joined[:, :QC] = jnp.where(low, roll(out[:T], HEAD_SIZE), out[T:]).astype(BF16)
+
+    for slot in range(done, steps):
+        advance(slot)
+    s_in = window[0][0]
+    s_in_out[...] = s_in
+    ssd = ssd_out[...] + nn(alive * jnp.exp(cum), E, HI) * nt(read, s_in, HI)
+    ssd_out[...] = ssd
+    gated = (ssd + skip_row[...] * inner) * silu(z_out[...])
+    sq_tx[...] = nt(jnp.ones((8, C), F32), gated * gated, HI)
+    sq_copies = [
+        push(
+            sq_tx, sq_rx.at[k - 1], sq_send.at[k - 1], sq_recv.at[k - 1],
+            {"state": lax.rem(t + k, ns)},
+        )
+        for k in range(1, ns)
+    ]
+    total = sq_tx[...]
+    for k in range(1, ns):
+        sq_copies[k - 1].wait_recv()
+        total = total + sq_rx[k - 1]
+    inv_row = lax.rsqrt(total / DM + EPSILON)
+    first = (iota((8, LANES), 0) == 0).astype(F32)
+    inv_g = tn(inv_row, first, HI)[:, :1]
+    inv_g_out[...] = inv_g
+    joined[:, QC:] = (gated * inv_g * ggain_row[...]).astype(BF16)
+    part = nn(joined[...], w_joint[...]).astype(BF16)
+    for k in range(ns):
+        rs_tx[k] = part[TO * k : TO * (k + 1)]
+    rs_copies = []
+    for k in range(1, ns):
+        p = lax.rem(t + k, ns)
+        rs_copies.append(
+            push(rs_tx.at[p], rs_rx.at[k - 1], rs_send.at[k - 1], rs_recv.at[k - 1], {"state": p})
+        )
+    total = x[pl.ds(pl.multiple_of(TO * t, TO), TO), :].astype(F32) + rs_tx[t].astype(F32)
+    for k in range(1, ns):
+        rs_copies[k - 1].wait_recv()
+        total = total + rs_rx[k - 1].astype(F32)
+    res[...] = total
+    inv = lax.rsqrt(jnp.mean(total * total, axis=1, keepdims=True) + EPSILON)
+    inv2[...] = inv
+    n2_all[t] = (total * inv * mgain[...]).astype(BF16)
+    ag_copies = spread(n2_all.at[t], ns, t, n2_all.at[t], ag_send, ag_recv)
+    for copy in ag_copies:
+        copy.wait_recv()
+    for k in range(ns):
+        n2[TO * k : TO * (k + 1), :] = n2_all[k]
+    for copy in [halo_copy] + st_copies + taps_copies + sq_copies + rs_copies + ag_copies:
+        copy.wait_send()
+    for slot in range(steps):
+        carry.finish(slot)
+
+    def kv_end(k, carried):
+        kv_copy(k, lax.rem(s + k, n)).wait_send()
+        return carried
+
+    lax.fori_loop(1, n - s, kv_end, 0)
+
+
+def forward(n, ns, args):
+    x, w_qkv, w_mix, w_step, st_own = args[:5]
+    T, D = x.shape
+    C = w_mix.shape[1] // 2
+    NW = st_own.shape[1]
+    N, TO = NW * ns, T // ns
+    steps = len(carry_steps(n))
+    sd = jax.ShapeDtypeStruct
+    outs = (
+        sd((T, D), BF16), sd((TO, D), F32), sd((TO, 1), F32), sd((T + HALO, D), BF16),
+        sd((T + HALO, 1), F32), sd((2 * T, LANES), BF16), sd((n, T, LANES), BF16),
+        sd((2 * T, LANES), F32), sd((2 * T, 1), F32), sd((T, C), F32), sd((T + HALO, C), BF16),
+        sd((T + HALO, 2 * N), BF16), sd((T, LANES), F32), sd((T, C), F32), sd((C, N), F32),
+        sd((T, 1), F32), sd((T, 2 * HEAD_SIZE + C), BF16),
+    )
+    vm, dma = pltpu.VMEM, lambda k: pltpu.SemaphoreType.DMA((k,))
+    scratch = [
+        vm((HALO, D), BF16), vm((2, N, D), BF16), vm((2, N, LANES), F32), vm((n, T, LANES), BF16),
+        vm((T + HALO, C), F32), vm((T + HALO, N), F32), vm((2 * T, 1), F32), vm((2 * T, 1), F32),
+        vm((2 * T, LANES), F32),
+        vm((steps, C, N), BF16), vm((steps, C, N), BF16), vm((steps, 8, LANES), F32),
+        vm((steps, 8, LANES), F32), vm((8, T), F32), vm((ns - 1, 8, T), F32),
+        vm((ns, TO, D), BF16), vm((ns - 1, TO, D), BF16), vm((ns, TO, D), BF16),
+        dma(2), dma(ns - 1), dma(ns - 1), dma(ns - 1), dma(ns - 1), dma(n - 1), dma(n - 1),
+        dma(steps), dma(steps), dma(steps), dma(steps), dma(ns - 1), dma(ns - 1), dma(ns - 1),
+        dma(ns - 1), dma(ns - 1), dma(ns - 1),
+    ]
+    whole = pl.BlockSpec(memory_space=pltpu.VMEM)
+    return pl.pallas_call(
+        functools.partial(forward_kernel, n, ns),
+        out_shape=outs,
+        in_specs=[whole] * (len(args) - 1) + [pl.BlockSpec(memory_space=pltpu.SMEM)],
+        out_specs=(whole,) * len(outs),
+        scratch_shapes=scratch,
+        name="forward",
+        compiler_params=pltpu.CompilerParams(
+            collective_id=1, has_side_effects=True, vmem_limit_bytes=VMEM_LIMIT
+        ),
+    )(*args)
+
+
+def rope_x(v, cosine, sine, direction):
+    first = (iota(v.shape, 1) % HEAD_SIZE) < HEAD_SIZE // 2
+    half = HEAD_SIZE // 2
+    partner = jnp.where(first, -jnp.roll(v, -half, axis=1), jnp.roll(v, half, axis=1))
+    return v * cosine + partner * (direction * sine)
 
 
 def local(
@@ -171,28 +592,29 @@
     angles = (pos - firsts).astype(F32)[:, None] * jnp.exp(-math.log(ROPE_BASE) * powers)[None, :]
     cosine, sine = jnp.cos(angles), jnp.sin(angles)
 
-    halo = lax.ppermute(layer_input[T - HALO :], "seq", [(i, (i + 1) % n) for i in range(n)])
-    st_all = lax.all_gather(st_own, "state", axis=1, tiled=True).reshape(-1, D)
-    taps_all = lax.all_gather(conv_state, "state", axis=2, tiled=True).reshape(KC, -1)
+    taps_rows = jnp.pad(jnp.transpose(conv_state, (1, 2, 0)), ((0, 0), (0, 0), (0, LANES - KC)))
+    (
+        n2, res, inv2, normed, inv1, q2, kv_all, out2, lse, z, inner_ext, state_ext, step_raw, ssd,
+        s_in, inv_g, joined,
+    ) = forward(
+        n,
+        NS,
+        (
+            layer_input, w_qkv, w_mix, w_step, st_own, taps_rows, taps_mix, ngain, bias_row,
+            rate_row, skip_row, ggain_row, w_joint, mgain, real_col, codes, cosine, sine, doc_starts,
+        ),
+    )
 
     doc, masks = masks_of(starts, first_row, T)
-    x_ext = jnp.concatenate([halo, layer_input]).astype(F32)
-    inv1 = lax.rsqrt(jnp.mean(x_ext * x_ext, axis=1, keepdims=True) + EPSILON)
-    normed = (x_ext * inv1 * ngain).astype(BF16)
     main = normed[HALO:]
-    qkv = nn(main, w_qkv)
     scale = 1.0 / math.sqrt(HEAD_SIZE)
-    q = (rope(qkv[:, :QC], cosine, sine, 1.0).astype(BF16) * scale).astype(BF16)
     lane = iota((T, LANES), 1)
     is_k = lane < HEAD_SIZE
     kcos, ksin = jnp.where(is_k, cosine, 1.0), jnp.where(is_k, sine, 0.0)
-    kv = rope(qkv[:, QC:], kcos, ksin, 1.0).astype(BF16)
-    z = nn(main, w_mix[:, :C])
-    inner_ext = nn(normed, w_mix[:, C:]).astype(BF16).astype(F32)
-    state_ext = nt(normed, st_all).astype(BF16).astype(F32)
-    step_raw = nn(main, w_step)
+    inner_ext, state_ext = inner_ext.astype(F32), state_ext.astype(F32)
     inner_lin = conv_fwd(inner_ext, taps_mix, masks)
     inner = silu(inner_lin)
+    taps_all = lax.all_gather(conv_state, "state", axis=2, tiled=True).reshape(KC, -1)
     state_conv = silu(conv_fwd(state_ext, taps_all, masks))
     N = state_conv.shape[1] // 2
     write, read = state_conv[:, :N], state_conv[:, N:]
@@ -210,18 +632,10 @@
     def link(h):
         return jnp.exp(jnp.where(linked, cum[:, h : h + 1] - cum_t[h : h + 1, :], FAR))
 
-    y = []
-    for p in range(C // LANES):
-        xp = in_x[:, LANES * p : LANES * (p + 1)]
-        y0 = nn(link(2 * p) * g_mat, xp, HI)
-        y1 = nn(link(2 * p + 1) * g_mat, xp, HI)
-        y.append(jnp.where(is_k, y0, y1))
-    y_intra = jnp.concatenate(y, axis=1)
     doc_last = doc[T - 1 : T]
     cum_last = cum[T - 1 : T]
     tail = jnp.where(doc == doc_last, jnp.exp(cum_last - cum), 0.0)
     tail_e = nn(tail, E, HI)
-    state_part = tn(tail_e * in_x, write, HI)
     prior = doc_of(starts, jnp.full((1, 1), first_row - 1, jnp.int32))
     alive = (doc == prior).astype(F32)
     through = alive[T - 1 : T] * jnp.exp(cum_last)
@@ -242,13 +656,7 @@
             d *= 2
         return total
 
-    s_in = carry(state_part, 1)
-    kv_all = lax.all_gather(kv, "seq")
     head0 = lane < HEAD_SIZE
-    qf = q.astype(F32)
-    q2 = jnp.where(
-        jnp.concatenate([head0, head0]), jnp.concatenate([qf, roll(qf, HEAD_SIZE)]), 0.0
-    ).astype(BF16)
     doc2 = jnp.concatenate([doc, doc])
     row2 = jnp.concatenate([iota((T, T), 0), iota((T, T), 0)])
     col2 = iota((2 * T, T), 1)
@@ -257,44 +665,15 @@
         code = codes[j]
         return ((code == doc2) & ((j < s) | (col2 <= row2))) | ((j == s) & (col2 == row2))
 
-    def attend(j, carried):
-        m, l, acc = carried
-        scores = jnp.where(allowed_at(j), nt(q2, kv_all[j]), FAR)
-        m_new = jnp.maximum(m, jnp.max(scores, axis=1, keepdims=True))
-        shrink = jnp.exp(m - m_new)
-        p = jnp.exp(scores - m_new)
-        return m_new, l * shrink + jnp.sum(p, axis=1, keepdims=True), acc * shrink + nn(
-            p.astype(BF16), kv_all[j]
-        )
-
-    begin = attend(
-        s, (jnp.full((2 * T, 1), FAR), jnp.zeros((2 * T, 1)), jnp.zeros((2 * T, LANES)))
-    )
-    m, l, acc = lax.fori_loop(0, s, attend, begin)
-    out2 = acc / l
-    lse = m + jnp.log(l)
-    attended_f = jnp.where(head0, roll(out2[:T], HEAD_SIZE), out2[T:])
-    attended = attended_f.astype(BF16)
-
-    y_inter = reach_e * nt(read, s_in, HI)
-    ssd = y_intra + y_inter
     full_mix = ssd + skip_row * inner
     gated = full_mix * silu(z)
-    sumsq = lax.psum(jnp.sum(gated * gated, axis=1, keepdims=True), "state")
-    inv_g = lax.rsqrt(sumsq / DM + EPSILON)
-    joined = jnp.concatenate([attended, (gated * inv_g * ggain_row).astype(BF16)], axis=1)
-    part = nn(joined, w_joint).astype(BF16)
+    x_own = dsl(layer_input, TO * t, TO, 0).astype(F32)
 
     def rs_state(v):
         return lax.psum_scatter(v.astype(F32), "state", scatter_dimension=0, tiled=True)
 
     def ag_state(v):
         return lax.all_gather(v, "state", axis=0, tiled=True)
-
-    x_own = dsl(layer_input, TO * t, TO, 0).astype(F32)
-    res = x_own + rs_state(part)
-    inv2 = lax.rsqrt(jnp.mean(res * res, axis=1, keepdims=True) + EPSILON)
-    n2 = ag_state((res * inv2 * mgain).astype(BF16))
 
     gu = nn(n2, w_gu)
     gate, up = gu[:, :F], gu[:, F:]
@@ -333,7 +712,7 @@
     later = carry(direct, -1)
 
     dout2 = jnp.where(
-        jnp.concatenate([head0, head0]), 0.0, jnp.concatenate([roll(d_att, HEAD_SIZE), d_att])
+        jnp.concatenate([head0, head0]), 0.0, jnp.concatenate([jnp.roll(d_att, HEAD_SIZE, axis=1), d_att])
     )
     delta = jnp.sum(dout2 * out2, axis=1, keepdims=True)
     dout2 = dout2.astype(BF16)
@@ -349,13 +728,13 @@
     dq2, dkv_all = lax.fori_loop(
         0, s + 1, attend_back, (jnp.zeros((2 * T, LANES)), jnp.zeros((n, T, LANES)))
     )
-    dq = jnp.where(head0, dq2[:T], roll(dq2[T:], HEAD_SIZE)) * scale
-    d_q = rope(dq, cosine, sine, -1.0).astype(BF16)
+    dq = jnp.where(head0, dq2[:T], jnp.roll(dq2[T:], HEAD_SIZE, axis=1)) * scale
+    d_q = rope_x(dq, cosine, sine, -1.0).astype(BF16)
     dkv = lax.psum_scatter(dkv_all, "seq", scatter_dimension=0, tiled=False)
     pair = NS // KEY_VALUE_HEADS
     groups = [[g * pair + i for i in range(pair)] for g in range(KEY_VALUE_HEADS)]
     dkv = lax.psum(dkv, "state", axis_index_groups=groups)
-    d_kv = rope(dkv, kcos, ksin, -1.0).astype(BF16)
+    d_kv = rope_x(dkv, kcos, ksin, -1.0).astype(BF16)
 
     w_r = nt(write, later, HI)
     tail_r = tail_e * w_r

time: 940 us -> 821 us (0.87)
  blocking collectives: 183 us -> 130 us
  starting transfers between devices: 58.2 us -> 12.8 us
  Pallas kernels: 0 us -> 43 us
  waiting for transfers between devices: 433 us -> 401 us
  matrix products: 69.5 us -> 55.5 us
  local copies, waits for them, and re-layouts: 90.9 us -> 81.5 us
    pallas_call x0 -> x1, Pallas kernels: none -> 43 us  [forward(): pl.pallas_call(functools.partial(forward_kernel, n, ns), out_shape=outs,...]
    ppermute x14 -> x7, starting transfers between devices: 51.9 us -> 9.45 us  [carry(): lax.ppermute(v, 'seq', [(i, i + d * direction) for i in range(n) if 0 <=...]
    reduce_scatter x4 -> x3, waiting for transfers between devices: 62.3 us -> 20.4 us  [rs_state(): lax.psum_scatter(v.astype(F32), 'state', scatter_dimension=0, tiled=True)]
    all_gather x2 -> x0, blocking collectives: 41.2 us -> none  [the longest x1 33.6 us: local(): kv_all = lax.all_gather(kv, 'seq')]
    ppermute x14 -> x7, waiting for transfers between devices: 61.5 us -> 77 us  [carry(): lax.ppermute(v, 'seq', [(i, i + d * direction) for i in range(n) if 0 <=...]
    dot_general x28 -> x16, matrix products: 27.7 us -> 16.6 us  [nn(): lax.dot_general(a, b, (((1,), (0,)), ((), ())), precision=p, preferred_el...]
    all_gather x3 -> x2, blocking collectives: 21.2 us -> 14.3 us  [ag_state(): return lax.all_gather(v, 'state', axis=0, tiled=True)]
    unnamed x402 -> x333, local copies, waits for them, and re-layouts: 22.1 us -> 17.4 us
  transfers between devices with their start and end apart: 29 -> 20, of which waited for: 18 -> 15; matrix products, arithmetic and copies ran while one was open for 18% -> 16% of each run, Pallas kernels for 0% -> 0%
where the time goes in v2:
time: 821 us; the launch traced here: 811 us
  waiting for transfers between devices  401 us (49%)
  blocking collectives  130 us (16%)
  local copies, waits for them, and re-layouts  81.5 us (10%)
  other arithmetic  63.7 us (8%)
  matrix products  55.5 us (7%)
  Pallas kernels  43 us (5%)
  between operations  23.3 us (3%)
  starting transfers between devices  12.8 us (2%)
    unnamed x15, waiting for transfers between devices  116 us
    ppermute x7, waiting for transfers between devices, carry(): lax.ppermute(v, 'seq', [(i, i + d * direction) for i in range(n) if 0 <=...  77 us
    reduce_scatter x1, waiting for transfers between devices, local(): r_joint = lax.psum_scatter(gj, 'seq', scatter_dimension=0, tiled=True)  73.7 us
    reduce_scatter x1, waiting for transfers between devices, local(): dkv = lax.psum_scatter(dkv_all, 'seq', scatter_dimension=0, tiled=False)  64.2 us
    pallas_call x1, Pallas kernels, forward(): pl.pallas_call(functools.partial(forward_kernel, n, ns), out_shape=outs,...  43 us
    psum x1, blocking collectives, local(): sums = lax.psum((g_ngain, g_mgain), ('seq', 'state'))  40.5 us
    psum x1, blocking collectives, local(): lax.psum((g_ggain, g_taps_mix, g_taps_st, g_bias[:, :HL], g_rate[:, :HL],...  35.3 us
    dot_general x21, matrix products, tn(): lax.dot_general(a, b, (((0,), (0,)), ((), ())), precision=p, preferred_el...  21 us
  transfers between devices with their start and end apart: 20, of which 15 were waited for; matrix products, arithmetic and copies ran while one was open for 16% of the time, Pallas kernels for 0%

profile of v2, /device:TPU:0, one launch (start us, length us, event | category | flops | bytes accessed | tf_op | source)
XLA Modules:
  0.0 811.0 jit_solution(9251492955022798135)
XLA Ops:
  7.3 6.5 fusion.300
  23.9 3.5 copy_bitcast_fusion
  29.7 5.7 constant_dynamic-slice_fusion.2
  42.2 4.9 add_select_fusion
  47.0 43.0 %forward.1 = (bf16[256,1024]{1,0:T(8,128)(2,1)}, f32[64,1024]{1,0:T(8,128)}, f32[64,1]{1,0:T(8,128)}, bf16[272,1024]{1,0:T(8,128)(2,1)}, f32[272,1]{1,0:T(8,128)...) custom-call(bf16[256,1024]{1,0:T(8,128)(2,1)} %x.16, ...), custom_call_target="tpu_custom_call" | custom-call | tf_op jit(solution)/shard_map/forward/pallas_call | solution.py:510
  90.0 2.1 fusion.21
  100.2 4.9 fusion.263
  115.8 5.4 compare_convert_fusion.8
  122.0 6.0 all_gather.41
  130.4 5.5 broadcast_compare_fusion.1
  139.2 2.9 fusion.293
  145.2 7.9 collective-permute-done.3
  163.5 2.6 collective-permute-done.5
  172.3 6.9 all_gather.40
  182.8 6.6 psum.71
  189.5 2.9 multiply_reduce_fusion.1
  193.5 2.4 fusion.144
  208.7 5.3 while.14
  218.5 12.4 %collective-permute-done.2 = f32[384,128]{1,0:T(8,128)S(1)} collective-permute-done((f32[384,128]{1,0:T(8,128)}, f32[384,128]{1,0:T(8,128)S(1)}, u32[]{:S(2)}, u32[]{:S(2)}) %collective-permute-start.2) | collective-permute-done | bytes 196640 | tf_op jit(solution)/shard_map/ppermute | solution.py:647
  233.4 21.3 %collective-permute-done.4 = f32[384,128]{1,0:T(8,128)S(1)} collective-permute-done((f32[384,128]{1,0:T(8,128)S(1)}, f32[384,128]{1,0:T(8,128)S(1)}, u32[]{:S(2)}, u32[]{:S(2)}) %collective-permute-start.4) | collective-permute-done | bytes 196640 | tf_op jit(solution)/shard_map/ppermute | solution.py:647
  256.8 32.7 %collective-permute-done.6 = f32[384,128]{1,0:T(8,128)S(1)} collective-permute-done((f32[384,128]{1,0:T(8,128)S(1)}, f32[384,128]{1,0:T(8,128)S(1)}, u32[]{:S(2)}, u32[]{:S(2)}) %collective-permute-start.6) | collective-permute-done | bytes 196640 | tf_op jit(solution)/shard_map/ppermute | solution.py:647
  293.4 2.3 fusion.84
  295.8 3.5 multiply_reduce_fusion.5
  305.4 15.5 %all-reduce.18.cloned.1.call-done = f32[4,2,32,256]{3,2,0,1:T(8,128)} async-done(((f32[4,2,32,256]{3,2,0,1:T(8,128)}), f32[4,2,32,256]{3,2,0,1:T(8,128)}) %all-reduce.18.cloned.1.call-update) | async-done | bytes 262160
  324.3 64.2 %reduce-scatter.20.cloned.1.call-done = f32[1,256,128]{2,1,0:T(8,128)} async-done(((f32[8,256,128]{2,1,0:T(8,128)}), f32[1,256,128]{2,1,0:T(8,128)}) %reduce-scatter.20.cloned.1.call-update) | async-done | bytes 131088 | tf_op jit(solution)/shard_map/reduce_scatter | solution.py:733
  390.2 2.3 collective-permute-start.7
  392.5 15.1 %all-reduce.16.cloned.1.call-done = f32[256,128]{1,0:T(8,128)} async-done(((f32[256,128]{1,0:T(8,128)}), f32[256,128]{1,0:T(8,128)}) %all-reduce.16.cloned.1.call-update) | async-done | bytes 131088 | tf_op jit(solution)/shard_map/psum | solution.py:736
  409.8 2.2 broadcast_select_fusion
  420.4 3.1 convolution_convert_fusion
  424.6 18.5 %reduce-scatter.22.cloned.1.call-done = f32[64,1024]{1,0:T(8,128)} async-done(((f32[256,1024]{1,0:T(8,128)}), f32[64,1024]{1,0:T(8,128)}) %reduce-scatter.22.cloned.1.call-update) | async-done | bytes 262160 | tf_op jit(solution)/shard_map/reduce_scatter | solution.py:673
  450.2 6.2 concatenate.135
  456.4 2.6 copy.172
  459.1 20.7 %all-gather.9.cloned.1.call-done = bf16[2048,1024]{1,0:T(8,128)(2,1)} async-done(((bf16[512,1024]{1,0:T(8,128)(2,1)}), bf16[2048,1024]{1,0:T(8,128)(2,1)}) %all-gather.9.cloned.1.call-update) | async-done | bytes 4194320 | tf_op jit(solution)/shard_map/all_gather | solution.py:814
  479.8 2.2 slice.509
  483.3 2.6 pad_maximum_fusion
  486.8 7.4 all_gather.39
  494.3 53.3 %reduce-scatter.30.cloned.1.call-done = bf16[128,512]{1,0:T(8,128)(2,1)} async-done(((bf16[1024,512]{1,0:T(8,128)(2,1)}), bf16[128,512]{1,0:T(8,128)(2,1)}) %reduce-scatter.30.cloned.1.call-update) | async-done | bytes 131088
  549.7 35.3 %all-reduce.11 = (f32[4,384]{1,0:T(4,128)S(1)}, f32[4,2,32]{2,1,0:T(2,128)}, f32[1,6]{1,0:T(1,128)S(1)}, f32[1,6]{1,0:T(1,128)S(1)}, f32[6,64]{1,0:T(8,128)S(1)}, /*index=5*/f32[1,384]{1,0:T(1,128)S(1)}) all-reduce(f32[4,384]{1,0:T(4,128)S(1)} %pad_maximum_fusion.15, ...), channel_id=1, replica_groups=mesh['seq'=8,'state'=4] {'seq'}, use_global_device_ids=true, to_apply=%region_23.24 | all-reduce | flops 2572 | bytes 20576 | tf_op jit(solution)/shard_map/psum | solution.py:831
  585.0 5.2 all_gather.45
  590.8 7.6 all-reduce.12
  598.3 5.1 all_gather.49
  604.1 13.9 %reduce-scatter.26.cloned.1.call-done = bf16[128,1024]{1,0:T(8,128)(2,1)} async-done(((bf16[1024,1024]{1,0:T(8,128)(2,1)}), bf16[128,1024]{1,0:T(8,128)(2,1)}) %reduce-scatter.26.cloned.1.call-update) | async-done | bytes 262160 | tf_op jit(solution)/shard_map/reduce_scatter | solution.py:809
  618.0 2.3 reshape.515
  620.3 40.5 %all-reduce.10 = (f32[1,1024]{1,0:T(1,128)S(1)}, f32[1,1024]{1,0:T(1,128)S(1)}) all-reduce(f32[1,1024]{1,0:T(1,128)S(1)} %bitcast.278, f32[1,1024]{1,0:T(1,128)S(1)} %bitcast.277), channel_id=1, replica_groups=mesh['seq'=8,'state'=4] {'seq','state'}, use_global_device_ids=true, to_apply=%region_17.18 | all-reduce | flops 2048 | bytes 16384 | tf_op jit(solution)/shard_map/psum | solution.py:830
  661.7 46.8 %reduce-scatter.28.cloned.1.call-done = bf16[128,1030]{1,0:T(8,128)(2,1)} async-done(((bf16[1024,1030]{1,0:T(8,128)(2,1)}), bf16[128,1030]{1,0:T(8,128)(2,1)}) %reduce-scatter.28.cloned.1.call-update) | async-done | bytes 263696
  709.7 9.7 %all-gather.3 = bf16[4,966,128]{2,1,0:T(8,128)(2,1)S(1)} all-gather(bf16[1,966,128]{2,1,0:T(8,128)(2,1)S(1)} %bitcast.264), channel_id=2, replica_groups=mesh['seq'=8,'state'=4] {'state'}, dimensions={0}, use_global_device_ids=true | all-gather | bytes 1236480 | tf_op jit(solution)/shard_map/all_gather | solution.py:818
  725.5 73.7 %reduce-scatter.24.cloned.1.call-done = bf16[256,1024]{1,0:T(8,128)(2,1)} async-done(((bf16[2048,1024]{1,0:T(8,128)(2,1)}), bf16[256,1024]{1,0:T(8,128)(2,1)}) %reduce-scatter.24.cloned.1.call-update) | async-done | bytes 524304 | tf_op jit(solution)/shard_map/reduce_scatter | solution.py:816
  799.2 2.1 convert_element_type.843
  (562 shorter events, 137.6 us)
Async XLA Ops:
  7.2 85.0 %copy-start = (bf16[1024,512]{1,0:T(8,128)(2,1)S(1)}, bf16[1024,512]{1,0:T(8,128)(2,1)}, u32[]{:S(2)}) copy-start(bf16[1024,512]{1,0:T(8,128)(2,1)} %param.39) | copy-start | bytes 3145732
  7.2 159.5 %reduce-scatter.18.cloned.1.call-start = ((), (), s32[]{:S(2)}) async-start(), calls=%async_computation.9 | async-start | bytes 1310720 | tf_op jit(solution)/shard_map/reduce_scatter | solution.py:673
  38.9 66.8 %copy-start.148 = (f32[128]{0:T(128)}, f32[128]{0:T(128)S(1)}, u32[]{:S(2)}) copy-start(f32[128]{0:T(128)S(1)} %get-tuple-element.553) | copy-start | bytes 1540
  38.9 100.2 %copy-start.133 = (f32[128]{0:T(128)}, f32[128]{0:T(128)S(1)}, u32[]{:S(2)}) copy-start(f32[128]{0:T(128)S(1)} %get-tuple-element.568) | copy-start | bytes 1540
  47.0 43.0 %copy-start.33 = (bf16[1024,512]{1,0:T(8,128)(2,1)S(1)}, bf16[1024,512]{1,0:T(8,128)(2,1)}, u32[]{:S(2)}) copy-start(bf16[1024,512]{1,0:T(8,128)(2,1)} %get-tuple-element.571) | copy-start | bytes 3145732
  95.3 75.0 %reduce-scatter.16.cloned.1.call-start = ((), (), s32[]{:S(2)}) async-start(), calls=%async_computation.8 | async-start | bytes 1310720 | tf_op jit(solution)/shard_map/reduce_scatter | solution.py:673
  107.1 35.6 %collective-permute-start.1 = (f32[384,1]{0,1:T(1,128)S(1)}, f32[384,1]{0,1:T(1,128)S(1)}, u32[]{:S(2)}, u32[]{:S(2)}) collective-permute-start(f32[384,1]{0,1:T(1,128)S(1)} %convolution_bitcast_fusion.1), channel_id=1, source_target_pairs={{4,0},{8,4},{12,8},{16,12},{20,16},{24,20},{28,24},{5,1},{9,5},{13... | collective-permute-start | bytes 4616 | tf_op jit(solution)/shard_map/ppermute | solution.py:647
  110.0 210.8 %all-reduce.18.cloned.1.call-start = ((), (), s32[]{:S(2)}) async-start(), calls=%async_computation.19 | async-start | bytes 524288
  115.0 51.7 %copy-start.122 = (f32[64]{0:T(128)}, f32[64]{0:T(128)S(1)}, u32[]{:S(2)}) copy-start(f32[64]{0:T(128)S(1)} %get-tuple-element.423) | copy-start | bytes 772
  142.2 47.3 %copy-start.23 = (f32[256,384]{1,0:T(8,128)}, f32[256,384]{1,0:T(8,128)S(1)}, u32[]{:S(2)}) copy-start(f32[256,384]{1,0:T(8,128)S(1)} %get-tuple-element.481) | copy-start | bytes 1179652
  142.7 10.4 %collective-permute-start.3 = (f32[384,1]{0,1:T(1,128)S(1)}, f32[384,1]{0,1:T(1,128)S(1)}, u32[]{:S(2)}, u32[]{:S(2)}) collective-permute-start(f32[384,1]{0,1:T(1,128)S(1)} %collective-permute-done.1), channel_id=1, source_target_pairs={{4,0},{8,4},{12,8},{16,12},{20,16},{24,20},{28,24},{5,1},{9,5},{13... | collective-permute-start | bytes 4616 | tf_op jit(solution)/shard_map/ppermute | solution.py:647
  153.8 12.3 %collective-permute-start.5 = (f32[384,1]{0,1:T(1,128)S(1)}, f32[384,1]{0,1:T(1,128)S(1)}, u32[]{:S(2)}, u32[]{:S(2)}) collective-permute-start(f32[384,1]{0,1:T(1,128)S(1)} %get-tuple-element.543), channel_id=1, source_target_pairs={{8,0},{12,4},{16,8},{20,12},{24,16},{28,20},{9,1},{13,5},{17,9},{2... | collective-permute-start | bytes 4616 | tf_op jit(solution)/shard_map/ppermute | solution.py:647
  195.9 21.2 %collective-permute-start = (f32[384,128]{1,0:T(8,128)}, f32[384,128]{1,0:T(8,128)}, u32[]{:S(2)}, u32[]{:S(2)}) collective-permute-start(f32[384,128]{1,0:T(8,128)} %fusion.144), channel_id=1, source_target_pairs={{4,0},{8,4},{12,8},{16,12},{20,16},{24,20},{28,24},{5,1},{9,5},{13... | collective-permute-start | bytes 589832 | tf_op jit(solution)/shard_map/ppermute | solution.py:647
  214.0 75.5 %copy-start.41 = (f32[384,128]{1,0:T(8,128)S(1)}, f32[384,128]{1,0:T(8,128)}, u32[]{:S(2)}) copy-start(f32[384,128]{1,0:T(8,128)} %get-tuple-element.216) | copy-start | bytes 589828
  214.0 75.5 %copy-start.109 = (f32[384]{0:T(512)S(1)}, f32[384]{0:T(512)}, u32[]{:S(2)}) copy-start(f32[384]{0:T(512)} %get-tuple-element.429) | copy-start | bytes 4612
  215.6 75.4 %copy-start.22 = (f32[256,384]{1,0:T(8,128)S(1)}, f32[256,384]{1,0:T(8,128)}, u32[]{:S(2)}) copy-start(f32[256,384]{1,0:T(8,128)} %fusion.77) | copy-start | bytes 1179652
  217.1 13.8 %collective-permute-start.2 = (f32[384,128]{1,0:T(8,128)}, f32[384,128]{1,0:T(8,128)S(1)}, u32[]{:S(2)}, u32[]{:S(2)}) collective-permute-start(f32[384,128]{1,0:T(8,128)} %collective-permute-done), channel_id=1, source_target_pairs={{4,0},{8,4},{12,8},{16,12},{20,16},{24,20},{28,24},{5,1},{9,5},{13... | collective-permute-start | bytes 589832 | tf_op jit(solution)/shard_map/ppermute | solution.py:647
  232.0 22.7 %collective-permute-start.4 = (f32[384,128]{1,0:T(8,128)S(1)}, f32[384,128]{1,0:T(8,128)S(1)}, u32[]{:S(2)}, u32[]{:S(2)}) collective-permute-start(f32[384,128]{1,0:T(8,128)S(1)} %multiply_add_fusion.4), channel_id=1, source_target_pairs={{8,0},{12,4},{16,8},{20,12},{24,16},{28,20},{9,1},{13,5},{17,9},{2... | collective-permute-start | bytes 589832 | tf_op jit(solution)/shard_map/ppermute | solution.py:647
  254.8 34.7 %collective-permute-start.6 = (f32[384,128]{1,0:T(8,128)S(1)}, f32[384,128]{1,0:T(8,128)S(1)}, u32[]{:S(2)}, u32[]{:S(2)}) collective-permute-start(f32[384,128]{1,0:T(8,128)S(1)} %multiply_add_fusion.3), channel_id=1, source_target_pairs={{16,0},{20,4},{24,8},{28,12},{17,1},{21,5},{25,9},{29,13},{18,2},{... | collective-permute-start | bytes 589832 | tf_op jit(solution)/shard_map/ppermute | solution.py:647
  292.3 96.2 %reduce-scatter.20.cloned.1.call-start = ((), (), s32[]{:S(2)}) async-start(), calls=%async_computation.10 | async-start | bytes 1179648 | tf_op jit(solution)/shard_map/reduce_scatter | solution.py:733
  293.2 114.4 %all-reduce.16.cloned.1.call-start = ((), (), s32[]{:S(2)}) async-start(), calls=%async_computation.11 | async-start | bytes 262144 | tf_op jit(solution)/shard_map/psum | solution.py:736
  302.2 86.3 %copy-start.19 = (bf16[1024,2,32]{0,2,1:T(8,128)(2,1)S(1)}, bf16[1024,2,32]{0,2,1:T(8,128)(2,1)}, u32[]{:S(2)}) copy-start(bf16[1024,2,32]{0,2,1:T(8,128)(2,1)} %param.28) | copy-start | bytes 393220
  304.1 107.8 %copy-start.3 = (bf16[1024,256]{1,0:T(8,128)(2,1)S(1)}, bf16[1024,256]{1,0:T(8,128)(2,1)}, u32[]{:S(2)}) copy-start(bf16[1024,256]{1,0:T(8,128)(2,1)} %pad_maximum_fusion.10.w_qkv) | copy-start | bytes 1572868
  323.3 89.8 %copy-start.11 = (bf16[1024,384]{1,0:T(8,128)(2,1)S(1)}, bf16[1024,384]{1,0:T(8,128)(2,1)}, u32[]{:S(2)}) copy-start(bf16[1024,384]{1,0:T(8,128)(2,1)} %copy-done.10) | copy-start | bytes 2359300
  323.3 89.8 %slice-start = ((bf16[272,384]{1,0:T(8,128)(2,1)}), bf16[256,384]{1,0:T(8,128)(2,1)S(1)}, s32[]{:S(2)}) async-start(bf16[272,384]{1,0:T(8,128)(2,1)} %copy-done.20), calls=%async_computation.20 | async-start | bytes 393216 | tf_op jit(solution)/shard_map/slice | solution.py:794
  323.4 89.8 %copy-start.39 = (bf16[256,384]{1,0:T(8,128)(2,1)S(1)}, bf16[256,384]{1,0:T(8,128)(2,1)}, u32[]{:S(2)}) copy-start(bf16[256,384]{1,0:T(8,128)(2,1)} %get-tuple-element.491) | copy-start | bytes 589828
  324.3 89.5 %copy-start.47 = (bf16[272,64]{0,1:T(8,128)(2,1)}, bf16[272,64]{0,1:T(8,128)(2,1)S(1)}, u32[]{:S(2)}) copy-start(bf16[272,64]{0,1:T(8,128)(2,1)S(1)} %fusion.161) | copy-start | bytes 104452
  388.5 54.6 %reduce-scatter.22.cloned.1.call-start = ((), (), s32[]{:S(2)}) async-start(), calls=%async_computation.12 | async-start | bytes 1310720 | tf_op jit(solution)/shard_map/reduce_scatter | solution.py:673
  390.2 24.6 %collective-permute-start.7 = (f32[16,1024]{1,0:T(8,128)}, f32[16,1024]{1,0:T(8,128)}, u32[]{:S(2)}, u32[]{:S(2)}) collective-permute-start(f32[16,1024]{1,0:T(8,128)} %convolution_add_fusion.6), channel_id=1, source_target_pairs={{4,0},{8,4},{12,8},{16,12},{20,16},{24,20},{28,24},{0,28},{5,1},{9... | collective-permute-start | bytes 196616 | tf_op jit(solution)/shard_map/ppermute | solution.py:791
  416.9 62.9 %all-gather.9.cloned.1.call-start = ((), (), s32[]{:S(2)}) async-start(), calls=%async_computation.16 | async-start | bytes 5242880 | tf_op jit(solution)/shard_map/all_gather | solution.py:814
  418.4 129.2 %reduce-scatter.30.cloned.1.call-start = ((), (), s32[]{:S(2)}) async-start(), calls=%async_computation.18 | async-start | bytes 1179648
  420.3 197.7 %reduce-scatter.26.cloned.1.call-start = ((), (), s32[]{:S(2)}) async-start(), calls=%async_computation.15 | async-start | bytes 2359296 | tf_op jit(solution)/shard_map/reduce_scatter | solution.py:809
  423.6 238.1 %all-gather.7.cloned.1.call-start = ((), (), s32[]{:S(2)}) async-start(), calls=%async_computation.13 | async-start | bytes 1310720 | tf_op jit(solution)/shard_map/all_gather | solution.py:676
  446.1 262.4 %reduce-scatter.28.cloned.1.call-start = ((), (), s32[]{:S(2)}) async-start(), calls=%async_computation.17 | async-start | bytes 2654208
  459.0 340.1 %reduce-scatter.24.cloned.1.call-start = ((), (), s32[]{:S(2)}) async-start(), calls=%async_computation.14 | async-start | bytes 4718592 | tf_op jit(solution)/shard_map/reduce_scatter | solution.py:816
  485.9 63.6 %copy-start.143 = (f32[384]{0:T(512)S(1)}, f32[384]{0:T(512)}, u32[]{:S(2)}) copy-start(f32[384]{0:T(512)} %get-tuple-element.408) | copy-start | bytes 4612
  485.9 63.6 %copy-start.142 = (f32[384]{0:T(512)S(1)}, f32[384]{0:T(512)}, u32[]{:S(2)}) copy-start(f32[384]{0:T(512)} %get-tuple-element.409) | copy-start | bytes 4612
  485.9 63.6 %copy-start.141 = (f32[384]{0:T(512)S(1)}, f32[384]{0:T(512)}, u32[]{:S(2)}) copy-start(f32[384]{0:T(512)} %get-tuple-element.410) | copy-start | bytes 4612
  485.9 63.6 %copy-start.140 = (f32[384]{0:T(512)S(1)}, f32[384]{0:T(512)}, u32[]{:S(2)}) copy-start(f32[384]{0:T(512)} %get-tuple-element.407) | copy-start | bytes 4612
  485.9 63.6 %copy-start.153 = (f32[128]{0:T(128)S(1)}, f32[128]{0:T(128)}, u32[]{:S(2)}) copy-start(f32[128]{0:T(128)} %get-tuple-element.503) | copy-start | bytes 1540
  485.9 63.6 %copy-start.135 = (f32[64]{0:T(128)S(1)}, f32[64]{0:T(128)}, u32[]{:S(2)}) copy-start(f32[64]{0:T(128)} %get-tuple-element.415) | copy-start | bytes 772
  485.9 63.6 %copy-start.136 = (f32[64]{0:T(128)S(1)}, f32[64]{0:T(128)}, u32[]{:S(2)}) copy-start(f32[64]{0:T(128)} %get-tuple-element.416) | copy-start | bytes 772
  486.0 63.6 %copy-start.137 = (f32[64]{0:T(128)S(1)}, f32[64]{0:T(128)}, u32[]{:S(2)}) copy-start(f32[64]{0:T(128)} %get-tuple-element.417) | copy-start | bytes 772
  486.0 63.6 %copy-start.138 = (f32[64]{0:T(128)S(1)}, f32[64]{0:T(128)}, u32[]{:S(2)}) copy-start(f32[64]{0:T(128)} %get-tuple-element.418) | copy-start | bytes 772
  486.0 63.7 %copy-start.147 = (f32[128]{0:T(128)S(1)}, f32[128]{0:T(128)}, u32[]{:S(2)}) copy-start(f32[128]{0:T(128)} %get-tuple-element.472) | copy-start | bytes 1540
  486.0 134.2 %copy-start.94 = (f32[1024]{0:T(1024)S(1)}, f32[1024]{0:T(1024)}, u32[]{:S(2)}) copy-start(f32[1024]{0:T(1024)} %get-tuple-element.413) | copy-start | bytes 12292
  723.2 78.9 %copy-start.30 = (f32[256,1024]{1,0:T(8,128)S(1)}, f32[256,1024]{1,0:T(8,128)}, u32[]{:S(2)}) copy-start(f32[256,1024]{1,0:T(8,128)} %all-gather.7.cloned.1.call-done) | copy-start | bytes 3145732
  724.9 78.8 %copy-start.1 = (bf16[1024,512]{1,0:T(8,128)(2,1)S(1)}, bf16[1024,512]{1,0:T(8,128)(2,1)}, u32[]{:S(2)}) copy-start(bf16[1024,512]{1,0:T(8,128)(2,1)} %param.39) | copy-start | bytes 3145732
  (127 other events, 1144.5 us)
Sparse Core Ops, SparseCore 0:
  95.4 46.6 reduce-scatter.17
  145.4 24.8 reduce-scatter.15
  292.4 28.3 all-reduce.17
  325.1 63.3 reduce-scatter.19
  390.7 16.9 all-reduce.15
  417.0 26.0 reduce-scatter.21
  445.3 34.4 all-gather.8
  484.2 63.3 reduce-scatter.29
  551.2 66.7 reduce-scatter.25
  620.0 15.7 all-gather.6
  639.3 69.1 reduce-scatter.27
  712.0 87.1 reduce-scatter.23

commit v3 on v2

v3 whole, which is shorter than its diff:
```python
import functools
import math
import types

import jax
import jax.numpy as jnp
from jax import lax
from jax.experimental import pallas as pl
from jax.experimental.pallas import tpu as pltpu
from jax.sharding import PartitionSpec as P

QUERY_HEADS = 8
KEY_VALUE_HEADS = 2
HEAD_SIZE = 64
NH = 24
HDM = 64
KC = 4
EPSILON = 1e-05
ROPE_BASE = 10000.0
HI = lax.Precision.HIGHEST
F32 = jnp.float32
BF16 = jnp.bfloat16
LANES = 128
HALO = 16
FAR = -1e30
MESH = pl.DeviceIdType.MESH
VMEM_LIMIT = 60 << 20


def nn(a, b, p=None):
    return lax.dot_general(a, b, (((1,), (0,)), ((), ())), precision=p, preferred_element_type=F32)


def nt(a, b, p=None):
    return lax.dot_general(a, b, (((1,), (1,)), ((), ())), precision=p, preferred_element_type=F32)


def tn(a, b, p=None):
    return lax.dot_general(a, b, (((0,), (0,)), ((), ())), precision=p, preferred_element_type=F32)


def sigmoid(v):
    return 1.0 / (1.0 + jnp.exp(-v))


def silu(v):
    return v * sigmoid(v)


def silu_slope(v):
    s = sigmoid(v)
    return s * (1.0 + v * (1.0 - s))


def softplus(v):
    return jnp.maximum(v, 0.0) + jnp.log1p(jnp.exp(-jnp.abs(v)))


def iota(shape, dim):
    return lax.broadcasted_iota(jnp.int32, shape, dim)


def doc_of(starts, pos):
    found = jnp.full(pos.shape, -1, jnp.int32)
    for start in starts:
        found = found + (pos >= start).astype(jnp.int32)
    return found


def roll(v, shift):
    return pltpu.roll(v, shift, 1)


def rope(v, cosine, sine, direction):
    first = (iota(v.shape, 1) % HEAD_SIZE) < HEAD_SIZE // 2
    half = HEAD_SIZE // 2
    partner = jnp.where(first, -roll(v, v.shape[1] - half), roll(v, half))
    return v * cosine + partner * (direction * sine)


def expander(width):
    return (iota((LANES, width), 1) // HDM == iota((LANES, width), 0)).astype(F32)


def conv_fwd(ext, taps, masks):
    rows = ext.shape[0] - HALO
    total = 0.0
    for k in range(KC):
        at = HALO - KC + 1 + k
        total = total + ext[at : at + rows] * taps[k : k + 1] * masks[k]
    return total


def conv_bwd(ext, taps, masks, up):
    rows = up.shape[0]
    total, weights = 0.0, []
    for k in range(KC):
        at = HALO - KC + 1 + k
        masked = up * masks[k]
        weights.append(jnp.sum(masked * ext[at : at + rows], axis=0, keepdims=True))
        parts = [jnp.zeros((at, up.shape[1]), F32), masked * taps[k : k + 1]]
        if KC - 1 - k:
            parts.append(jnp.zeros((KC - 1 - k, up.shape[1]), F32))
        total = total + jnp.concatenate(parts, axis=0)
    return total, jnp.concatenate(weights, axis=0)


def masks_of(starts, first_row, rows):
    pos = first_row + iota((rows, 1), 0)
    doc = doc_of(starts, pos)
    masks = [(doc_of(starts, pos - (KC - 1 - k)) == doc).astype(F32) for k in range(KC)]
    return doc, masks


def push(src, dst, send_sem, recv_sem, device):
    copy = pltpu.make_async_remote_copy(
        src_ref=src,
        dst_ref=dst,
        send_sem=send_sem,
        recv_sem=recv_sem,
        device_id=device,
        device_id_type=MESH,
    )
    copy.start()
    return copy


def greet(n, ns, s, t):
    barrier = pltpu.get_barrier_semaphore()

    def seq_turn(k, carried):
        pl.semaphore_signal(
            barrier, inc=1, device_id={"seq": lax.rem(s + k, n)}, device_id_type=MESH
        )
        return carried

    lax.fori_loop(1, n, seq_turn, 0)
    for k in range(1, ns):
        pl.semaphore_signal(
            barrier, inc=1, device_id={"state": lax.rem(t + k, ns)}, device_id_type=MESH
        )
    pl.semaphore_wait(barrier, n - 1 + ns - 1)


def spread(ref, ns, t, src, send, recv):
    return [
        push(src, ref, send.at[k - 1], recv.at[k - 1], {"state": lax.rem(t + k, ns)})
        for k in range(1, ns)
    ]


def conv_ref(ext_ref, taps, masks, rows):
    total = 0.0
    for k in range(KC):
        at = HALO - KC + 1 + k
        total = total + ext_ref[at : at + rows, :] * taps[k : k + 1] * masks[k]
    return total


class Carry:
    def __init__(self, n, s, direction, tx, rx, thr_tx, thr_rx, sems):
        self.n, self.s, self.direction = n, s, direction
        self.tx, self.rx, self.thr_tx, self.thr_rx = tx, rx, thr_tx, thr_rx
        self.send, self.recv, self.thr_send, self.thr_recv = sems
        self.steps = carry_steps(n)

    def copies(self, slot):
        d, source = self.steps[slot]
        to = lax.rem(self.s + self.direction * d + self.n, self.n)
        make = lambda src, dst, a, b: pltpu.make_async_remote_copy(
            src_ref=src,
            dst_ref=dst,
            send_sem=a,
            recv_sem=b,
            device_id={"seq": to},
            device_id_type=MESH,
        )
        return (
            make(self.tx.at[source], self.rx.at[slot], self.send.at[slot], self.recv.at[slot]),
            make(
                self.thr_tx.at[source],
                self.thr_rx.at[slot],
                self.thr_send.at[slot],
                self.thr_recv.at[slot],
            ),
        )

    def sends(self, slot):
        to = self.s + self.direction * self.steps[slot][0]
        return (to >= 0) & (to < self.n)

    def gets(self, slot):
        source = self.s - self.direction * self.steps[slot][0]
        return (source >= 0) & (source < self.n)

    def start(self, slot):
        @pl.when(self.sends(slot))
        def _():
            for copy in self.copies(slot):
                copy.start()

    def finish(self, slot):
        @pl.when(self.sends(slot))
        def _():
            for copy in self.copies(slot):
                copy.wait_send()

    def arrive(self, slot):
        @pl.when(self.gets(slot))
        def _():
            for copy in self.copies(slot):
                copy.wait_recv()

        @pl.when(jnp.logical_not(self.gets(slot)))
        def _():
            self.rx[slot] = jnp.zeros(self.rx.shape[1:], self.rx.dtype)
            self.thr_rx[slot] = jnp.zeros(self.thr_rx.shape[1:], F32)

        return self.rx[slot].astype(F32), self.thr_rx[slot]

    def begin(self, part, thr):
        self.tx[0] = part.astype(BF16)
        self.thr_tx[0] = thr
        self.start(0)
        if len(self.steps) > 1:
            self.start(1)

    def put(self, source, part, thr):
        self.tx[source] = part.astype(BF16)
        self.thr_tx[source] = thr


def carry_steps(n):
    steps = [(1, 0)]
    if n > 2:
        steps.append((2, 0))
    d, source = 2, 1
    while 2 * d < n + 1 and d < n - 1:
        steps.append((d, source))
        d, source = 2 * d, source + 1
    return steps


def expand_rows(width):
    return (iota((width, LANES), 0) // HDM == iota((width, LANES), 1)).astype(F32)


def link_of(linked, cum, cum_t, h):
    return jnp.exp(jnp.where(linked, cum[:, h : h + 1] - cum_t[h : h + 1, :], FAR))


def send_to(refs, name, k, src, dst, device):
    send, recv = getattr(refs, name)
    return push(src, dst, send.at[k], recv.at[k], device)


def row_sums(values):
    return nt(jnp.ones((8, values.shape[1]), F32), values, HI)


def as_column(row):
    first = (iota((8, LANES), 0) == 0).astype(F32)
    return tn(row, first, HI)[:, :1]


def share_rows(refs, name, ns, t, row):
    tx, rx = getattr(refs, name + "_tx"), getattr(refs, name + "_rx")
    tx[...] = row
    copies = [
        send_to(refs, name, k - 1, tx, rx.at[k - 1], {"state": lax.rem(t + k, ns)})
        for k in range(1, ns)
    ]

    def wait():
        total = tx[...]
        for k in range(1, ns):
            copies[k - 1].wait_recv()
            total = total + rx[k - 1]
        return total

    return copies, wait


def scatter_rows(refs, name, ns, t, part):
    tx, rx = getattr(refs, name + "_tx"), getattr(refs, name + "_rx")
    rows = tx.shape[1]
    part = part.astype(BF16)
    for k in range(ns):
        tx[k] = part[rows * k : rows * (k + 1)]
    copies = []
    for k in range(1, ns):
        p = lax.rem(t + k, ns)
        copies.append(send_to(refs, name, k - 1, tx.at[p], rx.at[k - 1], {"state": p}))

    def wait():
        total = tx[t].astype(F32)
        for k in range(1, ns):
            copies[k - 1].wait_recv()
            total = total + rx[k - 1].astype(F32)
        return total

    return copies, wait


def gather_rows(refs, name, ns, t, own):
    every = getattr(refs, name + "_all")
    every[t] = own
    return [
        send_to(refs, name, k - 1, every.at[t], every.at[t], {"state": lax.rem(t + k, ns)})
        for k in range(1, ns)
    ]


def layer_kernel(n, ns, names, *flat):
    refs = types.SimpleNamespace()
    at = 0
    for name, count in names:
        setattr(refs, name, flat[at] if count == 1 else flat[at : at + count])
        at += count
    x, normed, inv1, joined = refs.x, refs.normed, refs.inv1, refs.joined
    w_mix, w_qkv, w_joint, w_gu, down = refs.w_mix, refs.w_qkv, refs.w_joint, refs.w_gu, refs.down
    T, D = x.shape
    t, s = lax.axis_index("state"), lax.axis_index("seq")
    C = refs.taps_mix.shape[1]
    QC = 2 * HEAD_SIZE
    NW = refs.st_own.shape[1]
    N = NW * ns
    TO = T // ns
    DM = C * ns
    F = down.shape[1]
    pairs = C // LANES
    scale = 1.0 / math.sqrt(HEAD_SIZE)
    state_peer = lambda k: {"state": lax.rem(t + k, ns)}
    greet(n, ns, s, t)
    sent = []
    halo_copy = send_to(refs, "halo", 0, x.at[pl.ds(T - HALO, HALO)], refs.halo_rx, {"seq": lax.rem(s + 1, n)})
    mine = pl.ds(pl.multiple_of(NW * t, NW), NW)
    arriving = []
    for k in range(1, ns):
        arriving.append(send_to(refs, "st", k - 1, refs.st_own, refs.st_all.at[:, mine, :], state_peer(k)))
        arriving.append(send_to(refs, "taps", k - 1, refs.taps_st, refs.taps_all.at[:, mine, :], state_peer(k)))
    sent += [halo_copy] + arriving
    refs.st_all[:, mine, :] = refs.st_own[...]
    refs.taps_all[:, mine, :] = refs.taps_st[...]

    first_row = s * T
    starts = [refs.doc_starts[k] for k in range(refs.doc_starts.shape[0])]
    doc, masks = masks_of(starts, first_row, T)
    doc_row = doc_of(starts, first_row + iota((1, T), 1))
    lane = iota((T, LANES), 1)
    low = lane < HEAD_SIZE
    ngain = refs.ngain[...]

    xf = x[...].astype(F32)
    inv = lax.rsqrt(jnp.mean(xf * xf, axis=1, keepdims=True) + EPSILON)
    inv1[...] = inv
    normed[HALO:, :] = (xf * inv * ngain).astype(BF16)
    main = normed[HALO:, :]
    qkv = nn(main, w_qkv[...])
    cosine, sine = refs.cosine[...], refs.sine[...]
    q = (rope(qkv[:, :QC], cosine, sine, 1.0).astype(BF16) * scale).astype(F32)
    kcos, ksin = jnp.where(low, cosine, 1.0), jnp.where(low, sine, 0.0)
    kv_all = refs.kv_all
    kv_all[s] = rope(qkv[:, QC:], kcos, ksin, 1.0).astype(BF16)

    def kv_copy(k, to):
        return pltpu.make_async_remote_copy(
            src_ref=kv_all.at[s],
            dst_ref=kv_all.at[s],
            send_sem=refs.kv[0].at[k - 1],
            recv_sem=refs.kv[1].at[k - 1],
            device_id={"seq": to},
            device_id_type=MESH,
        )

    def kv_turn(k, carried):
        kv_copy(k, lax.rem(s + k, n)).start()
        return carried

    lax.fori_loop(1, n - s, kv_turn, 0)
    refs.q2[:T, :] = jnp.where(low, q, 0.0).astype(BF16)
    refs.q2[T:, :] = jnp.where(low, roll(q, HEAD_SIZE), 0.0).astype(BF16)
    refs.z[...] = nn(main, w_mix[:, :C])
    raw = nn(main, refs.w_step[...]) + refs.bias_row[...]

    halo_copy.wait_recv()
    hf = refs.halo_rx[...].astype(F32)
    inv_h = lax.rsqrt(jnp.mean(hf * hf, axis=1, keepdims=True) + EPSILON)
    normed[:HALO, :] = (hf * inv_h * ngain).astype(BF16)
    ext_f, ext_s, ext_o = refs.ext_f, refs.ext_s, refs.ext_o
    ext_f[...] = nn(normed[...], w_mix[:, C:]).astype(BF16).astype(F32)
    taps_mix = refs.taps_mix[...]
    inner_lin = conv_ref(ext_f, taps_mix, masks, T)
    refs.inner_lin[...] = inner_lin
    inner = silu(inner_lin)
    for copy in arriving:
        copy.wait_recv()
    for c in range(2):
        ext_s[...] = nt(normed[...], refs.st_all[c]).astype(BF16).astype(F32)
        taps = refs.taps_all[c].T
        refs.wr[c] = silu(conv_ref(ext_s, taps, masks, T))
    write, read = refs.wr[0], refs.wr[1]
    step = softplus(raw)
    causal = iota((T, T), 0) >= iota((T, T), 1)
    tri = causal.astype(F32)
    rate_row = refs.rate_row[...]
    cum = nn(tri, -step * rate_row, HI)
    cum_t = cum.T
    linked = (doc == doc_row) & causal
    E = expander(C)
    rows_e = expand_rows(C)
    real_col = refs.real_col[...]
    inflow = step * real_col
    inflow_e = nn(inflow, E, HI)
    in_x = inner * inflow_e
    refs.in_x[...] = in_x
    cum_last = cum[T - 1 : T]
    last = first_row + T - 1
    doc_last = doc_of(starts, jnp.full((T, 1), last, jnp.int32))
    prior = doc_of(starts, jnp.full((T, 1), first_row - 1, jnp.int32))
    tail = jnp.where(doc == doc_last, jnp.exp(cum_last - cum), 0.0)
    refs.tail_e[...] = nn(tail, E, HI)
    state_part = tn(refs.tail_e[...] * in_x, write, HI)
    alive = (doc == prior).astype(F32)
    alive_last = (doc_last == prior).astype(F32)[:8]
    thr = alive_last * jnp.exp(jnp.broadcast_to(cum_last, (8, LANES)))
    steps = len(carry_steps(n))

    def make_carry(direction, name):
        send, recv = getattr(refs, name)
        thr_send, thr_recv = getattr(refs, name + "_thr")
        carry = Carry(
            n, s, direction, getattr(refs, name + "_tx"), getattr(refs, name + "_rx"),
            getattr(refs, name + "_thr_tx"), getattr(refs, name + "_thr_rx"),
            (send, recv, thr_send, thr_recv),
        )
        window = [None]

        def advance(slot):
            total, thr_got = carry.arrive(slot)
            if slot == 0:
                window[0] = (total, thr_got)
            else:
                now, thr_now = window[0]
                window[0] = (now + nt(rows_e, thr_now, HI)[:, :1] * total, thr_now * thr_got)
            if slot >= 1 and slot + 1 < steps:
                carry.put(carry.steps[slot + 1][1], *window[0])
                carry.start(slot + 1)

        return carry, window, advance

    carry, window, advance = make_carry(1, "fc")
    carry.begin(state_part, thr)
    done = max(2, pairs + 1)

    def between(advance, p):
        if p == 0:
            advance(0)
            if steps > 1:
                advance(1)
        elif p + 1 < steps:
            advance(p + 1)

    g_mat = nt(read, write, HI)
    for p in range(pairs):
        cols = slice(LANES * p, LANES * (p + 1))
        ys = []
        for h in (2 * p, 2 * p + 1):
            link = link_of(linked, cum, cum_t, h)
            refs.link[h] = link
            ys.append(nn(link * g_mat, in_x[:, cols], HI))
        refs.ssd[:, cols] = jnp.where(low, ys[0], ys[1])
        between(advance, p)
    refs.g_mat[...] = g_mat

    doc2 = jnp.concatenate([doc, doc], axis=0)
    m_ref, l_ref, acc_ref = refs.m_acc, refs.l_acc, refs.o_acc
    m_ref[...] = jnp.full(m_ref.shape, FAR, F32)
    l_ref[...] = jnp.zeros(l_ref.shape, F32)
    acc_ref[...] = jnp.zeros(acc_ref.shape, F32)

    def allowed_at(j, diagonal):
        allowed = refs.codes[j] == doc2
        if diagonal:
            rows2 = jnp.concatenate([iota((T, T), 0)] * 2, axis=0)
            cols2 = iota((2 * T, T), 1)
            allowed = (allowed & (cols2 <= rows2)) | (cols2 == rows2)
        return allowed

    def attend(j, diagonal):
        block = kv_all[j]
        scores = jnp.where(allowed_at(j, diagonal), nt(refs.q2[...], block), FAR)
        m = m_ref[...]
        m_new = jnp.maximum(m, jnp.max(scores, axis=1, keepdims=True))
        shrink = jnp.exp(m - m_new)
        p = jnp.exp(scores - m_new)
        l_ref[...] = l_ref[...] * shrink + jnp.sum(p, axis=1, keepdims=True)
        acc_ref[...] = acc_ref[...] * shrink + nn(p.astype(BF16), block)
        m_ref[...] = m_new

    attend(s, True)

    def attend_turn(k, carried):
        kv_copy(k, lax.rem(s + k, n)).wait_recv()
        attend(s - k, False)
        return carried

    lax.fori_loop(1, s + 1, attend_turn, 0)
    out = acc_ref[...] / l_ref[...]
    acc_ref[...] = out
    m_ref[...] = m_ref[...] + jnp.log(l_ref[...])
    joined[:, :QC] = jnp.where(low, roll(out[:T], HEAD_SIZE), out[T:]).astype(BF16)

    for slot in range(done, steps):
        advance(slot)
    s_in = window[0][0]
    refs.s_in[...] = s_in
    refs.reach_e[...] = nn(alive * jnp.exp(cum), E, HI)
    ssd = refs.ssd[...] + refs.reach_e[...] * nt(read, s_in, HI)
    refs.ssd[...] = ssd
    z = refs.z[...]
    skip_row, ggain_row = refs.skip_row[...], refs.ggain_row[...]
    full_mix = ssd + skip_row * inner
    refs.full_mix[...] = full_mix
    gated = full_mix * silu(z)
    refs.gated[...] = gated
    copies, wait = share_rows(refs, "sq", ns, t, row_sums(gated * gated))
    sent += copies
    inv_g = as_column(lax.rsqrt(wait() / DM + EPSILON))
    joined[:, QC:] = (gated * inv_g * ggain_row).astype(BF16)
    copies, wait = scatter_rows(refs, "rs1", ns, t, nn(joined[...], w_joint[...]))
    sent += copies
    own_rows = pl.ds(pl.multiple_of(TO * t, TO), TO)
    dh = nn(refs.g[...], down[...])
    x_own = x[own_rows, :].astype(F32)
    res = x_own + wait()
    inv2 = lax.rsqrt(jnp.mean(res * res, axis=1, keepdims=True) + EPSILON)
    mgain = refs.mgain[...]
    ag = gather_rows(refs, "ag1", ns, t, (res * inv2 * mgain).astype(BF16))
    sent += ag
    for copy in ag:
        copy.wait_recv()

    n2 = jnp.concatenate([refs.ag1_all[k] for k in range(ns)], axis=0)
    gu = nn(n2, w_gu[...])
    gate, up = gu[:, :F], gu[:, F:]
    sig = sigmoid(gate)
    act = gate * sig
    hidden = (act * up).astype(BF16)
    d_gu = jnp.concatenate(
        [dh * up * (sig * (1.0 + gate * (1.0 - sig))), dh * act], axis=1
    ).astype(BF16)
    copies, wait_dn2 = scatter_rows(refs, "rs2", ns, t, nt(d_gu, w_gu[...]))
    sent += copies
    copies, wait_mlp = scatter_rows(refs, "rs3", ns, t, nt(hidden, down[...]))
    sent += copies
    refs.gw_down[...] = tn(refs.g[...], hidden).astype(BF16)
    for k in range(2):
        refs.gw_gu[:, F * k : F * (k + 1)] = tn(n2, d_gu[:, F * k : F * (k + 1)]).astype(BF16)
    dn2 = wait_dn2()
    scaled = dn2 * mgain
    d_res = (
        refs.g[own_rows, :].astype(F32)
        + inv2 * scaled
        - res * inv2 * inv2 * inv2 * jnp.mean(scaled * res, axis=1, keepdims=True)
    )
    ag2 = gather_rows(refs, "ag2", ns, t, d_res.astype(BF16))
    refs.g_mgain[...] = jnp.sum(dn2 * res * inv2, axis=0, keepdims=True)
    ag3 = gather_rows(refs, "ag3", ns, t, (res + wait_mlp()).astype(BF16))
    sent += ag2 + ag3
    for copy in ag2:
        copy.wait_recv()

    d_branch = jnp.concatenate([refs.ag2_all[k] for k in range(ns)], axis=0)
    d_joined = nt(d_branch, w_joint[...])
    d_gn = d_joined[:, QC:]
    scaled = d_gn * ggain_row
    copies, wait = share_rows(refs, "dot", ns, t, row_sums(scaled * gated))
    sent += copies
    refs.gw_joint[...] = tn(joined[...], d_branch).astype(BF16)
    refs.g_ggain[...] = jnp.sum(d_gn * gated * inv_g, axis=0, keepdims=True)
    d_att = d_joined[:, :QC].astype(BF16).astype(F32)
    dout2 = jnp.concatenate(
        [jnp.where(low, 0.0, roll(d_att, HEAD_SIZE)), jnp.where(low, 0.0, d_att)], axis=0
    )
    delta = jnp.sum(dout2 * acc_ref[...], axis=1, keepdims=True)
    l_ref[...] = delta
    refs.dout2[...] = dout2.astype(BF16)
    dot = as_column(wait() / DM)
    d_gated = inv_g * scaled - gated * (inv_g * inv_g * inv_g * dot)
    sig = sigmoid(z)
    dy = d_gated * z * sig
    refs.dy[...] = dy
    refs.d_z[...] = (d_gated * full_mix * (sig * (1.0 + z * (1.0 - sig)))).astype(BF16)
    refs.g_skip[...] = jnp.sum(dy * inner, axis=0, keepdims=True)
    reach_dy = refs.reach_e[...] * dy
    carry_b, window, advance = make_carry(-1, "bc")
    carry_b.begin(tn(reach_dy, read, HI), thr)
    d_g = jnp.zeros((T, T), F32)
    for p in range(pairs):
        cols = slice(LANES * p, LANES * (p + 1))
        xp, dyp = in_x[:, cols], dy[:, cols]
        halves = []
        for k in range(2):
            link = refs.link[2 * p + k]
            halves.append(tn(link * g_mat, dyp, HI))
            own = low if k == 0 else jnp.logical_not(low)
            d_g = d_g + link * nt(jnp.where(own, dyp, 0.0), xp, HI)
        refs.w_tot[:, cols] = jnp.where(low, halves[0], halves[1])
        between(advance, p)
    refs.d_g[...] = d_g

    refs.dq2[...] = jnp.zeros(refs.dq2.shape, F32)

    def attend_back(j, diagonal):
        block = kv_all[j]
        q2, dout2 = refs.q2[...], refs.dout2[...]
        scores = jnp.where(allowed_at(j, diagonal), nt(q2, block), FAR)
        p = jnp.exp(scores - m_ref[...])
        ds = (p * (nt(dout2, block) - l_ref[...])).astype(BF16)
        refs.dq2[...] += nn(ds, block)
        return tn(ds, q2) + tn(p.astype(BF16), dout2)

    def dkv_copy(k, to, source):
        return pltpu.make_async_remote_copy(
            src_ref=source,
            dst_ref=refs.dkv_rx.at[k - 1],
            send_sem=refs.dkv[0].at[k - 1],
            recv_sem=refs.dkv[1].at[k - 1],
            device_id={"seq": to},
            device_id_type=MESH,
        )

    def back_turn(k, carried):
        kv_all[s - k] = attend_back(s - k, False).astype(BF16)
        dkv_copy(k, lax.rem(s - k + n, n), kv_all.at[s - k]).start()
        return carried

    lax.fori_loop(1, s + 1, back_turn, 0)
    refs.dkv_sum[...] = attend_back(s, True)

    for slot in range(done, steps):
        advance(slot)
    later = window[0][0]
    tail_e = refs.tail_e[...]
    tail_r = tail_e * nt(write, later, HI)
    w_tot = refs.w_tot[...] + tail_r
    d_write = tn(refs.d_g[...], read, HI) + nn(tail_e * in_x, later, HI)
    d_read = nn(refs.d_g[...], write, HI) + nn(reach_dy, s_in, HI)
    refs.dwr_tx[0] = d_write.T.astype(BF16)
    refs.dwr_tx[1] = d_read.T.astype(BF16)
    dwr = []
    for k in range(1, ns):
        p = lax.rem(t + k, ns)
        theirs = pl.ds(pl.multiple_of(NW * p, NW), NW)
        dwr.append(
            send_to(refs, "dwr", k - 1, refs.dwr_tx.at[:, theirs, :], refs.dwr_rx.at[k - 1], {"state": p})
        )
    sent += dwr
    u = nt(inner * w_tot, E, HI)
    tl = nt(in_x * tail_r, E, HI)
    thr_s = jnp.sum(tn(later * s_in, rows_e, HI), axis=0, keepdims=True) * thr[:1]
    d_cum = nt(dy * ssd, E, HI) - inflow * u
    at_last = iota((T, LANES), 0) == T - 1
    d_cum = d_cum + jnp.where(at_last, jnp.sum(tl, axis=0, keepdims=True) + thr_s, 0.0)
    d_ld = tn(tri, d_cum, HI)
    d_step = real_col * u - rate_row * d_ld
    refs.g_rate[...] = -jnp.sum(step * d_ld, axis=0, keepdims=True)
    d_step = d_step * sigmoid(raw)
    refs.g_bias[...] = jnp.sum(d_step, axis=0, keepdims=True)
    d_step = d_step.astype(BF16)
    d_lin = (inflow_e * w_tot + skip_row * dy) * silu_slope(inner_lin)

    def conv_back(ext, grad, taps, up, g_taps):
        grad[...] = jnp.zeros(grad.shape, F32)
        for k in range(KC):
            at = HALO - KC + 1 + k
            masked = up * masks[k]
            g_taps[k : k + 1, :] = jnp.sum(masked * ext[at : at + T, :], axis=0, keepdims=True)
            grad[at : at + T, :] += masked * taps[k : k + 1]
        return grad[...].astype(BF16)

    d_ext = conv_back(ext_f, refs.grad_f, taps_mix, d_lin, refs.g_taps_mix)
    st64 = refs.st_own[...].reshape(2 * NW, D)
    taps_own = refs.taps_st[...].reshape(2 * NW, LANES).T
    ext_o[...] = nt(normed[...], st64).astype(BF16).astype(F32)
    slope_o = silu_slope(conv_ref(ext_o, taps_own, masks, T))
    for copy in dwr:
        copy.wait_recv()
    d_wr = refs.dwr_tx[:, mine, :].astype(F32)
    for k in range(1, ns):
        d_wr = d_wr + refs.dwr_rx[k - 1].astype(F32)
    d_st = conv_back(ext_o, refs.grad_o, taps_own, d_wr.reshape(2 * NW, T).T * slope_o, refs.g_taps_st)
    refs.back_tx[...] = (nt(d_ext[:HALO], w_mix[:, C:]) + nn(d_st[:HALO], st64)).astype(BF16)
    back = send_to(refs, "back", 0, refs.back_tx, refs.back_rx, {"seq": lax.rem(s + n - 1, n)})
    sent.append(back)
    def dkv_turn(k, carried):
        dkv_copy(k, lax.rem(s - k + n, n), refs.dkv_rx.at[k - 1]).wait_recv()
        refs.dkv_sum[...] += refs.dkv_rx[k - 1].astype(F32)
        return carried

    lax.fori_loop(1, n - s, dkv_turn, 0)
    refs.pair_tx[...] = refs.dkv_sum[...].astype(BF16)
    odd = lax.rem(t, 2)
    pair = send_to(refs, "pair", 0, refs.pair_tx, refs.pair_rx, {"state": t + 1 - 2 * odd})
    sent.append(pair)
    d_z = refs.d_z[...]
    refs.gw_mix[:, :C] = tn(main, d_z).astype(BF16)
    refs.gw_mix[:, C:] = tn(normed[...], d_ext).astype(BF16)
    refs.gw_st[...] = tn(normed[...], d_st).astype(BF16)
    refs.gw_step[...] = tn(main, d_step).astype(BF16)
    dq2 = refs.dq2[...]
    dq = jnp.where(low, dq2[:T], roll(dq2[T:], HEAD_SIZE)) * scale
    d_q = rope(dq, cosine, sine, -1.0).astype(BF16)
    d_n = (
        nt(jnp.concatenate([d_z, d_ext[HALO:]], axis=1), w_mix[...])
        + nn(d_st[HALO:], st64)
        + nt(d_step, refs.w_step[...])
    )
    pair.wait_recv()
    d_kv = rope(refs.dkv_sum[...] + refs.pair_rx[...].astype(F32), kcos, ksin, -1.0)
    d_kv = jnp.where(low == (odd == 0), d_kv, 0.0).astype(BF16)
    d_qkv = jnp.concatenate([d_q, d_kv], axis=1)
    refs.gw_qkv[...] = tn(main, d_qkv).astype(BF16)
    d_n = d_n + nt(d_qkv, w_qkv[...])
    back.wait_recv()
    tail_rows = d_n[T - HALO :] + refs.back_rx[...].astype(F32)
    d_n = jnp.concatenate([d_n[: T - HALO], tail_rows], axis=0)
    copies, wait = scatter_rows(refs, "rs4", ns, t, d_n)
    sent += copies
    inv_own = inv1[own_rows, :]
    d_n = wait()
    scaled = d_n * ngain
    in_g = (
        d_res
        + inv_own * scaled
        - x_own * inv_own * inv_own * inv_own * jnp.mean(scaled * x_own, axis=1, keepdims=True)
    )
    ag4 = gather_rows(refs, "ag4", ns, t, in_g.astype(BF16))
    sent += ag4
    refs.g_ngain[...] = jnp.sum(d_n * x_own * inv_own, axis=0, keepdims=True)
    for copy in ag3:
        copy.wait_recv()
    for k in range(ns):
        refs.layer_output[TO * k : TO * (k + 1), :] = refs.ag3_all[k]
    for copy in ag4:
        copy.wait_recv()
    for k in range(ns):
        refs.input_grad[TO * k : TO * (k + 1), :] = refs.ag4_all[k]
    for copy in sent:
        copy.wait_send()
    for slot in range(steps):
        carry.finish(slot)
        carry_b.finish(slot)

    def kv_end(k, carried):
        kv_copy(k, lax.rem(s + k, n)).wait_send()
        return carried

    lax.fori_loop(1, n - s, kv_end, 0)

    def dkv_end(k, carried):
        dkv_copy(k, lax.rem(s - k + n, n), kv_all.at[s - k]).wait_send()
        return carried

    lax.fori_loop(1, s + 1, dkv_end, 0)


def layer(n, ns, inputs):
    T, D = inputs["x"].shape
    C = inputs["w_mix"].shape[1] // 2
    NW = inputs["st_own"].shape[1]
    F = inputs["down"].shape[1]
    N, TO, H = NW * ns, T // ns, NH // ns
    steps = len(carry_steps(n))
    sd = jax.ShapeDtypeStruct
    J = 2 * HEAD_SIZE + C
    outs = {
        "layer_output": sd((T, D), BF16),
        "input_grad": sd((T, D), BF16),
        "gw_down": sd((D, F), BF16),
        "gw_gu": sd((D, 2 * F), BF16),
        "gw_joint": sd((J, D), BF16),
        "gw_mix": sd((D, 2 * C), BF16),
        "gw_qkv": sd((D, 4 * HEAD_SIZE), BF16),
        "gw_st": sd((D, 2 * NW), BF16),
        "gw_step": sd((D, LANES), BF16),
        "g_mgain": sd((1, D), F32),
        "g_ngain": sd((1, D), F32),
        "g_ggain": sd((1, C), F32),
        "g_skip": sd((1, C), F32),
        "g_rate": sd((1, LANES), F32),
        "g_bias": sd((1, LANES), F32),
        "g_taps_mix": sd((KC, C), F32),
        "g_taps_st": sd((KC, 2 * NW), F32),
    }
    vm = pltpu.VMEM
    dma = lambda k: (pltpu.SemaphoreType.DMA((k,)), pltpu.SemaphoreType.DMA((k,)))
    scratch = {
        "halo_rx": vm((HALO, D), BF16),
        "st_all": vm((2, N, D), BF16),
        "taps_all": vm((2, N, LANES), F32),
        "kv_all": vm((n, T, LANES), BF16),
        "normed": vm((T + HALO, D), BF16),
        "inv1": vm((T, 1), F32),
        "q2": vm((2 * T, LANES), BF16),
        "z": vm((T, C), F32),
        "ext_f": vm((T + HALO, C), F32),
        "ext_s": vm((T + HALO, N), F32),
        "ext_o": vm((T + HALO, 2 * NW), F32),
        "grad_f": vm((T + HALO, C), F32),
        "grad_o": vm((T + HALO, 2 * NW), F32),
        "inner_lin": vm((T, C), F32),
        "wr": vm((2, T, N), F32),
        "in_x": vm((T, C), F32),
        "tail_e": vm((T, C), F32),
        "reach_e": vm((T, C), F32),
        "link": vm((H, T, T), F32),
        "g_mat": vm((T, T), F32),
        "d_g": vm((T, T), F32),
        "ssd": vm((T, C), F32),
        "full_mix": vm((T, C), F32),
        "gated": vm((T, C), F32),
        "dy": vm((T, C), F32),
        "w_tot": vm((T, C), F32),
        "d_z": vm((T, C), BF16),
        "s_in": vm((C, N), F32),
        "joined": vm((T, J), BF16),
        "m_acc": vm((2 * T, 1), F32),
        "l_acc": vm((2 * T, 1), F32),
        "o_acc": vm((2 * T, LANES), F32),
        "dout2": vm((2 * T, LANES), BF16),
        "dq2": vm((2 * T, LANES), F32),
        "dkv_rx": vm((n, T, LANES), BF16),
        "dkv_sum": vm((T, LANES), F32),
        "pair_tx": vm((T, LANES), BF16),
        "pair_rx": vm((T, LANES), BF16),
        "back_tx": vm((HALO, D), BF16),
        "back_rx": vm((HALO, D), BF16),
        "dwr_tx": vm((2, N, T), BF16),
        "dwr_rx": vm((ns - 1, 2, NW, T), BF16),
        "halo": dma(1),
        "st": dma(ns - 1),
        "taps": dma(ns - 1),
        "kv": dma(n - 1),
        "dkv": dma(n - 1),
        "pair": dma(1),
        "back": dma(1),
        "dwr": dma(ns - 1),
    }
    for name in ("fc", "bc"):
        scratch[name + "_tx"] = vm((steps, C, N), BF16)
        scratch[name + "_rx"] = vm((steps, C, N), BF16)
        scratch[name + "_thr_tx"] = vm((steps, 8, LANES), F32)
        scratch[name + "_thr_rx"] = vm((steps, 8, LANES), F32)
        scratch[name] = dma(steps)
        scratch[name + "_thr"] = dma(steps)
    for name in ("sq", "dot"):
        scratch[name + "_tx"] = vm((8, T), F32)
        scratch[name + "_rx"] = vm((ns - 1, 8, T), F32)
        scratch[name] = dma(ns - 1)
    for name in ("rs1", "rs2", "rs3", "rs4"):
        scratch[name + "_tx"] = vm((ns, TO, D), BF16)
        scratch[name + "_rx"] = vm((ns - 1, TO, D), BF16)
        scratch[name] = dma(ns - 1)
    for name in ("ag1", "ag2", "ag3", "ag4"):
        scratch[name + "_all"] = vm((ns, TO, D), BF16)
        scratch[name] = dma(ns - 1)
    names, flat = [], []
    for group in (inputs, outs, scratch):
        for name, item in group.items():
            names.append((name, len(item) if isinstance(item, tuple) else 1))
    for item in scratch.values():
        flat += list(item) if isinstance(item, tuple) else [item]
    whole = pl.BlockSpec(memory_space=pltpu.VMEM)
    small = pl.BlockSpec(memory_space=pltpu.SMEM)
    got = pl.pallas_call(
        functools.partial(layer_kernel, n, ns, names),
        out_shape=tuple(outs.values()),
        in_specs=[small if name == "doc_starts" else whole for name in inputs],
        out_specs=(whole,) * len(outs),
        scratch_shapes=flat,
        name="layer",
        compiler_params=pltpu.CompilerParams(
            collective_id=1, has_side_effects=True, vmem_limit_bytes=VMEM_LIMIT
        ),
    )(*inputs.values())
    return types.SimpleNamespace(**dict(zip(outs, got)))


def local(
    layer_input,
    out_grad,
    doc_starts,
    real_mask,
    norm_gain,
    attention_input_rows,
    mixer_in,
    state_in,
    step_in,
    conv_mixer,
    conv_state,
    step_bias,
    decay_rate,
    skip_gain,
    gated_gain,
    joint_out,
    mlp_gain,
    gate_up,
    down_weight,
):
    T, D = layer_input.shape
    NS, n = lax.axis_size("state"), lax.axis_size("seq")
    t, s = lax.axis_index("state"), lax.axis_index("seq")
    HL = NH // NS
    C = HL * HDM
    QC = QUERY_HEADS * HEAD_SIZE // NS
    TO = T // NS
    DM = NH * HDM
    NW = state_in.shape[2]
    AQ = QUERY_HEADS * HEAD_SIZE
    KW = KEY_VALUE_HEADS * HEAD_SIZE
    kvh = t * KEY_VALUE_HEADS // NS
    first_row = s * T
    starts = [doc_starts[k] for k in range(doc_starts.shape[0])]
    dsl = lax.dynamic_slice_in_dim

    w_q = dsl(attention_input_rows, QC * t, QC, 1)
    w_k = dsl(attention_input_rows, AQ + HEAD_SIZE * kvh, HEAD_SIZE, 1)
    w_v = dsl(attention_input_rows, AQ + KW + HEAD_SIZE * kvh, HEAD_SIZE, 1)
    w_qkv = jnp.concatenate([w_q, w_k, w_v], axis=1)
    w_mix = dsl(mixer_in, C * t, C, 2)
    w_mix = jnp.concatenate([w_mix[:, 0], w_mix[:, 1]], axis=1)
    w_step = jnp.pad(dsl(step_in, HL * t, HL, 1), ((0, 0), (0, LANES - HL)))
    pad_row = lambda v: jnp.pad(dsl(v, HL * t, HL, 0), (0, LANES - HL))[None, :]
    bias_row, rate_row = pad_row(step_bias), pad_row(decay_rate)
    skip_row = jnp.repeat(dsl(skip_gain, HL * t, HL, 0), HDM)[None, :]
    taps_mix = dsl(conv_mixer, C * t, C, 1)
    ggain_row = dsl(gated_gain, C * t, C, 0)[None, :]
    w_joint = jnp.concatenate([dsl(joint_out, QC * t, QC, 0), dsl(joint_out, AQ + C * t, C, 0)], axis=0)
    st_own = jnp.transpose(state_in, (1, 2, 0))
    taps_own = conv_state.reshape(KC, 2 * NW)
    w_gu = jnp.concatenate([gate_up[:, 0], gate_up[:, 1]], axis=1)
    F = gate_up.shape[2]
    ngain, mgain = norm_gain[None, :], mlp_gain[None, :]
    real_f = real_mask.astype(F32)
    real_col = dsl(real_f, first_row, T, 0)[:, None]
    all_doc = doc_of(starts, jnp.arange(n * T, dtype=jnp.int32)[None, :])[0]
    codes = jnp.where(real_mask > 0, all_doc, -7).reshape(n, 1, T)
    pos = first_row + jnp.arange(T, dtype=jnp.int32)
    firsts = jnp.max(jnp.where(doc_starts[None, :] <= pos[:, None], doc_starts[None, :], 0), axis=1)
    powers = (jnp.arange(LANES) % (HEAD_SIZE // 2)).astype(F32) * (2.0 / HEAD_SIZE)
    angles = (pos - firsts).astype(F32)[:, None] * jnp.exp(-math.log(ROPE_BASE) * powers)[None, :]
    cosine, sine = jnp.cos(angles), jnp.sin(angles)

    taps_rows = jnp.pad(jnp.transpose(conv_state, (1, 2, 0)), ((0, 0), (0, 0), (0, LANES - KC)))
    o = layer(
        n,
        NS,
        {
            "x": layer_input,
            "g": out_grad,
            "w_qkv": w_qkv,
            "w_mix": w_mix,
            "w_step": w_step,
            "st_own": st_own,
            "taps_st": taps_rows,
            "taps_mix": taps_mix,
            "ngain": ngain,
            "bias_row": bias_row,
            "rate_row": rate_row,
            "skip_row": skip_row,
            "ggain_row": ggain_row,
            "w_joint": w_joint,
            "mgain": mgain,
            "w_gu": w_gu,
            "down": down_weight,
            "real_col": real_col,
            "codes": codes,
            "cosine": cosine,
            "sine": sine,
            "doc_starts": doc_starts,
        },
    )
    pair = NS // KEY_VALUE_HEADS
    odd = t % pair
    gw_q, gw_kv = o.gw_qkv[:, :QC], o.gw_qkv[:, QC:]
    gw_kv = jnp.where(odd == 0, gw_kv[:, :HEAD_SIZE], gw_kv[:, HEAD_SIZE:])
    gw_down, gw_gu, gw_joint, gw_mix, gw_step, gw_st = (
        o.gw_down, o.gw_gu, o.gw_joint, o.gw_mix, o.gw_step, o.gw_st
    )
    layer_output, input_grad = o.layer_output, o.input_grad.astype(F32)
    g_ngain, g_mgain, g_ggain, g_skip = o.g_ngain, o.g_mgain, o.g_ggain, o.g_skip
    g_taps_mix, g_taps_st, g_bias, g_rate = o.g_taps_mix, o.g_taps_st, o.g_bias, o.g_rate

    def rs_seq(v):
        return lax.psum_scatter(v, "seq", scatter_dimension=0, tiled=True)

    r_down, r_gu = rs_seq(gw_down), rs_seq(gw_gu)
    r_a = rs_seq(jnp.concatenate([gw_q, gw_kv, gw_mix, gw_step[:, :HL], gw_st], axis=1))
    rows = D // n
    gj = lax.all_gather(gw_joint, "state", axis=0)
    gj = jnp.concatenate([gj[:, :QC].reshape(AQ, D), gj[:, QC:].reshape(DM, D)], axis=0)
    r_joint = lax.psum_scatter(gj, "seq", scatter_dimension=0, tiled=True)
    W = QC + HEAD_SIZE + 2 * C + HL
    ga = lax.all_gather(r_a[:, :W], "state", axis=1)
    g_att = jnp.concatenate(
        [ga[:, :, :QC].reshape(rows, AQ)]
        + [ga[:, h * pair + k, QC : QC + HEAD_SIZE] for k in range(2) for h in range(KEY_VALUE_HEADS)],
        axis=1,
    )
    o = QC + HEAD_SIZE
    g_mix = jnp.stack(
        [ga[:, :, o : o + C].reshape(rows, DM), ga[:, :, o + C : o + 2 * C].reshape(rows, DM)], axis=1
    )
    g_step = ga[:, :, o + 2 * C :].reshape(rows, NH)
    g_st = r_a[:, W:].reshape(rows, 2, NW)
    sums = lax.psum((g_ngain, g_mgain), ("seq", "state"))
    small = lax.psum(
        (g_ggain, g_taps_mix, g_taps_st, g_bias[:, :HL], g_rate[:, :HL], g_skip), "seq"
    )
    s_ggain, s_taps, s_st, s_bias, s_rate, s_skip = small
    s_skip = jnp.sum(s_skip.reshape(1, HL, HDM), axis=2)
    cat = lambda v: lax.all_gather(v, "state", axis=1, tiled=True)
    s_ggain, s_taps, s_bias, s_rate, s_skip = map(cat, (s_ggain, s_taps, s_bias, s_rate, s_skip))
    take = lambda v: dsl(v[0], s * (v.shape[1] // n), v.shape[1] // n, 0)
    f = lambda v: v.astype(F32)
    return (
        layer_output,
        input_grad,
        take(sums[0]),
        f(g_att),
        f(g_mix),
        f(g_st),
        f(g_step),
        s_taps,
        s_st.reshape(KC, 2, NW),
        s_bias[0],
        s_rate[0],
        s_skip[0],
        take(s_ggain),
        f(r_joint),
        take(sums[1]),
        f(r_gu).reshape(rows, 2, F),
        f(r_down),
    )


def solution(mesh):
    rep = P()
    in_specs = (
        P("seq", None),
        P("seq", None),
        rep,
        rep,
        rep,
        rep,
        rep,
        P(None, None, "state"),
        rep,
        rep,
        P(None, None, "state"),
        rep,
        rep,
        rep,
        rep,
        rep,
        rep,
        P(None, None, "state"),
        P(None, "state"),
    )
    out_specs = (
        P("seq", None),
        P("seq", None),
        P("seq"),
        P("seq", None),
        P("seq", None, None),
        P("seq", None, "state"),
        P("seq", None),
        rep,
        P(None, None, "state"),
        rep,
        rep,
        rep,
        P("seq"),
        P("seq", None),
        P("seq"),
        P("seq", None, "state"),
        P("seq", "state"),
    )
    return jax.shard_map(local, mesh=mesh, in_specs=in_specs, out_specs=out_specs, check_vma=False)
```

time: 821 us -> 507 us (0.62)
  waiting for transfers between devices: 401 us -> 172 us
  Pallas kernels: 43 us -> 138 us
  matrix products: 55.5 us -> 0 us
  other arithmetic: 63.7 us -> 22 us
  local copies, waits for them, and re-layouts: 81.5 us -> 48.5 us
  blocking collectives: 130 us -> 102 us
  starting transfers between devices: 12.8 us -> 0.21 us
    unnamed x15 -> x5, waiting for transfers between devices: 116 us -> 1.07 us
    pallas_call x1, Pallas kernels: 43 us -> 138 us  [layer(): pl.pallas_call(functools.partial(layer_kernel, n, ns, names), out_shape=t...]
    reduce_scatter x4 -> x0, waiting for transfers between devices: 84.6 us -> none  [the longest x1 64.2 us: local(): dkv = lax.psum_scatter(dkv_all, 'seq', scatter_dimension=0, tiled=False)]
    ppermute x8 -> x0, waiting for transfers between devices: 77 us -> none  [the longest x7 77 us: carry(): lax.ppermute(v, 'seq', [(i, i + d * direction) for i in range(n) if 0 <=...]
    dot_general x55 -> x0, matrix products: 55.5 us -> none  [the longest x21 21 us: tn(): lax.dot_general(a, b, (((0,), (0,)), ((), ())), precision=p, preferred_el...]
    reduce_scatter x1 -> x3, waiting for transfers between devices: 13.9 us -> 67.7 us  [rs_seq(): return lax.psum_scatter(v, 'seq', scatter_dimension=0, tiled=True)]
    all_gather x3 -> x0, blocking collectives: 20.4 us -> none  [the longest x2 14.3 us: ag_state(): return lax.all_gather(v, 'state', axis=0, tiled=True)]
    psum x1 -> x0, waiting for transfers between devices: 15.1 us -> none  [local(): dkv = lax.psum(dkv, 'state', axis_index_groups=groups)]
  transfers between devices with their start and end apart: 20 -> 5, of which waited for: 15 -> 3; matrix products, arithmetic and copies ran while one was open for 16% -> 5% of each run, Pallas kernels for 0% -> 0%
where the time goes in v3:
time: 507 us; the launch traced here: 500 us
  waiting for transfers between devices  172 us (34%)
  Pallas kernels  138 us (27%)
  blocking collectives  102 us (20%)
  local copies, waits for them, and re-layouts  48.5 us (10%)
  other arithmetic  22 us (4%)
  between operations  17.3 us (3%)
    pallas_call x1, Pallas kernels, layer(): pl.pallas_call(functools.partial(layer_kernel, n, ns, names), out_shape=t...  138 us
    reduce_scatter x1, waiting for transfers between devices, local(): r_joint = lax.psum_scatter(gj, 'seq', scatter_dimension=0, tiled=True)  74.2 us
    reduce_scatter x3, waiting for transfers between devices, rs_seq(): return lax.psum_scatter(v, 'seq', scatter_dimension=0, tiled=True)  67.7 us
    psum x1, blocking collectives, local(): lax.psum((g_ggain, g_taps_mix, g_taps_st, g_bias[:, :HL], g_rate[:, :HL],...  37.2 us
    psum x1, blocking collectives, local(): sums = lax.psum((g_ngain, g_mgain), ('seq', 'state'))  36.9 us
    all_gather x1, waiting for transfers between devices, local(): gj = lax.all_gather(gw_joint, 'state', axis=0)  29.6 us
    all_gather x2, blocking collectives, local(): cat = lambda v: lax.all_gather(v, 'state', axis=1, tiled=True)  10.9 us
  transfers between devices with their start and end apart: 5, of which 3 were waited for; matrix products, arithmetic and copies ran while one was open for 5% of the time, Pallas kernels for 0%

profile of v3, /device:TPU:0, one launch (start us, length us, event | category | flops | bytes accessed | tf_op | source)
XLA Modules:
  0.0 499.8 jit_solution(8169756327203062232)
XLA Ops:
  8.2 0.9 dynamic_slice.60
  9.0 0.7 dynamic_slice.61
  9.8 0.7 dynamic_slice.62
  10.5 1.6 fusion.11
  12.1 0.7 select_reduce_fusion
  12.9 0.8 dynamic_slice.63
  14.9 1.3 constant_dynamic-slice_fusion.6.flat_7_
  16.2 0.8 copy.77
  17.0 0.8 dynamic-slice_convert_fusion
  17.8 0.8 copy.80.flat_17_
  18.8 1.0 constant_dynamic-slice_fusion.5
  19.8 1.2 constant_dynamic-slice_fusion.4
  21.0 4.2 fusion.9
  26.3 0.8 pad.15.flat_4_
  27.0 1.2 multiply_sine_fusion
  28.3 1.0 constant_dynamic-slice_fusion.11
  29.2 1.3 constant_dynamic-slice_fusion.10
  30.5 1.0 pad_maximum_fusion.3.flat_13_
  31.5 5.7 %constant_dynamic-slice_fusion = (bf16[1024,1,384]{2,1,0:T(2,128)(2,1)S(1)}, bf16[1024,1,384]{2,1,0:T(2,128)(2,1)S(1)}) fusion(bf16[1024,2,1536]{2,1,0:T(2,128)(2,1)} %param.25, s32[]{:T(128)S(6)} %select_n.77, s32[]{:T(128)S(6)} %add.180), kind=kLoop, calls=%fused_computation.35 | loop fusion | bytes 3145736 | tf_op jit(solution)/shard_map/slice | solution.py:933
  37.5 1.3 pad_maximum_fusion.2.flat_3_
  39.3 0.8 copy-done.3
  40.7 1.6 pad_maximum_fusion.1.flat_15_
  42.3 1.0 pad_maximum_fusion.4.flat_2_
  43.2 5.8 %add_select_fusion = s32[2048]{0:T(1024)} fusion(s32[2048]{0:T(1024)S(1)} %copy-done.11, s32[]{:T(128)} %bitcast.18, s32[]{:T(128)} %bitcast.17, s32[]{:T(128)} %bitcast.16, s32[]{:T(128)} %bitcast.15, s32[]{:T(128)} %bitcast.14, s32[]{:T(128)} %bitcast.13, s32[]{:T(128)} %bitcast.12, s32[]{:T(128)} %bitcast.11), kind=kLoop, calls=%fused_computation.26 | loop fusion | flops 53248 | bytes 16416 | tf_op jit(solution)/shard_map/jit(_where)/select_n | solution.py:949
  49.1 137.5 %layer.1 = (bf16[256,1024]{1,0:T(8,128)(2,1)}, bf16[256,1024]{1,0:T(8,128)(2,1)}, bf16[1024,512]{1,0:T(8,128)(2,1)}, bf16[1024,1024]{1,0:T(8,128)(2,1)}, bf16[51...) custom-call(bf16[256,1024]{1,0:T(8,128)(2,1)} %flat_0_.1, ...), custom_call_target="tpu_custom_call" | custom-call | tf_op jit(solution)/shard_map/layer/pallas_call | solution.py:877
  188.3 4.1 concatenate.25
  192.5 29.6 %all-gather.6.cloned.1.call-done = bf16[2048,1024]{1,0:T(8,128)(2,1)} async-done(((bf16[512,1024]{1,0:T(8,128)(2,1)}), bf16[2048,1024]{1,0:T(8,128)(2,1)}) %all-gather.6.cloned.1.call-update) | async-done | bytes 4194320 | tf_op jit(solution)/shard_map/all_gather | solution.py:1002
  222.1 1.3 slice.133
  223.4 2.2 slice.134
  225.6 2.4 pad_maximum_fusion
  228.8 37.2 %all-reduce.8 = (f32[4,384]{1,0:T(4,128)S(1)}, f32[4,2,32]{2,1,0:T(2,128)}, f32[1,6]{1,0:T(1,128)S(1)}, f32[1,6]{1,0:T(1,128)S(1)}, f32[6,64]{1,0:T(8,128)S(1)}, /*index=5*/f32[1,384]{1,0:T(1,128)S(1)}) all-reduce(f32[4,384]{1,0:T(4,128)S(1)} %copy-done.12, f32[4,2,32]{2,1,0:T(2,128)S(1)} %reshape.126, ...), channel_id=1, replica_groups=mesh['seq'=8,'state'=4] {'seq'}, use_global_device_ids=true, to_apply=%region_3.4 | all-reduce | flops 2572 | bytes 20576 | tf_op jit(solution)/shard_map/psum | solution.py:1019
  266.0 5.2 %all_gather.29 = f32[4,1536]{1,0:T(4,128)S(1)} all-gather(f32[4,384]{1,0:T(4,128)S(1)} %get-tuple-element.138), channel_id=1, replica_groups=mesh['seq'=8,'state'=4] {'state'}, dimensions={1}, use_global_device_ids=true | all-gather | bytes 30720 | tf_op jit(solution)/shard_map/all_gather | solution.py:1024
  271.2 1.1 convert_element_type.111
  274.1 7.1 %all-reduce.9 = (f32[24]{0:T(128)}, f32[24]{0:T(128)}, f32[24]{0:T(128)}) all-reduce(f32[24]{0:T(128)S(1)} %bitcast_dynamic-update-slice_fusion.1, f32[24]{0:T(128)S(1)} %bitcast_dynamic-update-slice_fusion, f32[24]{0:T(128)S(1)} %dynamic-update-slice.2), channel_id=1, replica_groups=mesh['seq'=8,'state'=4] {'state'}, use_global_device_ids=true, to_apply=%add.4 | all-reduce | flops 72 | bytes 576 | tf_op jit(solution)/shard_map/squeeze | solution.py:1038
  281.2 36.9 %all-reduce.7 = (f32[1,1024]{1,0:T(1,128)S(1)}, f32[1,1024]{1,0:T(1,128)S(1)}) all-reduce(f32[1,1024]{1,0:T(1,128)S(1)} %copy-done.14, f32[1,1024]{1,0:T(1,128)S(1)} %copy-done.13), channel_id=1, replica_groups=mesh['seq'=8,'state'=4] {'seq','state'}, use_global_device_ids=true, to_apply=%region_1.2 | all-reduce | flops 2048 | bytes 16384 | tf_op jit(solution)/shard_map/psum | solution.py:1018
  318.2 5.7 %all_gather.33 = f32[1,1536]{1,0:T(1,128)S(1)} all-gather(f32[1,384]{1,0:T(1,128)S(1)} %get-tuple-element.143), channel_id=1, replica_groups=mesh['seq'=8,'state'=4] {'state'}, dimensions={1}, use_global_device_ids=true | all-gather | bytes 7680 | tf_op jit(solution)/shard_map/all_gather | solution.py:1024
  325.5 1.6 convert_element_type.119
  327.2 2.3 reshape.135
  329.4 67.7 %reduce-scatter.5.cloned.1.call-done = bf16[128,1030]{1,0:T(8,128)(2,1)} async-done(((bf16[1024,1030]{1,0:T(8,128)(2,1)}), bf16[128,1030]{1,0:T(8,128)(2,1)}) %reduce-scatter.5.cloned.1.call-update) | async-done | bytes 263696 | tf_op jit(solution)/shard_map/reduce_scatter | solution.py:997
  397.1 0.9 slice_convert_fusion
  398.0 0.7 copy.82
  398.7 1.0 slice_bitcast_fusion
  399.9 9.7 %all-gather.3 = bf16[4,966,128]{2,1,0:T(8,128)(2,1)S(1)} all-gather(bf16[1,966,128]{2,1,0:T(8,128)(2,1)S(1)} %copy.81), channel_id=2, replica_groups=mesh['seq'=8,'state'=4] {'state'}, dimensions={0}, use_global_device_ids=true | all-gather | bytes 1236480 | tf_op jit(solution)/shard_map/all_gather | solution.py:1006
  410.8 0.9 copy.83
  411.9 2.1 copy.84
  414.0 74.2 %reduce-scatter.7.cloned.1.call-done = bf16[256,1024]{1,0:T(8,128)(2,1)} async-done(((bf16[2048,1024]{1,0:T(8,128)(2,1)}), bf16[256,1024]{1,0:T(8,128)(2,1)}) %reduce-scatter.7.cloned.1.call-update) | async-done | bytes 524304 | tf_op jit(solution)/shard_map/reduce_scatter | solution.py:1004
  488.1 2.1 convert_element_type.118
  490.3 0.8 copy.106
  (95 shorter events, 11.4 us)
Async XLA Ops:
  8.0 8.2 %copy-start = (bf16[1024,24]{0,1:T(8,128)(2,1)S(1)}, bf16[1024,24]{0,1:T(8,128)(2,1)}, u32[]{:S(2)}) copy-start(bf16[1024,24]{0,1:T(8,128)(2,1)} %param.27) | copy-start | bytes 147460
  8.0 12.9 %copy-start.2 = (bf16[1024,2,512]{2,1,0:T(2,128)(2,1)S(1)}, bf16[1024,2,512]{2,1,0:T(2,128)(2,1)}, u32[]{:S(2)}) copy-start(bf16[1024,2,512]{2,1,0:T(2,128)(2,1)} %param.36) | copy-start | bytes 6291460
  8.0 214.0 %all-gather.6.cloned.1.call-start = ((), (), s32[]{:S(2)}) async-start(), calls=%async_computation.8 | async-start | bytes 5242880 | tf_op jit(solution)/shard_map/all_gather | solution.py:1002
  37.2 2.1 copy-start.4
  37.5 2.6 copy-start.3
  40.7 2.6 copy-start.11
  186.6 1.3 copy-start.6
  186.6 138.9 %reduce-scatter.11.cloned.1.call-start = ((), (), s32[]{:S(2)}) async-start(), calls=%async_computation.7 | async-start | bytes 1179648 | tf_op jit(solution)/shard_map/reduce_scatter | solution.py:997
  186.7 1.5 copy-start.5
  186.7 1.5 copy-start.9
  186.7 1.6 copy-start.10
  187.2 140.0 %reduce-scatter.9.cloned.1.call-start = ((), (), s32[]{:S(2)}) async-start(), calls=%async_computation.6 | async-start | bytes 2359296 | tf_op jit(solution)/shard_map/reduce_scatter | solution.py:997
  187.8 209.3 %reduce-scatter.5.cloned.1.call-start = ((), (), s32[]{:S(2)}) async-start(), calls=%async_computation.4 | async-start | bytes 2654208 | tf_op jit(solution)/shard_map/reduce_scatter | solution.py:997
  192.4 295.7 %reduce-scatter.7.cloned.1.call-start = ((), (), s32[]{:S(2)}) async-start(), calls=%async_computation.5 | async-start | bytes 4718592 | tf_op jit(solution)/shard_map/reduce_scatter | solution.py:1004
  228.0 0.7 copy-start.17
  228.0 0.8 copy-start.15
  228.0 0.8 copy-start.12
  228.0 0.8 copy-start.16
  228.0 0.8 copy-start.18
  228.0 0.8 copy-start.19
  228.0 43.2 %copy-start.7 = (bf16[256,1024]{1,0:T(8,128)(2,1)S(1)}, bf16[256,1024]{1,0:T(8,128)(2,1)}, u32[]{:S(2)}) copy-start(bf16[256,1024]{1,0:T(8,128)(2,1)} %get-tuple-element.35) | copy-start | bytes 1572868
  228.0 44.3 %copy-start.20 = (u32[32]{0:T(128)S(1)}, u32[32]{0:T(128)}, u32[]{:S(2)}) copy-start(u32[32]{0:T(128)} %constant.111) | copy-start | bytes 388
  228.0 53.2 %copy-start.13 = (f32[1,1024]{1,0:T(1,128)S(1)}, f32[1,1024]{1,0:T(1,128)}, u32[]{:S(2)}) copy-start(f32[1,1024]{1,0:T(1,128)} %get-tuple-element.48) | copy-start | bytes 12292
  228.0 53.2 %copy-start.14 = (f32[1,1024]{1,0:T(1,128)S(1)}, f32[1,1024]{1,0:T(1,128)}, u32[]{:S(2)}) copy-start(f32[1,1024]{1,0:T(1,128)} %get-tuple-element.36) | copy-start | bytes 12292
  411.9 78.4 %copy-start.8 = (bf16[256,1024]{1,0:T(8,128)(2,1)S(1)}, bf16[256,1024]{1,0:T(8,128)(2,1)}, u32[]{:S(2)}) copy-start(bf16[256,1024]{1,0:T(8,128)(2,1)} %get-tuple-element.188) | copy-start | bytes 1572868
  411.9 79.8 %copy-start.1 = (bf16[1024,24]{0,1:T(8,128)(2,1)S(1)}, bf16[1024,24]{0,1:T(8,128)(2,1)}, u32[]{:S(2)}) copy-start(bf16[1024,24]{0,1:T(8,128)(2,1)} %param.27) | copy-start | bytes 147460
Sparse Core Ops, SparseCore 0:
  186.7 35.2 all-gather.5
Sparse Core Ops, SparseCore 1:
  190.5 64.3 reduce-scatter.10
  258.6 66.9 reduce-scatter.8
  329.4 67.7 reduce-scatter.4
  401.2 86.9 reduce-scatter.6
